TPU v7x, 256 devices: a whole 4x4x8 slice. The times are simulated.
256 devices in a mesh: row: 16 (over z, y_lo), col: 16 (over x, y_hi, core).
Axes of the slice: x: 4, y: 4 (y_hi: 2, y_lo: 2; y = y_hi * 2 + y_lo), z: 8, core: 2. Of those that a mesh axis runs over, the one named last changes fastest.
Arguments:
- pair_rep: bfloat16 [768, 768, 128], P('row', 'col'), may hold values from -6 to 6
- tok_mask: int32 [768], replicated, may hold values 0 or 1
- windows: int32 [2, 2], replicated, may hold values from 0 to 15, as said below
- in_gain: float32 [2, 128], replicated, may hold values from 0.5 to 1.5
- in_bias: float32 [2, 128], replicated, may hold values from -3 to 3
- w_proj: bfloat16 [2, 128, 256], replicated, may hold values from -0.5 to 0.5
- w_gate: bfloat16 [2, 128, 256], replicated, may hold values from -0.5 to 0.5
- out_gain: float32 [2, 128], replicated, may hold values from 0.5 to 1.5
- out_bias: float32 [2, 128], replicated, may hold values from -3 to 3
- w_out: bfloat16 [2, 128, 128], replicated, may hold values from -0.5 to 0.5
- w_outgate: bfloat16 [2, 128, 128], replicated, may hold values from -0.5 to 0.5
Outputs:
- pair_out: bfloat16 [768, 768, 128], P('row', 'col')
Inputs may be any that keep to these rules, and one draw needn't show every extreme that they name: windows[0,0] and windows[0,1] are two different column blocks below 16; windows[1,0] and windows[1,1] are two different row blocks below 16, one of them the last row block 15.
All inputs are finite; a program needn't handle non-finite values.
Results may differ from a plain program's by a relative error of at most 0.0055.
Values may be sent and summed in bfloat16 or wider, within the bound.
No kernel may reach another device: no remote copies, remote signals or barrier semaphores. Data moves between devices by JAX's collectives and lax.ppermute only.
A program may use at most 64 MiB of HBM per device.

v0:
```python
import jax
import jax.numpy as jnp
from jax import lax
from jax.experimental.layout import Layout, with_layout_constraint
from jax.sharding import PartitionSpec as P


def layer_norm(values, ln_gain, ln_bias):
    values = values.astype(jnp.float32)
    average = jnp.mean(values, axis=-1, keepdims=True)
    centred = values - average
    variance = jnp.mean(centred * centred, axis=-1, keepdims=True)
    return centred * lax.rsqrt(variance + 1e-05) * ln_gain + ln_bias


def gate_project(normed, keep, weight_proj, weight_gate):
    flat = normed.reshape(-1, normed.shape[-1])
    projected = jnp.dot(flat, weight_proj, preferred_element_type=jnp.float32)
    gate_logit = jnp.dot(flat, weight_gate, preferred_element_type=jnp.float32)
    gated = jax.nn.sigmoid(gate_logit) * projected * keep[:, None]
    return gated.astype(jnp.bfloat16).reshape(normed.shape[0], normed.shape[1], -1)


def out_gate(normed, w_outgate):
    flat = normed.reshape(-1, normed.shape[-1])
    return jax.nn.sigmoid(jnp.dot(flat, w_outgate, preferred_element_type=jnp.float32))


def spread_of(contracted):
    return contracted, jnp.mean(contracted, axis=0, keepdims=True)


def rescale(contracted, average, out_gain, out_bias):
    centred = contracted - average
    variance = jnp.mean(centred * centred, axis=0, keepdims=True)
    scaled = centred * lax.rsqrt(variance + 1e-05) * out_gain[:, None, None] + out_bias[:, None, None]
    return scaled.astype(jnp.bfloat16)


def finish(current, scaled, gate, w_out):
    branch = jnp.einsum("hij,hc->ijc", scaled, w_out, preferred_element_type=jnp.float32)
    updated = current.astype(jnp.float32) + branch * gate.reshape(branch.shape)
    return updated.astype(jnp.bfloat16)


def swap(x, axis, bits):
    n = lax.axis_size(axis)
    return lax.ppermute(x, axis, [(p, p ^ bits) for p in range(n)])


def put(buffer, x, *at):
    at = at + (jnp.uint32(0),) * x.ndim
    return lax.dynamic_update_slice(buffer, x.reshape((1,) * (len(at) - x.ndim) + x.shape), at)


def gather_col(piece, places, meanwhile=(), second=lambda x: x):
    half, other_half, ring, core, other_core = places
    pair = jnp.zeros((2,) + piece.shape, piece.dtype)
    pair = put(put(pair, piece, half), swap(piece, "col", 2), other_half)
    pair, meanwhile = lax.optimization_barrier((pair, meanwhile))
    four = put(jnp.zeros((4,) + pair.shape, piece.dtype), pair, ring[0])
    for d in (2, 1, 3):
        four = put(four, swap(pair, "col", 4 * d), ring[d])
    four, meanwhile = lax.optimization_barrier((four, second(meanwhile)))
    whole = jnp.zeros((2,) + four.shape, piece.dtype)
    whole = put(put(whole, four, core), swap(four, "col", 1), other_core)
    return jnp.moveaxis(whole, 0, 2).reshape((16,) + piece.shape), meanwhile


def transpose_devices(x):
    n = lax.axis_size("row")
    pairs = [(a * n + b, b * n + a) for a in range(n) for b in range(n)]
    return lax.ppermute(x, ("row", "col"), pairs)


def body(
    pair_rep,
    tok_mask,
    windows,
    in_gain,
    in_bias,
    w_proj,
    w_gate,
    out_gain,
    out_bias,
    w_out,
    w_outgate,
):
    tile = pair_rep.shape[0]
    width = pair_rep.shape[2]
    hidden = w_out.shape[1]
    n = lax.axis_size("row")
    part = tile // n
    row_idx = lax.axis_index("row")
    col_idx = lax.axis_index("col")

    def pick(stacked, update):
        return [
            lax.dynamic_index_in_dim(stacked, windows[update, slot], 0, keepdims=False)
            for slot in range(2)
        ]

    def norm_in(values, update):
        return layer_norm(values, in_gain[update], in_bias[update]).astype(jnp.bfloat16)

    def gate_of(normed, update):
        return out_gate(normed, w_outgate[update])

    def scale(made, update):
        return rescale(*made, out_gain[update], out_bias[update])

    row = row_idx.astype(jnp.uint32)
    col = col_idx.astype(jnp.uint32)
    zero = jnp.uint32(0)
    keeps = tok_mask.astype(jnp.float32).reshape(n, tile)

    def keep_of(block):
        return lax.dynamic_slice(keeps, (block.astype(jnp.uint32), zero), (1, tile))[0]

    def part_of(keep, place):
        return lax.dynamic_slice(keep, (place * part,), (part,))

    window_keep = jnp.concatenate([keep_of(windows[0, slot]) for slot in range(2)])
    rows_keep = jnp.concatenate([part_of(keep_of(windows[1, slot]), row) for slot in range(2)])
    band_keep = (part_of(keep_of(row), col)[:, None] * window_keep[None, :]).reshape(-1)
    rows_keep = (rows_keep[:, None] * keep_of(col)[None, :]).reshape(-1)
    half, core = (col >> 1) & 1, col & 1
    places = (half, half ^ 1, [(col >> 2) ^ d for d in range(4)], core, core ^ 1)

    pieces = lax.all_to_all(pair_rep.reshape(n, part, tile, width), "col", 0, 0, tiled=True)
    pieces, places, band_keep, rows_keep = lax.optimization_barrier(
        (pieces, places, band_keep, rows_keep)
    )
    band = jnp.concatenate(pick(pieces, 0), axis=1)
    gated = gate_project(norm_in(band, 0), band_keep, w_proj[0], w_gate[0])
    left_own, right_own = gated[..., :hidden], gated[..., hidden:]
    right_moved = transpose_devices(right_own)
    left_moved = transpose_devices(left_own)
    source, _ = lax.optimization_barrier((pair_rep, right_own))
    gate = gate_of(norm_in(source, 0), 0)
    right_moved, gate = lax.optimization_barrier((right_moved, gate))

    rows = pair_rep.reshape(n, part, tile, width)
    chunks = jnp.concatenate([jnp.broadcast_to(right_moved, (n,) + right_moved.shape), rows], axis=2)
    chunks, left_own = lax.optimization_barrier((chunks, left_own))
    chunks = lax.all_to_all(chunks, "row", 0, 0, tiled=True)
    rows = jnp.concatenate(pick(chunks[:, :, 2 * tile :], 1), axis=0)
    chunks, rows = lax.optimization_barrier((chunks, rows))
    right = chunks[:, :, : 2 * tile].reshape(tile, 2 * tile, hidden)
    lefts, _ = gather_col(jnp.stack([left_own, left_moved]), places)
    left = lefts[:, 0].reshape(tile, 2 * tile, hidden)
    left_rows = jnp.concatenate(pick(lefts[:, 1], 1), axis=0)

    contracted = jnp.einsum("ikh,jkh->hij", left_rows, right, preferred_element_type=jnp.float32)
    scaled = scale(spread_of(contracted), 0)
    rows = finish(rows, scaled, gate_of(norm_in(rows, 0), 0), w_out[0])
    gated = gate_project(norm_in(rows, 1), rows_keep, w_proj[1], w_gate[1])
    next_left = transpose_devices(gated[..., :hidden])
    copies = jnp.broadcast_to(gated[..., hidden:], (n, 2 * part, tile, hidden))
    next_right = lax.all_to_all(copies, "row", 0, 0, tiled=True).reshape(2 * tile, tile, hidden)

    def main_tile(x):
        contracted = jnp.einsum("hik,jkh->hij", x, right, preferred_element_type=jnp.float32)
        return scale(spread_of(contracted), 0)

    next_left, left = lax.optimization_barrier((next_left, left))
    left = with_layout_constraint(left.transpose(2, 0, 1), Layout(major_to_minor=(0, 1, 2)))
    next_left, scaled = gather_col(next_left, places, left, main_tile)
    next_left = next_left.reshape(2 * tile, tile, hidden)
    current = finish(pair_rep, scaled, gate, w_out[0])
    gate = gate_of(norm_in(current, 1), 1)

    contracted = jnp.einsum(
        "kih,kjh->hij", next_left, next_right, preferred_element_type=jnp.float32
    )
    return finish(current, scale(spread_of(contracted), 1), gate, w_out[1])


def solution(mesh):
    placed = (P("row", "col", None), P(), P(), P(), P(), P(), P(), P(), P(), P(), P())
    return jax.shard_map(
        body, mesh=mesh, in_specs=placed, out_specs=P("row", "col", None), check_vma=False
    )
```

profile of v0, /device:TPU:4, one launch (start us, length us, event | category | flops | bytes accessed | tf_op | source)
XLA Modules:
  0.0 147.1 jit_solution(16498626717573564360)
XLA Ops:
  0.0 7.6 %all-to-all-start = ((bf16[16,3,48,128]{3,2,1,0:T(8,128)(2,1)}), bf16[16,3,48,128]{3,2,1,0:T(8,128)(2,1)S(1)}, u32[]{:S(2)}, u32[]{:S(2)}) async-start(bf16[16,3,48,128]{3,2,1,0:T(8,128)(2,1)} %bitcast.161), calls=%async_computation | async-start | bytes 1179648 | tf_op jit(solution)/shard_map/all_to_all | solution.py:130
  7.7 0.7 fusion.94
  13.8 0.7 mul.277
  16.5 1.8 %all-to-all-done = bf16[16,3,48,128]{3,2,1,0:T(8,128)(2,1)S(1)} async-done(((bf16[16,3,48,128]{3,2,1,0:T(8,128)(2,1)}), bf16[16,3,48,128]{3,2,1,0:T(8,128)(2,1)S(1)}, u32[]{:S(2)}, u32[]{:S(2)}) %all-to-all-start) | async-done | bytes 589856 | tf_op jit(solution)/shard_map/all_to_all | solution.py:130
  19.3 11.0 %collective-permute-start = (bf16[3,96,128]{2,1,0:T(8,128)(2,1)S(1)}, bf16[3,96,128]{2,1,0:T(8,128)(2,1)S(1)}, u32[]{:S(2)}, u32[]{:S(2)}) collective-permute-start(bf16[3,96,128]{2,1,0:T(8,128)(2,1)S(1)} %get-tuple-element.64), channel_id=1, source_target_pairs={{0,0},{1,16},{2,32},{3,48},{4,64},{5,80},{6,96},{7,112},{8,128},{9... | collective-permute-start | bytes 221192 | tf_op jit(solution)/shard_map/ppermute | solution.py:73
  30.8 0.7 fusion.26
  31.5 0.8 fusion.29
  32.3 1.9 %collective-permute-start.1 = (bf16[3,96,128]{2,1,0:T(8,128)(2,1)S(1)}, bf16[3,96,128]{2,1,0:T(8,128)(2,1)S(1)}, u32[]{:S(2)}, u32[]{:S(2)}) collective-permute-start(bf16[3,96,128]{2,1,0:T(8,128)(2,1)S(1)} %get-tuple-element.35), channel_id=1, source_target_pairs={{0,0},{1,16},{2,32},{3,48},{4,64},{5,80},{6,96},{7,112},{8,128},{9... | collective-permute-start | bytes 221192 | tf_op jit(solution)/shard_map/ppermute | solution.py:73
  34.2 1.5 %fusion.5 = f32[2304,128]{1,0:T(8,128)} fusion(bf16[2304,128]{1,0:T(8,128)(2,1)S(1)} %bitcast.174, bf16[2,128,128]{2,1,0:T(8,128)(2,1)S(1)} %copy-done.33), kind=kOutput, calls=%fused_computation.7 | convolution fusion | flops 76382208 | bytes 1802240 | tf_op jit(solution)/shard_map/dot_general | solution.py:26
  35.9 1.3 pad_maximum_fusion
  37.2 5.2 %all-to-all-start.1 = ((bf16[16,3,144,128]{3,2,1,0:T(8,128)(2,1)}), bf16[16,3,144,128]{3,2,1,0:T(8,128)(2,1)S(1)}, u32[]{:S(2)}, u32[]{:S(2)}) async-start(bf16[16,3,144,128]{3,2,1,0:T(8,128)(2,1)} %pad_maximum_fusion), calls=%async_computation.1 | async-start | bytes 3538944 | tf_op jit(solution)/shard_map/all_to_all | solution.py:146
  42.5 2.4 %collective-permute-done.1 = bf16[3,96,128]{2,1,0:T(8,128)(2,1)S(1)} collective-permute-done((bf16[3,96,128]{2,1,0:T(8,128)(2,1)S(1)}, bf16[3,96,128]{2,1,0:T(8,128)(2,1)S(1)}, u32[]{:S(2)}, u32[]{:S(2)}) %collective-permute-start.1) | collective-permute-done | bytes 73760 | tf_op jit(solution)/shard_map/ppermute | solution.py:73
  44.9 4.3 %collective-permute-start.2 = (bf16[2,3,96,128]{3,2,1,0:T(8,128)(2,1)S(1)}, bf16[2,3,96,128]{3,2,1,0:T(8,128)(2,1)S(1)}, u32[]{:S(2)}, u32[]{:S(2)}) collective-permute-start(bf16[2,3,96,128]{3,2,1,0:T(8,128)(2,1)S(1)} %pad_maximum_fusion.1), channel_id=1, source_target_pairs={{0,2},{1,3},{2,0},{3,1},{4,6},{5,7},{6,4},{7,5},{8,10},{9,11},{10,... | collective-permute-start | bytes 442376 | tf_op jit(solution)/shard_map/ppermute | solution.py:48
  49.3 3.6 %collective-permute-done.2 = bf16[2,3,96,128]{3,2,1,0:T(8,128)(2,1)S(1)} collective-permute-done((bf16[2,3,96,128]{3,2,1,0:T(8,128)(2,1)S(1)}, bf16[2,3,96,128]{3,2,1,0:T(8,128)(2,1)S(1)}, u32[]{:S(2)}, u32[]{:S(2)}) %collective-permute-start.2) | collective-permute-done | bytes 147488 | tf_op jit(solution)/shard_map/ppermute | solution.py:48
  52.9 5.1 %collective-permute-start.3 = (bf16[2,2,3,96,128]{4,3,2,0,1:T(8,128)(2,1)S(1)}, bf16[2,2,3,96,128]{4,3,2,0,1:T(8,128)(2,1)S(1)}, u32[]{:S(2)}, u32[]{:S(2)}) collective-permute-start(bf16[2,2,3,96,128]{4,3,2,0,1:T(8,128)(2,1)S(1)} %bitcast_dynamic-update-slice_fusion.8), channel_id=1, source_target_pairs={{0,8},{1,9},{2,10},{3,11},{4,12},{5,13},{6,14},{7,15},{8,0},{9,1},... | collective-permute-start | bytes 884744 | tf_op jit(solution)/shard_map/ppermute | solution.py:48
  58.1 0.7 collective-permute-start.5
  59.0 6.8 %collective-permute-done.3 = bf16[2,2,3,96,128]{4,3,2,0,1:T(8,128)(2,1)S(1)} collective-permute-done((bf16[2,2,3,96,128]{4,3,2,0,1:T(8,128)(2,1)S(1)}, bf16[2,2,3,96,128]{4,3,2,0,1:T(8,128)(2,1)S(1)}, u32[]{:S(2)}, u32[]{:S(2)}) %collective-permute-start.3) | collective-permute-done | bytes 294944 | tf_op jit(solution)/shard_map/ppermute | solution.py:48
  65.8 2.2 %collective-permute-done.4 = bf16[2,2,3,96,128]{4,3,2,0,1:T(8,128)(2,1)S(1)} collective-permute-done((bf16[2,2,3,96,128]{4,3,2,0,1:T(8,128)(2,1)S(1)}, bf16[2,2,3,96,128]{4,3,2,0,1:T(8,128)(2,1)S(1)}, u32[]{:S(2)}, u32[]{:S(2)}) %collective-permute-start.4) | collective-permute-done | bytes 294944 | tf_op jit(solution)/shard_map/ppermute | solution.py:48
  68.0 1.0 collective-permute-done.5
  74.8 1.4 bitcast_dynamic-update-slice_fusion.1
  76.2 1.2 fusion.91
  77.4 0.8 copy.38
  78.2 0.8 copy.39
  79.0 6.8 %all-to-all-done.1 = bf16[16,3,144,128]{3,2,1,0:T(8,128)(2,1)S(1)} async-done(((bf16[16,3,144,128]{3,2,1,0:T(8,128)(2,1)}), bf16[16,3,144,128]{3,2,1,0:T(8,128)(2,1)S(1)}, u32[]{:S(2)}, u32[]{:S(2)}) %all-to-all-start.1) | async-done | bytes 1769504 | tf_op jit(solution)/shard_map/all_to_all | solution.py:146
  86.6 1.0 copy.40
  87.7 1.9 %fusion.95 = (f32[6,48]{1,0:T(8,128)S(1)}, f32[128,6,48]{2,1,0:T(8,128)S(1)}) fusion(bf16[48,96,128]{1,0,2:T(8,128)(2,1)S(1)} %copy.40, bf16[3,96,128]{1,0,2:T(4,128)(2,1)} %bitcast.177, bf16[3,96,128]{1,0,2:T(4,128)(2,1)S(1)} %bitcast.176), kind=kOutput, calls=%fused_computation.171 | convolution fusion | flops 7409376 | bytes 1475712 | tf_op jit(solution)/shard_map/ikh,jkh->hij/dot_general | solution.py:154
  92.1 8.5 %collective-permute-start.7 = (bf16[6,48,128]{2,1,0:T(8,128)(2,1)S(1)}, bf16[6,48,128]{2,1,0:T(8,128)(2,1)}, u32[]{:S(2)}, u32[]{:S(2)}) collective-permute-start(bf16[6,48,128]{2,1,0:T(8,128)(2,1)S(1)} %get-tuple-element.62), channel_id=1, source_target_pairs={{0,0},{1,16},{2,32},{3,48},{4,64},{5,80},{6,96},{7,112},{8,128},{9... | collective-permute-start | bytes 221192 | tf_op jit(solution)/shard_map/ppermute | solution.py:73
  100.5 1.2 broadcast_in_dim.23
  101.7 4.5 %all-to-all-start.2 = ((bf16[16,6,48,128]{3,2,1,0:T(8,128)(2,1)}), bf16[16,6,48,128]{3,2,1,0:T(8,128)(2,1)}, u32[]{:S(2)}, u32[]{:S(2)}) async-start(bf16[16,6,48,128]{3,2,1,0:T(8,128)(2,1)} %broadcast_in_dim.23), calls=%async_computation.2 | async-start | bytes 2359296 | tf_op jit(solution)/shard_map/all_to_all | solution.py:160
  106.2 0.8 collective-permute-done.7
  107.0 4.2 %collective-permute-start.8 = (bf16[6,48,128]{2,1,0:T(8,128)(2,1)}, bf16[6,48,128]{2,1,0:T(8,128)(2,1)}, u32[]{:S(2)}, u32[]{:S(2)}) collective-permute-start(bf16[6,48,128]{2,1,0:T(8,128)(2,1)} %collective-permute-done.7), channel_id=1, source_target_pairs={{0,2},{1,3},{2,0},{3,1},{4,6},{5,7},{6,4},{7,5},{8,10},{9,11},{10,... | collective-permute-start | bytes 221192 | tf_op jit(solution)/shard_map/ppermute | solution.py:48
  111.2 0.9 bitcast_dynamic-update-slice_fusion.15
  112.1 1.8 %copy.42 = bf16[48,96,128]{1,0,2:T(8,128)(2,1)} copy(bf16[48,96,128]{2,1,0:T(8,128)(2,1)S(1)} %bitcast.167) | data formatting | bytes 2359296 | tf_op jit(solution)/shard_map/optimization_barrier | solution.py:166
  114.0 0.9 bitcast_dynamic-update-slice_fusion.14
  115.2 2.9 %collective-permute-start.10 = (bf16[2,6,48,128]{3,2,1,0:T(8,128)(2,1)S(1)}, bf16[2,6,48,128]{3,2,1,0:T(8,128)(2,1)S(1)}, u32[]{:S(2)}, u32[]{:S(2)}) collective-permute-start(bf16[2,6,48,128]{3,2,1,0:T(8,128)(2,1)S(1)} %bitcast_dynamic-update-slice_fusion.14), channel_id=1, source_target_pairs={{0,4},{1,5},{2,6},{3,7},{4,0},{5,1},{6,2},{7,3},{8,12},{9,13},{10,... | collective-permute-start | bytes 442376 | tf_op jit(solution)/shard_map/ppermute | solution.py:48
  118.0 1.2 collective-permute-start.11
  119.2 2.3 %fusion.97 = (f32[48,48]{1,0:T(8,128)S(1)}, f32[128,48,48]{2,1,0:T(8,128)S(1)}) fusion(bf16[128,48,96]{2,1,0:T(8,128)(2,1)} %bitcast.164, bf16[48,96,128]{1,0,2:T(8,128)(2,1)S(1)} %copy.40), kind=kOutput, calls=%fused_computation.173 | convolution fusion | flops 56915712 | bytes 3548160 | tf_op jit(solution)/shard_map/hik,jkh->hij/dot_general | solution.py:163
  124.1 0.8 convert_reduce_fusion
  125.0 0.7 fusion.22
  126.4 0.8 fusion.25
  127.2 1.5 %fusion.2 = f32[2304,128]{1,0:T(8,128)} fusion(bf16[2304,128]{1,0:T(8,128)(2,1)S(1)} %bitcast.175, bf16[2,128,128]{2,1,0:T(8,128)(2,1)S(1)} %copy-done.35), kind=kOutput, calls=%fused_computation.3 | convolution fusion | flops 76382208 | bytes 1802240 | tf_op jit(solution)/shard_map/dot_general | solution.py:26
  128.8 1.0 copy-done.1
  129.8 2.4 %copy.47 = bf16[96,48,128]{0,1,2:T(8,128)(2,1)S(1)} copy(bf16[96,48,128]{2,1,0:T(8,128)(2,1)} %bitcast.165) | data formatting | bytes 2359296 | tf_op jit(solution)/shard_map/reshape;reshape | solution.py:169
  132.2 6.1 %all-to-all-done.2 = bf16[16,6,48,128]{3,2,1,0:T(8,128)(2,1)} async-done(((bf16[16,6,48,128]{3,2,1,0:T(8,128)(2,1)}), bf16[16,6,48,128]{3,2,1,0:T(8,128)(2,1)}, u32[]{:S(2)}, u32[]{:S(2)}) %all-to-all-start.2) | async-done | bytes 1179680 | tf_op jit(solution)/shard_map/all_to_all | solution.py:160
  138.3 3.1 %copy.48 = bf16[96,48,128]{0,1,2:T(8,128)(2,1)} copy(bf16[96,48,128]{2,1,0:T(8,128)(2,1)} %bitcast.72) | data formatting | bytes 2359296 | tf_op jit(solution)/shard_map/reshape | solution.py:160
  141.4 2.3 %fusion.98 = (f32[48,48]{1,0:T(8,128)S(1)}, f32[128,48,48]{2,1,0:T(8,128)S(1)}) fusion(bf16[96,48,128]{0,1,2:T(8,128)(2,1)S(1)} %copy.47, bf16[96,48,128]{0,1,2:T(8,128)(2,1)} %copy.48), kind=kOutput, calls=%fused_computation.174 | convolution fusion | flops 56915712 | bytes 3548160 | tf_op jit(solution)/shard_map/kih,kjh->hij/dot_general | solution.py:173
  145.0 0.7 copy-done.5
  145.7 1.4 fusion.19
  (158 shorter events, 12.5 us)
Async XLA Ops:
  0.0 7.6 %copy-start.24 = (s32[2,2]{1,0:T(2,128)S(1)}, s32[2,2]{1,0:T(2,128)}, u32[]{:S(2)}) copy-start(s32[2,2]{1,0:T(2,128)} %param.13) | copy-start | bytes 52
  0.0 13.4 %copy-start.23 = (s32[768]{0:T(1024)S(1)}, s32[768]{0:T(1024)}, u32[]{:S(2)}) copy-start(s32[768]{0:T(1024)} %param.12) | copy-start | bytes 9220
  0.0 15.9 %copy-start.28 = (f32[2,128]{1,0:T(2,128)S(1)}, f32[2,128]{1,0:T(2,128)}, u32[]{:S(2)}) copy-start(f32[2,128]{1,0:T(2,128)} %param.14) | copy-start | bytes 3076
  0.0 15.9 %copy-start.27 = (f32[2,128]{1,0:T(2,128)S(1)}, f32[2,128]{1,0:T(2,128)}, u32[]{:S(2)}) copy-start(f32[2,128]{1,0:T(2,128)} %param.15) | copy-start | bytes 3076
  0.0 18.8 %copy-start.31 = (bf16[2,128,256]{2,1,0:T(8,128)(2,1)S(1)}, bf16[2,128,256]{2,1,0:T(8,128)(2,1)}, u32[]{:S(2)}) copy-start(bf16[2,128,256]{2,1,0:T(8,128)(2,1)} %param.17) | copy-start | bytes 393220
  0.0 18.3 %all-to-all-start = ((bf16[16,3,48,128]{3,2,1,0:T(8,128)(2,1)}), bf16[16,3,48,128]{3,2,1,0:T(8,128)(2,1)S(1)}, u32[]{:S(2)}, u32[]{:S(2)}) async-start(bf16[16,3,48,128]{3,2,1,0:T(8,128)(2,1)} %bitcast.161), calls=%async_computation | async-start | bytes 1179648 | tf_op jit(solution)/shard_map/all_to_all | solution.py:130
  7.6 11.5 %copy-start.8 = (bf16[2,128,256]{2,1,0:T(8,128)(2,1)S(1)}, bf16[2,128,256]{2,1,0:T(8,128)(2,1)}, u32[]{:S(2)}) copy-start(bf16[2,128,256]{2,1,0:T(8,128)(2,1)} %param.16) | copy-start | bytes 393220
  16.5 15.0 %copy-start.10 = (f32[128]{0:T(128)}, f32[128]{0:T(128)S(1)}, u32[]{:S(2)}) copy-start(f32[128]{0:T(128)S(1)} %get-tuple-element.78) | copy-start | bytes 1540
  16.5 15.0 %copy-start.12 = (f32[128]{0:T(128)}, f32[128]{0:T(128)S(1)}, u32[]{:S(2)}) copy-start(f32[128]{0:T(128)S(1)} %get-tuple-element.93) | copy-start | bytes 1540
  18.7 11.7 %copy-start = (bf16[48,48,128]{2,1,0:T(8,128)(2,1)S(1)}, bf16[48,48,128]{2,1,0:T(8,128)(2,1)}, u32[]{:S(2)}) copy-start(bf16[48,48,128]{2,1,0:T(8,128)(2,1)} %param.11) | copy-start | bytes 1769476
  19.3 14.9 %copy-start.33 = (bf16[2,128,128]{2,1,0:T(8,128)(2,1)S(1)}, bf16[2,128,128]{2,1,0:T(8,128)(2,1)}, u32[]{:S(2)}) copy-start(bf16[2,128,128]{2,1,0:T(8,128)(2,1)} %param.21) | copy-start | bytes 196612
  19.3 16.4 %collective-permute-start = (bf16[3,96,128]{2,1,0:T(8,128)(2,1)S(1)}, bf16[3,96,128]{2,1,0:T(8,128)(2,1)S(1)}, u32[]{:S(2)}, u32[]{:S(2)}) collective-permute-start(bf16[3,96,128]{2,1,0:T(8,128)(2,1)S(1)} %get-tuple-element.64), channel_id=1, source_target_pairs={{0,0},{1,16},{2,32},{3,48},{4,64},{5,80},{6,96},{7,112},{8,128},{9... | collective-permute-start | bytes 221192 | tf_op jit(solution)/shard_map/ppermute | solution.py:73
  32.3 12.6 %collective-permute-start.1 = (bf16[3,96,128]{2,1,0:T(8,128)(2,1)S(1)}, bf16[3,96,128]{2,1,0:T(8,128)(2,1)S(1)}, u32[]{:S(2)}, u32[]{:S(2)}) collective-permute-start(bf16[3,96,128]{2,1,0:T(8,128)(2,1)S(1)} %get-tuple-element.35), channel_id=1, source_target_pairs={{0,0},{1,16},{2,32},{3,48},{4,64},{5,80},{6,96},{7,112},{8,128},{9... | collective-permute-start | bytes 221192 | tf_op jit(solution)/shard_map/ppermute | solution.py:73
  37.2 48.6 %all-to-all-start.1 = ((bf16[16,3,144,128]{3,2,1,0:T(8,128)(2,1)}), bf16[16,3,144,128]{3,2,1,0:T(8,128)(2,1)S(1)}, u32[]{:S(2)}, u32[]{:S(2)}) async-start(bf16[16,3,144,128]{3,2,1,0:T(8,128)(2,1)} %pad_maximum_fusion), calls=%async_computation.1 | async-start | bytes 3538944 | tf_op jit(solution)/shard_map/all_to_all | solution.py:146
  44.9 8.0 %collective-permute-start.2 = (bf16[2,3,96,128]{3,2,1,0:T(8,128)(2,1)S(1)}, bf16[2,3,96,128]{3,2,1,0:T(8,128)(2,1)S(1)}, u32[]{:S(2)}, u32[]{:S(2)}) collective-permute-start(bf16[2,3,96,128]{3,2,1,0:T(8,128)(2,1)S(1)} %pad_maximum_fusion.1), channel_id=1, source_target_pairs={{0,2},{1,3},{2,0},{3,1},{4,6},{5,7},{6,4},{7,5},{8,10},{9,11},{10,... | collective-permute-start | bytes 442376 | tf_op jit(solution)/shard_map/ppermute | solution.py:48
  52.9 12.8 %collective-permute-start.3 = (bf16[2,2,3,96,128]{4,3,2,0,1:T(8,128)(2,1)S(1)}, bf16[2,2,3,96,128]{4,3,2,0,1:T(8,128)(2,1)S(1)}, u32[]{:S(2)}, u32[]{:S(2)}) collective-permute-start(bf16[2,2,3,96,128]{4,3,2,0,1:T(8,128)(2,1)S(1)} %bitcast_dynamic-update-slice_fusion.8), channel_id=1, source_target_pairs={{0,8},{1,9},{2,10},{3,11},{4,12},{5,13},{6,14},{7,15},{8,0},{9,1},... | collective-permute-start | bytes 884744 | tf_op jit(solution)/shard_map/ppermute | solution.py:48
  58.1 9.9 %collective-permute-start.4 = (bf16[2,2,3,96,128]{4,3,2,0,1:T(8,128)(2,1)S(1)}, bf16[2,2,3,96,128]{4,3,2,0,1:T(8,128)(2,1)S(1)}, u32[]{:S(2)}, u32[]{:S(2)}) collective-permute-start(bf16[2,2,3,96,128]{4,3,2,0,1:T(8,128)(2,1)S(1)} %bitcast_dynamic-update-slice_fusion.8), channel_id=1, source_target_pairs={{0,4},{1,5},{2,6},{3,7},{4,0},{5,1},{6,2},{7,3},{8,12},{9,13},{10,... | collective-permute-start | bytes 884744 | tf_op jit(solution)/shard_map/ppermute | solution.py:48
  58.1 11.0 %collective-permute-start.5 = (bf16[2,2,3,96,128]{4,3,2,0,1:T(8,128)(2,1)S(1)}, bf16[2,2,3,96,128]{4,3,2,0,1:T(8,128)(2,1)S(1)}, u32[]{:S(2)}, u32[]{:S(2)}) collective-permute-start(bf16[2,2,3,96,128]{4,3,2,0,1:T(8,128)(2,1)S(1)} %bitcast_dynamic-update-slice_fusion.8), channel_id=1, source_target_pairs={{0,12},{1,13},{2,14},{3,15},{4,8},{5,9},{6,10},{7,11},{8,4},{9,5},... | collective-permute-start | bytes 884744 | tf_op jit(solution)/shard_map/ppermute | solution.py:48
  58.9 14.6 %copy-start.29 = (f32[2,128]{1,0:T(2,128)S(1)}, f32[2,128]{1,0:T(2,128)}, u32[]{:S(2)}) copy-start(f32[2,128]{1,0:T(2,128)} %param.19) | copy-start | bytes 3076
  58.9 14.6 %copy-start.30 = (f32[2,128]{1,0:T(2,128)S(1)}, f32[2,128]{1,0:T(2,128)}, u32[]{:S(2)}) copy-start(f32[2,128]{1,0:T(2,128)} %param.18) | copy-start | bytes 3076
  69.1 5.7 %collective-permute-start.6 = (bf16[4,2,2,3,96,128]{5,4,3,1,0,2:T(8,128)(2,1)S(1)}, bf16[4,2,2,3,96,128]{5,4,3,1,0,2:T(8,128)(2,1)}, u32[]{:S(2)}, u32[]{:S(2)}) collective-permute-start(bf16[4,2,2,3,96,128]{5,4,3,1,0,2:T(8,128)(2,1)S(1)} %bitcast_dynamic-update-slice_fusion.7), channel_id=1, source_target_pairs={{0,1},{1,0},{2,3},{3,2},{4,5},{5,4},{6,7},{7,6},{8,9},{9,8},{10,11... | collective-permute-start | bytes 3538952 | tf_op jit(solution)/shard_map/ppermute | solution.py:48
  86.6 1.0 copy-start.6
  87.7 2.1 %copy-start.3 = (bf16[6,48,128]{2,1,0:T(8,128)(2,1)S(1)}, bf16[6,48,128]{2,1,0:T(8,128)(2,1)}, u32[]{:S(2)}) copy-start(bf16[6,48,128]{2,1,0:T(8,128)(2,1)} %pad_maximum_fusion.3) | copy-start | bytes 221188
  87.7 2.4 %copy-start.11 = (f32[128]{0:T(128)S(1)}, f32[128]{0:T(128)}, u32[]{:S(2)}) copy-start(f32[128]{0:T(128)} %copy-done.10) | copy-start | bytes 1540
  87.7 2.4 %copy-start.13 = (f32[128]{0:T(128)S(1)}, f32[128]{0:T(128)}, u32[]{:S(2)}) copy-start(f32[128]{0:T(128)} %copy-done.12) | copy-start | bytes 1540
  87.7 2.6 %copy-start.34 = (bf16[2,128,128]{2,1,0:T(8,128)(2,1)S(1)}, bf16[2,128,128]{2,1,0:T(8,128)(2,1)}, u32[]{:S(2)}) copy-start(bf16[2,128,128]{2,1,0:T(8,128)(2,1)} %param.21) | copy-start | bytes 196612
  89.6 0.9 copy-start.19
  89.6 0.9 copy-start.21
  89.6 1.3 copy-start.7
  90.1 1.3 copy-start.15
  90.1 1.3 copy-start.17
  90.3 1.3 copy-start.32
  90.9 1.0 copy-start.9
  90.9 1.0 copy-start.14
  92.1 14.9 %collective-permute-start.7 = (bf16[6,48,128]{2,1,0:T(8,128)(2,1)S(1)}, bf16[6,48,128]{2,1,0:T(8,128)(2,1)}, u32[]{:S(2)}, u32[]{:S(2)}) collective-permute-start(bf16[6,48,128]{2,1,0:T(8,128)(2,1)S(1)} %get-tuple-element.62), channel_id=1, source_target_pairs={{0,0},{1,16},{2,32},{3,48},{4,64},{5,80},{6,96},{7,112},{8,128},{9... | collective-permute-start | bytes 221192 | tf_op jit(solution)/shard_map/ppermute | solution.py:73
  101.7 10.4 %copy-start.2 = (bf16[16,1,3,96,128]{4,3,2,0,1:T(8,128)(2,1)S(1)}, bf16[16,1,3,96,128]{4,3,2,0,1:T(8,128)(2,1)}, u32[]{:S(2)}) copy-start(bf16[16,1,3,96,128]{4,3,2,0,1:T(8,128)(2,1)} %get-tuple-element.53) | copy-start | bytes 3538948
  101.7 36.6 %all-to-all-start.2 = ((bf16[16,6,48,128]{3,2,1,0:T(8,128)(2,1)}), bf16[16,6,48,128]{3,2,1,0:T(8,128)(2,1)}, u32[]{:S(2)}, u32[]{:S(2)}) async-start(bf16[16,6,48,128]{3,2,1,0:T(8,128)(2,1)} %broadcast_in_dim.23), calls=%async_computation.2 | async-start | bytes 2359296 | tf_op jit(solution)/shard_map/all_to_all | solution.py:160
  107.0 7.0 %collective-permute-start.8 = (bf16[6,48,128]{2,1,0:T(8,128)(2,1)}, bf16[6,48,128]{2,1,0:T(8,128)(2,1)}, u32[]{:S(2)}, u32[]{:S(2)}) collective-permute-start(bf16[6,48,128]{2,1,0:T(8,128)(2,1)} %collective-permute-done.7), channel_id=1, source_target_pairs={{0,2},{1,3},{2,0},{3,1},{4,6},{5,7},{6,4},{7,5},{8,10},{9,11},{10,... | collective-permute-start | bytes 221192 | tf_op jit(solution)/shard_map/ppermute | solution.py:48
  114.9 8.1 %collective-permute-start.9 = (bf16[2,6,48,128]{3,2,1,0:T(8,128)(2,1)S(1)}, bf16[2,6,48,128]{3,2,1,0:T(8,128)(2,1)S(1)}, u32[]{:S(2)}, u32[]{:S(2)}) collective-permute-start(bf16[2,6,48,128]{3,2,1,0:T(8,128)(2,1)S(1)} %bitcast_dynamic-update-slice_fusion.14), channel_id=1, source_target_pairs={{0,8},{1,9},{2,10},{3,11},{4,12},{5,13},{6,14},{7,15},{8,0},{9,1},... | collective-permute-start | bytes 442376 | tf_op jit(solution)/shard_map/ppermute | solution.py:48
  115.2 7.9 %collective-permute-start.10 = (bf16[2,6,48,128]{3,2,1,0:T(8,128)(2,1)S(1)}, bf16[2,6,48,128]{3,2,1,0:T(8,128)(2,1)S(1)}, u32[]{:S(2)}, u32[]{:S(2)}) collective-permute-start(bf16[2,6,48,128]{3,2,1,0:T(8,128)(2,1)S(1)} %bitcast_dynamic-update-slice_fusion.14), channel_id=1, source_target_pairs={{0,4},{1,5},{2,6},{3,7},{4,0},{5,1},{6,2},{7,3},{8,12},{9,13},{10,... | collective-permute-start | bytes 442376 | tf_op jit(solution)/shard_map/ppermute | solution.py:48
  118.0 5.4 %collective-permute-start.11 = (bf16[2,6,48,128]{3,2,1,0:T(8,128)(2,1)S(1)}, bf16[2,6,48,128]{3,2,1,0:T(8,128)(2,1)S(1)}, u32[]{:S(2)}, u32[]{:S(2)}) collective-permute-start(bf16[2,6,48,128]{3,2,1,0:T(8,128)(2,1)S(1)} %bitcast_dynamic-update-slice_fusion.14), channel_id=1, source_target_pairs={{0,12},{1,13},{2,14},{3,15},{4,8},{5,9},{6,10},{7,11},{8,4},{9,5},... | collective-permute-start | bytes 442376 | tf_op jit(solution)/shard_map/ppermute | solution.py:48
  121.6 0.7 copy-start.20
  122.9 1.3 copy-start.4
  123.4 5.3 %collective-permute-start.12 = (bf16[4,2,6,48,128]{4,3,2,1,0:T(8,128)(2,1)S(1)}, bf16[4,2,6,48,128]{4,3,2,1,0:T(8,128)(2,1)S(1)}, u32[]{:S(2)}, u32[]{:S(2)}) collective-permute-start(bf16[4,2,6,48,128]{4,3,2,1,0:T(8,128)(2,1)S(1)} %bitcast_dynamic-update-slice_fusion.10), channel_id=1, source_target_pairs={{0,1},{1,0},{2,3},{3,2},{4,5},{5,4},{6,7},{7,6},{8,9},{9,8},{10,11... | collective-permute-start | bytes 1769480 | tf_op jit(solution)/shard_map/ppermute | solution.py:48
  125.9 1.3 copy-start.35
  128.8 1.0 copy-start.1
  143.7 0.7 copy-start.25
  144.4 1.3 copy-start.5
  (4 other events, 2.7 us)
where the time goes:
time: 148 us; the launch traced here: 147 us
  starting transfers between devices  58 us (39%)
  waiting for transfers between devices  31.7 us (21%)
  local copies, waits for them, and re-layouts  23.4 us (16%)
  matrix products  13.1 us (9%)
  between operations  11.4 us (8%)
  other arithmetic  9.53 us (6%)
    ppermute x3, starting transfers between devices, transpose_devices(): return lax.ppermute(x, ('row', 'col'), pairs)  21.4 us
    ppermute x10, starting transfers between devices, swap(): return lax.ppermute(x, axis, [(p, p ^ bits) for p in range(n)])  19.2 us
    ppermute x10, waiting for transfers between devices, swap(): return lax.ppermute(x, axis, [(p, p ^ bits) for p in range(n)])  13.8 us
    all_to_all x1, starting transfers between devices, body(): lax.all_to_all(pair_rep.reshape(n, part, tile, width), 'col', 0, 0, tiled...  7.6 us
    all_to_all x1, waiting for transfers between devices, body(): chunks = lax.all_to_all(chunks, 'row', 0, 0, tiled=True)  6.83 us
    all_to_all x1, waiting for transfers between devices, body(): lax.all_to_all(copies, 'row', 0, 0, tiled=True)  6.09 us
    all_to_all x1, starting transfers between devices, body(): chunks = lax.all_to_all(chunks, 'row', 0, 0, tiled=True)  5.24 us
    all_to_all x1, starting transfers between devices, body(): lax.all_to_all(copies, 'row', 0, 0, tiled=True)  4.51 us
  transfers between devices with their start and end apart: 16, of which 10 were waited for; matrix products, arithmetic and copies ran while one was open for 19% of the time, Pallas kernels for 0%

commit v1 on v0

--- a/solution.py
+++ b/solution.py
@@ -144,8 +144,9 @@
     chunks = jnp.concatenate([jnp.broadcast_to(right_moved, (n,) + right_moved.shape), rows], axis=2)
     chunks, left_own = lax.optimization_barrier((chunks, left_own))
     chunks = lax.all_to_all(chunks, "row", 0, 0, tiled=True)
-    rows = jnp.concatenate(pick(chunks[:, :, 2 * tile :], 1), axis=0)
+    rows = pick(chunks[:, :, 2 * tile :], 1)
     chunks, rows = lax.optimization_barrier((chunks, rows))
+    rows = jnp.concatenate(rows, axis=0)
     right = chunks[:, :, : 2 * tile].reshape(tile, 2 * tile, hidden)
     lefts, _ = gather_col(jnp.stack([left_own, left_moved]), places)
     left = lefts[:, 0].reshape(tile, 2 * tile, hidden)
@@ -168,12 +169,13 @@
     next_left, scaled = gather_col(next_left, places, left, main_tile)
     next_left = next_left.reshape(2 * tile, tile, hidden)
     current = finish(pair_rep, scaled, gate, w_out[0])
-    gate = gate_of(norm_in(current, 1), 1)
+    gate = gate_of(norm_in(current, 1), 1).reshape(current.shape)
+    kept = lax.optimization_barrier(jnp.stack([gate, current.astype(jnp.float32)]))
 
     contracted = jnp.einsum(
         "kih,kjh->hij", next_left, next_right, preferred_element_type=jnp.float32
     )
-    return finish(current, scale(spread_of(contracted), 1), gate, w_out[1])
+    return finish(kept[1], scale(spread_of(contracted), 1), kept[0], w_out[1])
 
 
 def solution(mesh):

time: 148 us -> 148 us (level); the launches traced: 147 us -> 146 us
  starting transfers between devices: 58 us -> 51.6 us
  waiting for transfers between devices: 31.7 us -> 36.6 us
    ppermute x10, starting transfers between devices: 19.2 us -> 15.4 us  [swap(): return lax.ppermute(x, axis, [(p, p ^ bits) for p in range(n)])]
    ppermute x10, waiting for transfers between devices: 13.8 us -> 16.7 us  [swap(): return lax.ppermute(x, axis, [(p, p ^ bits) for p in range(n)])]
    all_to_all x1, waiting for transfers between devices: 6.83 us -> 8.84 us  [body(): chunks = lax.all_to_all(chunks, 'row', 0, 0, tiled=True)]
    ppermute x3, starting transfers between devices: 21.4 us -> 19.4 us  [transpose_devices(): return lax.ppermute(x, ('row', 'col'), pairs)]
    another operation x0 -> x2, other arithmetic: none -> 1.67 us  [body(): jnp.stack([gate, current.astype(jnp.float32)])]
    ppermute x3, waiting for transfers between devices: 3.15 us -> 4.78 us  [transpose_devices(): return lax.ppermute(x, ('row', 'col'), pairs)]
  transfers between devices with their start and end apart: 16 -> 16, of which waited for: 10 -> 12; matrix products, arithmetic and copies ran while one was open for 19% -> 20% of each run, Pallas kernels for 0% -> 0%
where the time goes in v1:
time: 148 us; the launch traced here: 146 us
  starting transfers between devices  51.6 us (35%)
  waiting for transfers between devices  36.6 us (25%)
  local copies, waits for them, and re-layouts  23.3 us (16%)
  matrix products  12.1 us (8%)
  between operations  11.4 us (8%)
  other arithmetic  10.6 us (7%)
    ppermute x3, starting transfers between devices, transpose_devices(): return lax.ppermute(x, ('row', 'col'), pairs)  19.4 us
    ppermute x10, waiting for transfers between devices, swap(): return lax.ppermute(x, axis, [(p, p ^ bits) for p in range(n)])  16.7 us
    ppermute x10, starting transfers between devices, swap(): return lax.ppermute(x, axis, [(p, p ^ bits) for p in range(n)])  15.4 us
    all_to_all x1, waiting for transfers between devices, body(): chunks = lax.all_to_all(chunks, 'row', 0, 0, tiled=True)  8.84 us
    all_to_all x1, starting transfers between devices, body(): lax.all_to_all(pair_rep.reshape(n, part, tile, width), 'col', 0, 0, tiled...  7.6 us
    all_to_all x1, starting transfers between devices, body(): chunks = lax.all_to_all(chunks, 'row', 0, 0, tiled=True)  5.24 us
    ppermute x3, waiting for transfers between devices, transpose_devices(): return lax.ppermute(x, ('row', 'col'), pairs)  4.78 us
    all_to_all x1, waiting for transfers between devices, body(): lax.all_to_all(copies, 'row', 0, 0, tiled=True)  4.63 us
  transfers between devices with their start and end apart: 16, of which 12 were waited for; matrix products, arithmetic and copies ran while one was open for 20% of the time, Pallas kernels for 0%

profile of v1, /device:TPU:4, one launch (start us, length us, event | category | flops | bytes accessed | tf_op | source)
XLA Modules:
  0.0 145.6 jit_solution(15940930689583799959)
XLA Ops:
  0.0 7.6 %all-to-all-start = ((bf16[16,3,48,128]{3,2,1,0:T(8,128)(2,1)}), bf16[16,3,48,128]{3,2,1,0:T(8,128)(2,1)S(1)}, u32[]{:S(2)}, u32[]{:S(2)}) async-start(bf16[16,3,48,128]{3,2,1,0:T(8,128)(2,1)} %bitcast.171), calls=%async_computation | async-start | bytes 1179648 | tf_op jit(solution)/shard_map/all_to_all | solution.py:130
  13.9 0.7 mul.293
  16.7 1.6 %all-to-all-done = bf16[16,3,48,128]{3,2,1,0:T(8,128)(2,1)S(1)} async-done(((bf16[16,3,48,128]{3,2,1,0:T(8,128)(2,1)}), bf16[16,3,48,128]{3,2,1,0:T(8,128)(2,1)S(1)}, u32[]{:S(2)}, u32[]{:S(2)}) %all-to-all-start) | async-done | bytes 589856 | tf_op jit(solution)/shard_map/all_to_all | solution.py:130
  19.3 11.0 %collective-permute-start = (bf16[3,96,128]{2,1,0:T(8,128)(2,1)S(1)}, bf16[3,96,128]{2,1,0:T(8,128)(2,1)S(1)}, u32[]{:S(2)}, u32[]{:S(2)}) collective-permute-start(bf16[3,96,128]{2,1,0:T(8,128)(2,1)S(1)} %get-tuple-element.66), channel_id=1, source_target_pairs={{0,0},{1,16},{2,32},{3,48},{4,64},{5,80},{6,96},{7,112},{8,128},{9... | collective-permute-start | bytes 221192 | tf_op jit(solution)/shard_map/ppermute | solution.py:73
  30.8 0.7 fusion.27
  31.5 0.8 fusion.30
  32.3 1.9 %collective-permute-start.1 = (bf16[3,96,128]{2,1,0:T(8,128)(2,1)S(1)}, bf16[3,96,128]{2,1,0:T(8,128)(2,1)S(1)}, u32[]{:S(2)}, u32[]{:S(2)}) collective-permute-start(bf16[3,96,128]{2,1,0:T(8,128)(2,1)S(1)} %get-tuple-element.37), channel_id=1, source_target_pairs={{0,0},{1,16},{2,32},{3,48},{4,64},{5,80},{6,96},{7,112},{8,128},{9... | collective-permute-start | bytes 221192 | tf_op jit(solution)/shard_map/ppermute | solution.py:73
  34.2 1.5 %fusion.5 = f32[2304,128]{1,0:T(8,128)} fusion(bf16[2304,128]{1,0:T(8,128)(2,1)S(1)} %bitcast.185, bf16[2,128,128]{2,1,0:T(8,128)(2,1)S(1)} %copy-done.33), kind=kOutput, calls=%fused_computation.7 | convolution fusion | flops 76382208 | bytes 1802240 | tf_op jit(solution)/shard_map/dot_general | solution.py:26
  35.9 1.4 pad_maximum_fusion.1
  37.2 5.2 %all-to-all-start.1 = ((bf16[16,3,144,128]{3,2,1,0:T(8,128)(2,1)}), bf16[16,3,144,128]{3,2,1,0:T(8,128)(2,1)S(1)}, u32[]{:S(2)}, u32[]{:S(2)}) async-start(bf16[16,3,144,128]{3,2,1,0:T(8,128)(2,1)} %pad_maximum_fusion.1), calls=%async_computation.1 | async-start | bytes 3538944 | tf_op jit(solution)/shard_map/all_to_all | solution.py:146
  42.5 2.4 %collective-permute-done.1 = bf16[3,96,128]{2,1,0:T(8,128)(2,1)S(1)} collective-permute-done((bf16[3,96,128]{2,1,0:T(8,128)(2,1)S(1)}, bf16[3,96,128]{2,1,0:T(8,128)(2,1)S(1)}, u32[]{:S(2)}, u32[]{:S(2)}) %collective-permute-start.1) | collective-permute-done | bytes 73760 | tf_op jit(solution)/shard_map/ppermute | solution.py:73
  44.9 4.3 %collective-permute-start.2 = (bf16[2,3,96,128]{3,2,1,0:T(8,128)(2,1)S(1)}, bf16[2,3,96,128]{3,2,1,0:T(8,128)(2,1)S(1)}, u32[]{:S(2)}, u32[]{:S(2)}) collective-permute-start(bf16[2,3,96,128]{3,2,1,0:T(8,128)(2,1)S(1)} %pad_maximum_fusion.2), channel_id=1, source_target_pairs={{0,2},{1,3},{2,0},{3,1},{4,6},{5,7},{6,4},{7,5},{8,10},{9,11},{10,... | collective-permute-start | bytes 442376 | tf_op jit(solution)/shard_map/ppermute | solution.py:48
  49.3 3.5 %collective-permute-done.2 = bf16[2,3,96,128]{3,2,1,0:T(8,128)(2,1)S(1)} collective-permute-done((bf16[2,3,96,128]{3,2,1,0:T(8,128)(2,1)S(1)}, bf16[2,3,96,128]{3,2,1,0:T(8,128)(2,1)S(1)}, u32[]{:S(2)}, u32[]{:S(2)}) %collective-permute-start.2) | collective-permute-done | bytes 147488 | tf_op jit(solution)/shard_map/ppermute | solution.py:48
  52.8 5.3 %collective-permute-start.3 = (bf16[2,2,3,96,128]{4,3,2,0,1:T(8,128)(2,1)S(1)}, bf16[2,2,3,96,128]{4,3,2,0,1:T(8,128)(2,1)S(1)}, u32[]{:S(2)}, u32[]{:S(2)}) collective-permute-start(bf16[2,2,3,96,128]{4,3,2,0,1:T(8,128)(2,1)S(1)} %bitcast_dynamic-update-slice_fusion.8), channel_id=1, source_target_pairs={{0,8},{1,9},{2,10},{3,11},{4,12},{5,13},{6,14},{7,15},{8,0},{9,1},... | collective-permute-start | bytes 884744 | tf_op jit(solution)/shard_map/ppermute | solution.py:48
  58.1 0.7 collective-permute-start.5
  59.0 6.5 %collective-permute-done.3 = bf16[2,2,3,96,128]{4,3,2,0,1:T(8,128)(2,1)S(1)} collective-permute-done((bf16[2,2,3,96,128]{4,3,2,0,1:T(8,128)(2,1)S(1)}, bf16[2,2,3,96,128]{4,3,2,0,1:T(8,128)(2,1)S(1)}, u32[]{:S(2)}, u32[]{:S(2)}) %collective-permute-start.3) | collective-permute-done | bytes 294944 | tf_op jit(solution)/shard_map/ppermute | solution.py:48
  65.6 2.5 %collective-permute-done.4 = bf16[2,2,3,96,128]{4,3,2,0,1:T(8,128)(2,1)S(1)} collective-permute-done((bf16[2,2,3,96,128]{4,3,2,0,1:T(8,128)(2,1)S(1)}, bf16[2,2,3,96,128]{4,3,2,0,1:T(8,128)(2,1)S(1)}, u32[]{:S(2)}, u32[]{:S(2)}) %collective-permute-start.4) | collective-permute-done | bytes 294944 | tf_op jit(solution)/shard_map/ppermute | solution.py:48
  68.1 1.2 collective-permute-done.5
  74.8 1.4 bitcast_dynamic-update-slice_fusion.1
  76.2 1.2 fusion.92
  77.4 0.8 copy.38
  78.2 0.8 copy.39
  79.0 8.8 %all-to-all-done.1 = bf16[16,3,144,128]{3,2,1,0:T(8,128)(2,1)S(1)} async-done(((bf16[16,3,144,128]{3,2,1,0:T(8,128)(2,1)}), bf16[16,3,144,128]{3,2,1,0:T(8,128)(2,1)S(1)}, u32[]{:S(2)}, u32[]{:S(2)}) %all-to-all-start.1) | async-done | bytes 1769504 | tf_op jit(solution)/shard_map/all_to_all | solution.py:146
  88.6 1.0 copy.40
  89.7 1.9 %fusion.96 = (f32[6,48]{1,0:T(8,128)S(1)}, f32[128,6,48]{2,1,0:T(8,128)S(1)}) fusion(bf16[48,96,128]{1,0,2:T(8,128)(2,1)S(1)} %copy.40, bf16[3,96,128]{1,0,2:T(4,128)(2,1)} %bitcast.188, bf16[3,96,128]{1,0,2:T(4,128)(2,1)S(1)} %bitcast.187), kind=kOutput, calls=%fused_computation.175 | convolution fusion | flops 7409376 | bytes 1475712 | tf_op jit(solution)/shard_map/ikh,jkh->hij/dot_general | solution.py:155
  94.1 6.5 %collective-permute-start.7 = (bf16[6,48,128]{2,1,0:T(8,128)(2,1)S(1)}, bf16[6,48,128]{2,1,0:T(8,128)(2,1)}, u32[]{:S(2)}, u32[]{:S(2)}) collective-permute-start(bf16[6,48,128]{2,1,0:T(8,128)(2,1)S(1)} %get-tuple-element.64), channel_id=1, source_target_pairs={{0,0},{1,16},{2,32},{3,48},{4,64},{5,80},{6,96},{7,112},{8,128},{9... | collective-permute-start | bytes 221192 | tf_op jit(solution)/shard_map/ppermute | solution.py:73
  100.6 1.2 broadcast_in_dim.23
  101.8 4.0 %all-to-all-start.2 = ((bf16[16,6,48,128]{3,2,1,0:T(8,128)(2,1)}), bf16[16,6,48,128]{3,2,1,0:T(8,128)(2,1)S(1)}, u32[]{:S(2)}, u32[]{:S(2)}) async-start(bf16[16,6,48,128]{3,2,1,0:T(8,128)(2,1)} %broadcast_in_dim.23), calls=%async_computation.2 | async-start | bytes 2359296 | tf_op jit(solution)/shard_map/all_to_all | solution.py:161
  105.8 2.4 %collective-permute-done.7 = bf16[6,48,128]{2,1,0:T(8,128)(2,1)} collective-permute-done((bf16[6,48,128]{2,1,0:T(8,128)(2,1)S(1)}, bf16[6,48,128]{2,1,0:T(8,128)(2,1)}, u32[]{:S(2)}, u32[]{:S(2)}) %collective-permute-start.7) | collective-permute-done | bytes 73760 | tf_op jit(solution)/shard_map/ppermute | solution.py:73
  108.6 0.9 bitcast_dynamic-update-slice_fusion.15
  109.5 2.8 %copy.42 = bf16[48,96,128]{1,0,2:T(8,128)(2,1)} copy(bf16[48,96,128]{2,1,0:T(8,128)(2,1)} %bitcast.178) | data formatting | bytes 2359296 | tf_op jit(solution)/shard_map/optimization_barrier | solution.py:167
  112.3 2.1 %collective-permute-done.8 = bf16[6,48,128]{2,1,0:T(8,128)(2,1)} collective-permute-done((bf16[6,48,128]{2,1,0:T(8,128)(2,1)}, bf16[6,48,128]{2,1,0:T(8,128)(2,1)}, u32[]{:S(2)}, u32[]{:S(2)}) %collective-permute-start.8) | collective-permute-done | bytes 73760 | tf_op jit(solution)/shard_map/ppermute | solution.py:48
  114.4 0.9 bitcast_dynamic-update-slice_fusion.14
  115.5 2.1 %collective-permute-start.10 = (bf16[2,6,48,128]{3,2,1,0:T(8,128)(2,1)S(1)}, bf16[2,6,48,128]{3,2,1,0:T(8,128)(2,1)S(1)}, u32[]{:S(2)}, u32[]{:S(2)}) collective-permute-start(bf16[2,6,48,128]{3,2,1,0:T(8,128)(2,1)S(1)} %bitcast_dynamic-update-slice_fusion.14), channel_id=1, source_target_pairs={{0,4},{1,5},{2,6},{3,7},{4,0},{5,1},{6,2},{7,3},{8,12},{9,13},{10,... | collective-permute-start | bytes 442376 | tf_op jit(solution)/shard_map/ppermute | solution.py:48
  117.6 2.0 %collective-permute-start.11 = (bf16[2,6,48,128]{3,2,1,0:T(8,128)(2,1)S(1)}, bf16[2,6,48,128]{3,2,1,0:T(8,128)(2,1)S(1)}, u32[]{:S(2)}, u32[]{:S(2)}) collective-permute-start(bf16[2,6,48,128]{3,2,1,0:T(8,128)(2,1)S(1)} %bitcast_dynamic-update-slice_fusion.14), channel_id=1, source_target_pairs={{0,12},{1,13},{2,14},{3,15},{4,8},{5,9},{6,10},{7,11},{8,4},{9,5},... | collective-permute-start | bytes 442376 | tf_op jit(solution)/shard_map/ppermute | solution.py:48
  119.6 2.3 %fusion.98 = (f32[48,48]{1,0:T(8,128)S(1)}, f32[128,48,48]{2,1,0:T(8,128)S(1)}) fusion(bf16[128,48,96]{2,1,0:T(8,128)(2,1)} %bitcast.174, bf16[48,96,128]{1,0,2:T(8,128)(2,1)S(1)} %copy.40), kind=kOutput, calls=%fused_computation.177 | convolution fusion | flops 56915712 | bytes 3548160 | tf_op jit(solution)/shard_map/hik,jkh->hij/dot_general | solution.py:164
  123.5 0.9 collective-permute-done.11
  124.6 0.8 convert_reduce_fusion
  125.4 0.7 fusion.23
  126.2 0.8 fusion.26
  127.5 1.6 %pad_maximum_fusion = f32[2,48,48,128]{3,2,1,0:T(8,128)} fusion(f32[1,48,48,128]{3,2,1,0:T(8,128)S(1)} %convert_bitcast_fusion, f32[1,48,48,128]{3,2,1,0:T(8,128)S(1)} %bitcast.180), kind=kLoop, calls=%fused_computation.12 | loop fusion | flops 589824 | bytes 4718592 | tf_op jit(solution)/shard_map/stack | solution.py:173
  129.5 1.0 copy-done.2
  130.5 2.4 %copy.47 = bf16[96,48,128]{0,1,2:T(8,128)(2,1)S(1)} copy(bf16[96,48,128]{2,1,0:T(8,128)(2,1)} %bitcast.176) | data formatting | bytes 2359296 | tf_op jit(solution)/shard_map/reshape;reshape | solution.py:170
  132.9 4.6 %all-to-all-done.2 = bf16[16,6,48,128]{3,2,1,0:T(8,128)(2,1)S(1)} async-done(((bf16[16,6,48,128]{3,2,1,0:T(8,128)(2,1)}), bf16[16,6,48,128]{3,2,1,0:T(8,128)(2,1)S(1)}, u32[]{:S(2)}, u32[]{:S(2)}) %all-to-all-start.2) | async-done | bytes 1179680 | tf_op jit(solution)/shard_map/all_to_all | solution.py:161
  137.5 2.0 %copy.48 = bf16[96,48,128]{0,1,2:T(8,128)(2,1)} copy(bf16[96,48,128]{2,1,0:T(8,128)(2,1)S(1)} %bitcast.175) | data formatting | bytes 2359296 | tf_op jit(solution)/shard_map/reshape | solution.py:161
  139.6 2.3 %fusion.99 = (f32[48,48]{1,0:T(8,128)S(1)}, f32[128,48,48]{2,1,0:T(8,128)S(1)}) fusion(bf16[96,48,128]{0,1,2:T(8,128)(2,1)S(1)} %copy.47, bf16[96,48,128]{0,1,2:T(8,128)(2,1)} %copy.48), kind=kOutput, calls=%fused_computation.178 | convolution fusion | flops 56915712 | bytes 3548160 | tf_op jit(solution)/shard_map/kih,kjh->hij/dot_general | solution.py:175
  143.2 1.1 copy-done.1
  144.2 1.4 fusion.20
  (159 shorter events, 12.7 us)
Async XLA Ops:
  0.0 7.6 %copy-start.24 = (s32[2,2]{1,0:T(2,128)S(1)}, s32[2,2]{1,0:T(2,128)}, u32[]{:S(2)}) copy-start(s32[2,2]{1,0:T(2,128)} %param.13) | copy-start | bytes 52
  0.0 13.5 %copy-start.23 = (s32[768]{0:T(1024)S(1)}, s32[768]{0:T(1024)}, u32[]{:S(2)}) copy-start(s32[768]{0:T(1024)} %param.12) | copy-start | bytes 9220
  0.0 16.1 %copy-start.28 = (f32[2,128]{1,0:T(2,128)S(1)}, f32[2,128]{1,0:T(2,128)}, u32[]{:S(2)}) copy-start(f32[2,128]{1,0:T(2,128)} %param.14) | copy-start | bytes 3076
  0.0 16.1 %copy-start.27 = (f32[2,128]{1,0:T(2,128)S(1)}, f32[2,128]{1,0:T(2,128)}, u32[]{:S(2)}) copy-start(f32[2,128]{1,0:T(2,128)} %param.15) | copy-start | bytes 3076
  0.0 18.8 %copy-start.31 = (bf16[2,128,256]{2,1,0:T(8,128)(2,1)S(1)}, bf16[2,128,256]{2,1,0:T(8,128)(2,1)}, u32[]{:S(2)}) copy-start(bf16[2,128,256]{2,1,0:T(8,128)(2,1)} %param.17) | copy-start | bytes 393220
  0.0 18.3 %all-to-all-start = ((bf16[16,3,48,128]{3,2,1,0:T(8,128)(2,1)}), bf16[16,3,48,128]{3,2,1,0:T(8,128)(2,1)S(1)}, u32[]{:S(2)}, u32[]{:S(2)}) async-start(bf16[16,3,48,128]{3,2,1,0:T(8,128)(2,1)} %bitcast.171), calls=%async_computation | async-start | bytes 1179648 | tf_op jit(solution)/shard_map/all_to_all | solution.py:130
  7.6 11.5 %copy-start.8 = (bf16[2,128,256]{2,1,0:T(8,128)(2,1)S(1)}, bf16[2,128,256]{2,1,0:T(8,128)(2,1)}, u32[]{:S(2)}) copy-start(bf16[2,128,256]{2,1,0:T(8,128)(2,1)} %param.16) | copy-start | bytes 393220
  16.7 14.8 %copy-start.10 = (f32[128]{0:T(128)}, f32[128]{0:T(128)S(1)}, u32[]{:S(2)}) copy-start(f32[128]{0:T(128)S(1)} %get-tuple-element.80) | copy-start | bytes 1540
  16.7 14.8 %copy-start.12 = (f32[128]{0:T(128)}, f32[128]{0:T(128)S(1)}, u32[]{:S(2)}) copy-start(f32[128]{0:T(128)S(1)} %get-tuple-element.95) | copy-start | bytes 1540
  18.7 11.7 %copy-start = (bf16[48,48,128]{2,1,0:T(8,128)(2,1)S(1)}, bf16[48,48,128]{2,1,0:T(8,128)(2,1)}, u32[]{:S(2)}) copy-start(bf16[48,48,128]{2,1,0:T(8,128)(2,1)} %param.11) | copy-start | bytes 1769476
  19.3 14.9 %copy-start.33 = (bf16[2,128,128]{2,1,0:T(8,128)(2,1)S(1)}, bf16[2,128,128]{2,1,0:T(8,128)(2,1)}, u32[]{:S(2)}) copy-start(bf16[2,128,128]{2,1,0:T(8,128)(2,1)} %param.21) | copy-start | bytes 196612
  19.3 16.4 %collective-permute-start = (bf16[3,96,128]{2,1,0:T(8,128)(2,1)S(1)}, bf16[3,96,128]{2,1,0:T(8,128)(2,1)S(1)}, u32[]{:S(2)}, u32[]{:S(2)}) collective-permute-start(bf16[3,96,128]{2,1,0:T(8,128)(2,1)S(1)} %get-tuple-element.66), channel_id=1, source_target_pairs={{0,0},{1,16},{2,32},{3,48},{4,64},{5,80},{6,96},{7,112},{8,128},{9... | collective-permute-start | bytes 221192 | tf_op jit(solution)/shard_map/ppermute | solution.py:73
  32.3 12.6 %collective-permute-start.1 = (bf16[3,96,128]{2,1,0:T(8,128)(2,1)S(1)}, bf16[3,96,128]{2,1,0:T(8,128)(2,1)S(1)}, u32[]{:S(2)}, u32[]{:S(2)}) collective-permute-start(bf16[3,96,128]{2,1,0:T(8,128)(2,1)S(1)} %get-tuple-element.37), channel_id=1, source_target_pairs={{0,0},{1,16},{2,32},{3,48},{4,64},{5,80},{6,96},{7,112},{8,128},{9... | collective-permute-start | bytes 221192 | tf_op jit(solution)/shard_map/ppermute | solution.py:73
  37.2 50.6 %all-to-all-start.1 = ((bf16[16,3,144,128]{3,2,1,0:T(8,128)(2,1)}), bf16[16,3,144,128]{3,2,1,0:T(8,128)(2,1)S(1)}, u32[]{:S(2)}, u32[]{:S(2)}) async-start(bf16[16,3,144,128]{3,2,1,0:T(8,128)(2,1)} %pad_maximum_fusion.1), calls=%async_computation.1 | async-start | bytes 3538944 | tf_op jit(solution)/shard_map/all_to_all | solution.py:146
  44.9 7.9 %collective-permute-start.2 = (bf16[2,3,96,128]{3,2,1,0:T(8,128)(2,1)S(1)}, bf16[2,3,96,128]{3,2,1,0:T(8,128)(2,1)S(1)}, u32[]{:S(2)}, u32[]{:S(2)}) collective-permute-start(bf16[2,3,96,128]{3,2,1,0:T(8,128)(2,1)S(1)} %pad_maximum_fusion.2), channel_id=1, source_target_pairs={{0,2},{1,3},{2,0},{3,1},{4,6},{5,7},{6,4},{7,5},{8,10},{9,11},{10,... | collective-permute-start | bytes 442376 | tf_op jit(solution)/shard_map/ppermute | solution.py:48
  52.8 12.7 %collective-permute-start.3 = (bf16[2,2,3,96,128]{4,3,2,0,1:T(8,128)(2,1)S(1)}, bf16[2,2,3,96,128]{4,3,2,0,1:T(8,128)(2,1)S(1)}, u32[]{:S(2)}, u32[]{:S(2)}) collective-permute-start(bf16[2,2,3,96,128]{4,3,2,0,1:T(8,128)(2,1)S(1)} %bitcast_dynamic-update-slice_fusion.8), channel_id=1, source_target_pairs={{0,8},{1,9},{2,10},{3,11},{4,12},{5,13},{6,14},{7,15},{8,0},{9,1},... | collective-permute-start | bytes 884744 | tf_op jit(solution)/shard_map/ppermute | solution.py:48
  58.1 9.9 %collective-permute-start.4 = (bf16[2,2,3,96,128]{4,3,2,0,1:T(8,128)(2,1)S(1)}, bf16[2,2,3,96,128]{4,3,2,0,1:T(8,128)(2,1)S(1)}, u32[]{:S(2)}, u32[]{:S(2)}) collective-permute-start(bf16[2,2,3,96,128]{4,3,2,0,1:T(8,128)(2,1)S(1)} %bitcast_dynamic-update-slice_fusion.8), channel_id=1, source_target_pairs={{0,4},{1,5},{2,6},{3,7},{4,0},{5,1},{6,2},{7,3},{8,12},{9,13},{10,... | collective-permute-start | bytes 884744 | tf_op jit(solution)/shard_map/ppermute | solution.py:48
  58.1 11.2 %collective-permute-start.5 = (bf16[2,2,3,96,128]{4,3,2,0,1:T(8,128)(2,1)S(1)}, bf16[2,2,3,96,128]{4,3,2,0,1:T(8,128)(2,1)S(1)}, u32[]{:S(2)}, u32[]{:S(2)}) collective-permute-start(bf16[2,2,3,96,128]{4,3,2,0,1:T(8,128)(2,1)S(1)} %bitcast_dynamic-update-slice_fusion.8), channel_id=1, source_target_pairs={{0,12},{1,13},{2,14},{3,15},{4,8},{5,9},{6,10},{7,11},{8,4},{9,5},... | collective-permute-start | bytes 884744 | tf_op jit(solution)/shard_map/ppermute | solution.py:48
  59.0 14.5 %copy-start.29 = (f32[2,128]{1,0:T(2,128)S(1)}, f32[2,128]{1,0:T(2,128)}, u32[]{:S(2)}) copy-start(f32[2,128]{1,0:T(2,128)} %param.19) | copy-start | bytes 3076
  59.0 14.5 %copy-start.30 = (f32[2,128]{1,0:T(2,128)S(1)}, f32[2,128]{1,0:T(2,128)}, u32[]{:S(2)}) copy-start(f32[2,128]{1,0:T(2,128)} %param.18) | copy-start | bytes 3076
  69.4 5.4 %collective-permute-start.6 = (bf16[4,2,2,3,96,128]{5,4,3,1,0,2:T(8,128)(2,1)S(1)}, bf16[4,2,2,3,96,128]{5,4,3,1,0,2:T(8,128)(2,1)}, u32[]{:S(2)}, u32[]{:S(2)}) collective-permute-start(bf16[4,2,2,3,96,128]{5,4,3,1,0,2:T(8,128)(2,1)S(1)} %bitcast_dynamic-update-slice_fusion.7), channel_id=1, source_target_pairs={{0,1},{1,0},{2,3},{3,2},{4,5},{5,4},{6,7},{7,6},{8,9},{9,8},{10,11... | collective-permute-start | bytes 3538952 | tf_op jit(solution)/shard_map/ppermute | solution.py:48
  88.6 1.0 copy-start.6
  89.7 2.1 %copy-start.4 = (bf16[3,48,128]{2,1,0:T(8,128)(2,1)S(1)}, bf16[3,48,128]{2,1,0:T(8,128)(2,1)}, u32[]{:S(2)}) copy-start(bf16[3,48,128]{2,1,0:T(8,128)(2,1)} %get-tuple-element.36) | copy-start | bytes 110596
  89.7 2.1 %copy-start.5 = (bf16[3,48,128]{2,1,0:T(8,128)(2,1)S(1)}, bf16[3,48,128]{2,1,0:T(8,128)(2,1)}, u32[]{:S(2)}) copy-start(bf16[3,48,128]{2,1,0:T(8,128)(2,1)} %get-tuple-element.35) | copy-start | bytes 110596
  89.7 2.4 %copy-start.11 = (f32[128]{0:T(128)S(1)}, f32[128]{0:T(128)}, u32[]{:S(2)}) copy-start(f32[128]{0:T(128)} %copy-done.10) | copy-start | bytes 1540
  89.7 2.4 %copy-start.13 = (f32[128]{0:T(128)S(1)}, f32[128]{0:T(128)}, u32[]{:S(2)}) copy-start(f32[128]{0:T(128)} %copy-done.12) | copy-start | bytes 1540
  89.7 2.6 %copy-start.34 = (bf16[2,128,128]{2,1,0:T(8,128)(2,1)S(1)}, bf16[2,128,128]{2,1,0:T(8,128)(2,1)}, u32[]{:S(2)}) copy-start(bf16[2,128,128]{2,1,0:T(8,128)(2,1)} %param.21) | copy-start | bytes 196612
  91.6 0.9 copy-start.19
  91.6 1.0 copy-start.21
  91.6 1.3 copy-start.7
  92.1 1.3 copy-start.15
  92.1 1.3 copy-start.17
  92.3 1.3 copy-start.32
  92.9 1.0 copy-start.9
  92.9 1.0 copy-start.14
  94.1 14.1 %collective-permute-start.7 = (bf16[6,48,128]{2,1,0:T(8,128)(2,1)S(1)}, bf16[6,48,128]{2,1,0:T(8,128)(2,1)}, u32[]{:S(2)}, u32[]{:S(2)}) collective-permute-start(bf16[6,48,128]{2,1,0:T(8,128)(2,1)S(1)} %get-tuple-element.64), channel_id=1, source_target_pairs={{0,0},{1,16},{2,32},{3,48},{4,64},{5,80},{6,96},{7,112},{8,128},{9... | collective-permute-start | bytes 221192 | tf_op jit(solution)/shard_map/ppermute | solution.py:73
  101.8 35.7 %all-to-all-start.2 = ((bf16[16,6,48,128]{3,2,1,0:T(8,128)(2,1)}), bf16[16,6,48,128]{3,2,1,0:T(8,128)(2,1)S(1)}, u32[]{:S(2)}, u32[]{:S(2)}) async-start(bf16[16,6,48,128]{3,2,1,0:T(8,128)(2,1)} %broadcast_in_dim.23), calls=%async_computation.2 | async-start | bytes 2359296 | tf_op jit(solution)/shard_map/all_to_all | solution.py:161
  108.2 6.2 %collective-permute-start.8 = (bf16[6,48,128]{2,1,0:T(8,128)(2,1)}, bf16[6,48,128]{2,1,0:T(8,128)(2,1)}, u32[]{:S(2)}, u32[]{:S(2)}) collective-permute-start(bf16[6,48,128]{2,1,0:T(8,128)(2,1)} %collective-permute-done.7), channel_id=1, source_target_pairs={{0,2},{1,3},{2,0},{3,1},{4,6},{5,7},{6,4},{7,5},{8,10},{9,11},{10,... | collective-permute-start | bytes 221192 | tf_op jit(solution)/shard_map/ppermute | solution.py:48
  115.3 8.1 %collective-permute-start.9 = (bf16[2,6,48,128]{3,2,1,0:T(8,128)(2,1)S(1)}, bf16[2,6,48,128]{3,2,1,0:T(8,128)(2,1)S(1)}, u32[]{:S(2)}, u32[]{:S(2)}) collective-permute-start(bf16[2,6,48,128]{3,2,1,0:T(8,128)(2,1)S(1)} %bitcast_dynamic-update-slice_fusion.14), channel_id=1, source_target_pairs={{0,8},{1,9},{2,10},{3,11},{4,12},{5,13},{6,14},{7,15},{8,0},{9,1},... | collective-permute-start | bytes 442376 | tf_op jit(solution)/shard_map/ppermute | solution.py:48
  115.5 7.9 %collective-permute-start.10 = (bf16[2,6,48,128]{3,2,1,0:T(8,128)(2,1)S(1)}, bf16[2,6,48,128]{3,2,1,0:T(8,128)(2,1)S(1)}, u32[]{:S(2)}, u32[]{:S(2)}) collective-permute-start(bf16[2,6,48,128]{3,2,1,0:T(8,128)(2,1)S(1)} %bitcast_dynamic-update-slice_fusion.14), channel_id=1, source_target_pairs={{0,4},{1,5},{2,6},{3,7},{4,0},{5,1},{6,2},{7,3},{8,12},{9,13},{10,... | collective-permute-start | bytes 442376 | tf_op jit(solution)/shard_map/ppermute | solution.py:48
  117.6 6.8 %collective-permute-start.11 = (bf16[2,6,48,128]{3,2,1,0:T(8,128)(2,1)S(1)}, bf16[2,6,48,128]{3,2,1,0:T(8,128)(2,1)S(1)}, u32[]{:S(2)}, u32[]{:S(2)}) collective-permute-start(bf16[2,6,48,128]{3,2,1,0:T(8,128)(2,1)S(1)} %bitcast_dynamic-update-slice_fusion.14), channel_id=1, source_target_pairs={{0,12},{1,13},{2,14},{3,15},{4,8},{5,9},{6,10},{7,11},{8,4},{9,5},... | collective-permute-start | bytes 442376 | tf_op jit(solution)/shard_map/ppermute | solution.py:48
  123.2 1.3 copy-start.3
  124.4 4.9 %collective-permute-start.12 = (bf16[4,2,6,48,128]{4,3,2,1,0:T(8,128)(2,1)S(1)}, bf16[4,2,6,48,128]{4,3,2,1,0:T(8,128)(2,1)S(1)}, u32[]{:S(2)}, u32[]{:S(2)}) collective-permute-start(bf16[4,2,6,48,128]{4,3,2,1,0:T(8,128)(2,1)S(1)} %bitcast_dynamic-update-slice_fusion.10), channel_id=1, source_target_pairs={{0,1},{1,0},{2,3},{3,2},{4,5},{5,4},{6,7},{7,6},{8,9},{9,8},{10,11... | collective-permute-start | bytes 1769480 | tf_op jit(solution)/shard_map/ppermute | solution.py:48
  124.6 1.6 %copy-start.16 = (f32[128]{0:T(128)S(1)}, f32[128]{0:T(128)}, u32[]{:S(2)}) copy-start(f32[128]{0:T(128)} %get-tuple-element.79) | copy-start | bytes 1540
  124.6 1.6 %copy-start.18 = (f32[128]{0:T(128)S(1)}, f32[128]{0:T(128)}, u32[]{:S(2)}) copy-start(f32[128]{0:T(128)} %get-tuple-element.96) | copy-start | bytes 1540
  125.4 1.6 %copy-start.35 = (bf16[2,128,128]{2,1,0:T(8,128)(2,1)S(1)}, bf16[2,128,128]{2,1,0:T(8,128)(2,1)}, u32[]{:S(2)}) copy-start(bf16[2,128,128]{2,1,0:T(8,128)(2,1)} %param.21) | copy-start | bytes 196612
  129.5 1.0 copy-start.2
  142.6 1.7 %copy-start.1 = (f32[2,48,48,128]{3,2,1,0:T(8,128)S(1)}, f32[2,48,48,128]{3,2,1,0:T(8,128)}, u32[]{:S(2)}) copy-start(f32[2,48,48,128]{3,2,1,0:T(8,128)} %pad_maximum_fusion) | copy-start | bytes 7077892
  (4 other events, 2.6 us)

commit v2 on v1

--- a/solution.py
+++ b/solution.py
@@ -123,22 +123,24 @@
     window_keep = jnp.concatenate([keep_of(windows[0, slot]) for slot in range(2)])
     rows_keep = jnp.concatenate([part_of(keep_of(windows[1, slot]), row) for slot in range(2)])
     band_keep = (part_of(keep_of(row), col)[:, None] * window_keep[None, :]).reshape(-1)
+    moved_keep = (part_of(keep_of(col), row)[:, None] * window_keep[None, :]).reshape(-1)
     rows_keep = (rows_keep[:, None] * keep_of(col)[None, :]).reshape(-1)
     half, core = (col >> 1) & 1, col & 1
     places = (half, half ^ 1, [(col >> 2) ^ d for d in range(4)], core, core ^ 1)
 
     pieces = lax.all_to_all(pair_rep.reshape(n, part, tile, width), "col", 0, 0, tiled=True)
-    pieces, places, band_keep, rows_keep = lax.optimization_barrier(
-        (pieces, places, band_keep, rows_keep)
+    pieces, places, band_keep, moved_keep, rows_keep = lax.optimization_barrier(
+        (pieces, places, band_keep, moved_keep, rows_keep)
     )
     band = jnp.concatenate(pick(pieces, 0), axis=1)
-    gated = gate_project(norm_in(band, 0), band_keep, w_proj[0], w_gate[0])
-    left_own, right_own = gated[..., :hidden], gated[..., hidden:]
-    right_moved = transpose_devices(right_own)
-    left_moved = transpose_devices(left_own)
-    source, _ = lax.optimization_barrier((pair_rep, right_own))
+    band = norm_in(band, 0)
+    moved = transpose_devices(band)
+    source, band = lax.optimization_barrier((pair_rep, band))
     gate = gate_of(norm_in(source, 0), 0)
-    right_moved, gate = lax.optimization_barrier((right_moved, gate))
+    left_own = gate_project(band, band_keep, w_proj[0][:, :hidden], w_gate[0][:, :hidden])
+    moved, gate, left_own = lax.optimization_barrier((moved, gate, left_own))
+    gated = gate_project(moved, moved_keep, w_proj[0], w_gate[0])
+    left_moved, right_moved = gated[..., :hidden], gated[..., hidden:]
 
     rows = pair_rep.reshape(n, part, tile, width)
     chunks = jnp.concatenate([jnp.broadcast_to(right_moved, (n,) + right_moved.shape), rows], axis=2)

time: 148 us -> 145 us (0.980)
  waiting for transfers between devices: 36.6 us -> 33.3 us
    ppermute x3 -> x2, waiting for transfers between devices: 4.78 us -> 1.41 us  [transpose_devices(): return lax.ppermute(x, ('row', 'col'), pairs)]
    ppermute x10, waiting for transfers between devices: 16.7 us -> 19.1 us  [swap(): return lax.ppermute(x, axis, [(p, p ^ bits) for p in range(n)])]
    ppermute x3 -> x2, starting transfers between devices: 19.4 us -> 18.2 us  [transpose_devices(): return lax.ppermute(x, ('row', 'col'), pairs)]
  transfers between devices with their start and end apart: 16 -> 15, of which waited for: 12 -> 8; matrix products, arithmetic and copies ran while one was open for 20% -> 20% of each run, Pallas kernels for 0% -> 0%
where the time goes in v2:
time: 145 us; the launch traced here: 144 us
  starting transfers between devices  52.2 us (36%)
  waiting for transfers between devices  33.3 us (23%)
  local copies, waits for them, and re-layouts  24.1 us (17%)
  matrix products  12.4 us (9%)
  between operations  11.4 us (8%)
  other arithmetic  10.7 us (7%)
    ppermute x10, waiting for transfers between devices, swap(): return lax.ppermute(x, axis, [(p, p ^ bits) for p in range(n)])  19.1 us
    ppermute x2, starting transfers between devices, transpose_devices(): return lax.ppermute(x, ('row', 'col'), pairs)  18.2 us
    ppermute x10, starting transfers between devices, swap(): return lax.ppermute(x, axis, [(p, p ^ bits) for p in range(n)])  16 us
    all_to_all x1, starting transfers between devices, body(): lax.all_to_all(pair_rep.reshape(n, part, tile, width), 'col', 0, 0, tiled...  7.6 us
    all_to_all x1, waiting for transfers between devices, body(): chunks = lax.all_to_all(chunks, 'row', 0, 0, tiled=True)  7.43 us
    all_to_all x1, starting transfers between devices, body(): chunks = lax.all_to_all(chunks, 'row', 0, 0, tiled=True)  6.12 us
    all_to_all x1, starting transfers between devices, body(): lax.all_to_all(copies, 'row', 0, 0, tiled=True)  4.2 us
    all_to_all x1, waiting for transfers between devices, body(): lax.all_to_all(copies, 'row', 0, 0, tiled=True)  3.85 us
  transfers between devices with their start and end apart: 15, of which 8 were waited for; matrix products, arithmetic and copies ran while one was open for 20% of the time, Pallas kernels for 0%

profile of v2, /device:TPU:4, one launch (start us, length us, event | category | flops | bytes accessed | tf_op | source)
XLA Modules:
  0.0 144.0 jit_solution(6020906232228833073)
XLA Ops:
  0.1 7.6 %all-to-all-start = ((bf16[16,3,48,128]{3,2,1,0:T(8,128)(2,1)}), bf16[16,3,48,128]{3,2,1,0:T(8,128)(2,1)S(1)}, u32[]{:S(2)}, u32[]{:S(2)}) async-start(bf16[16,3,48,128]{3,2,1,0:T(8,128)(2,1)} %bitcast.178), calls=%async_computation | async-start | bytes 1179648 | tf_op jit(solution)/shard_map/all_to_all | solution.py:131
  7.7 0.7 fusion.99
  14.8 0.7 mul.302
  16.8 1.5 %all-to-all-done = bf16[16,3,48,128]{3,2,1,0:T(8,128)(2,1)S(1)} async-done(((bf16[16,3,48,128]{3,2,1,0:T(8,128)(2,1)}), bf16[16,3,48,128]{3,2,1,0:T(8,128)(2,1)S(1)}, u32[]{:S(2)}, u32[]{:S(2)}) %all-to-all-start) | async-done | bytes 589856 | tf_op jit(solution)/shard_map/all_to_all | solution.py:131
  18.9 11.0 %collective-permute-start = (bf16[3,96,128]{2,1,0:T(8,128)(2,1)S(1)}, bf16[3,96,128]{2,1,0:T(8,128)(2,1)S(1)}, u32[]{:S(2)}, u32[]{:S(2)}) collective-permute-start(bf16[3,96,128]{2,1,0:T(8,128)(2,1)S(1)} %fusion.69), channel_id=1, source_target_pairs={{0,0},{1,16},{2,32},{3,48},{4,64},{5,80},{6,96},{7,112},{8,128},{9... | collective-permute-start | bytes 221192 | tf_op jit(solution)/shard_map/ppermute | solution.py:73
  30.3 0.7 fusion.27
  31.0 0.8 fusion.30
  32.0 1.5 %fusion.5 = f32[2304,128]{1,0:T(8,128)} fusion(bf16[2304,128]{1,0:T(8,128)(2,1)S(1)} %bitcast.190, bf16[2,128,128]{2,1,0:T(8,128)(2,1)S(1)} %copy-done.33), kind=kOutput, calls=%fused_computation.7 | convolution fusion | flops 76382208 | bytes 1802240 | tf_op jit(solution)/shard_map/dot_general | solution.py:26
  34.3 1.4 pad_maximum_fusion.1
  35.7 6.1 %all-to-all-start.1 = ((bf16[16,3,144,128]{3,2,1,0:T(8,128)(2,1)}), bf16[16,3,144,128]{3,2,1,0:T(8,128)(2,1)S(1)}, u32[]{:S(2)}, u32[]{:S(2)}) async-start(bf16[16,3,144,128]{3,2,1,0:T(8,128)(2,1)} %pad_maximum_fusion.1), calls=%async_computation.1 | async-start | bytes 3538944 | tf_op jit(solution)/shard_map/all_to_all | solution.py:148
  41.8 1.0 collective-permute-start.1
  42.9 6.4 %collective-permute-done.1 = bf16[2,3,96,128]{3,2,1,0:T(8,128)(2,1)S(1)} collective-permute-done((bf16[2,3,96,128]{3,2,1,0:T(8,128)(2,1)S(1)}, bf16[2,3,96,128]{3,2,1,0:T(8,128)(2,1)S(1)}, u32[]{:S(2)}, u32[]{:S(2)}) %collective-permute-start.1) | collective-permute-done | bytes 147488 | tf_op jit(solution)/shard_map/ppermute | solution.py:48
  49.3 5.5 %collective-permute-start.2 = (bf16[2,2,3,96,128]{4,3,2,0,1:T(8,128)(2,1)S(1)}, bf16[2,2,3,96,128]{4,3,2,0,1:T(8,128)(2,1)S(1)}, u32[]{:S(2)}, u32[]{:S(2)}) collective-permute-start(bf16[2,2,3,96,128]{4,3,2,0,1:T(8,128)(2,1)S(1)} %bitcast_dynamic-update-slice_fusion.8), channel_id=1, source_target_pairs={{0,8},{1,9},{2,10},{3,11},{4,12},{5,13},{6,14},{7,15},{8,0},{9,1},... | collective-permute-start | bytes 884744 | tf_op jit(solution)/shard_map/ppermute | solution.py:48
  54.8 0.9 collective-permute-start.3
  56.0 6.7 %collective-permute-done.2 = bf16[2,2,3,96,128]{4,3,2,0,1:T(8,128)(2,1)S(1)} collective-permute-done((bf16[2,2,3,96,128]{4,3,2,0,1:T(8,128)(2,1)S(1)}, bf16[2,2,3,96,128]{4,3,2,0,1:T(8,128)(2,1)S(1)}, u32[]{:S(2)}, u32[]{:S(2)}) %collective-permute-start.2) | collective-permute-done | bytes 294944 | tf_op jit(solution)/shard_map/ppermute | solution.py:48
  62.8 5.7 %collective-permute-done.3 = bf16[2,2,3,96,128]{4,3,2,0,1:T(8,128)(2,1)S(1)} collective-permute-done((bf16[2,2,3,96,128]{4,3,2,0,1:T(8,128)(2,1)S(1)}, bf16[2,2,3,96,128]{4,3,2,0,1:T(8,128)(2,1)S(1)}, u32[]{:S(2)}, u32[]{:S(2)}) %collective-permute-start.3) | collective-permute-done | bytes 294944 | tf_op jit(solution)/shard_map/ppermute | solution.py:48
  72.6 0.6 slice_bitcast_fusion.5
  73.9 1.4 bitcast_dynamic-update-slice_fusion.1
  75.3 1.2 fusion.97
  76.5 0.8 copy.38
  77.3 0.8 copy.39
  78.1 7.4 %all-to-all-done.1 = bf16[16,3,144,128]{3,2,1,0:T(8,128)(2,1)S(1)} async-done(((bf16[16,3,144,128]{3,2,1,0:T(8,128)(2,1)}), bf16[16,3,144,128]{3,2,1,0:T(8,128)(2,1)S(1)}, u32[]{:S(2)}, u32[]{:S(2)}) %all-to-all-start.1) | async-done | bytes 1769504 | tf_op jit(solution)/shard_map/all_to_all | solution.py:148
  85.6 0.6 dynamic-slice_bitcast_fusion
  86.3 1.0 copy.40
  87.4 1.9 %fusion.100 = (f32[6,48]{1,0:T(8,128)S(1)}, f32[128,6,48]{2,1,0:T(8,128)S(1)}) fusion(bf16[48,96,128]{1,0,2:T(8,128)(2,1)S(1)} %copy.40, bf16[3,96,128]{1,0,2:T(4,128)(2,1)} %bitcast.193, bf16[3,96,128]{1,0,2:T(4,128)(2,1)S(1)} %bitcast.192), kind=kOutput, calls=%fused_computation.185 | convolution fusion | flops 7409376 | bytes 1475712 | tf_op jit(solution)/shard_map/ikh,jkh->hij/dot_general | solution.py:157
  91.7 7.2 %collective-permute-start.6 = (bf16[6,48,128]{2,1,0:T(8,128)(2,1)S(1)}, bf16[6,48,128]{2,1,0:T(8,128)(2,1)}, u32[]{:S(2)}, u32[]{:S(2)}) collective-permute-start(bf16[6,48,128]{2,1,0:T(8,128)(2,1)S(1)} %get-tuple-element.70), channel_id=1, source_target_pairs={{0,0},{1,16},{2,32},{3,48},{4,64},{5,80},{6,96},{7,112},{8,128},{9... | collective-permute-start | bytes 221192 | tf_op jit(solution)/shard_map/ppermute | solution.py:73
  99.0 1.2 broadcast_in_dim.23
  100.2 4.2 %all-to-all-start.2 = ((bf16[16,6,48,128]{3,2,1,0:T(8,128)(2,1)}), bf16[16,6,48,128]{3,2,1,0:T(8,128)(2,1)S(1)}, u32[]{:S(2)}, u32[]{:S(2)}) async-start(bf16[16,6,48,128]{3,2,1,0:T(8,128)(2,1)} %broadcast_in_dim.23), calls=%async_computation.2 | async-start | bytes 2359296 | tf_op jit(solution)/shard_map/all_to_all | solution.py:163
  104.4 1.4 collective-permute-done.6
  105.8 4.1 %collective-permute-start.7 = (bf16[6,48,128]{2,1,0:T(8,128)(2,1)}, bf16[6,48,128]{2,1,0:T(8,128)(2,1)}, u32[]{:S(2)}, u32[]{:S(2)}) collective-permute-start(bf16[6,48,128]{2,1,0:T(8,128)(2,1)} %collective-permute-done.6), channel_id=1, source_target_pairs={{0,2},{1,3},{2,0},{3,1},{4,6},{5,7},{6,4},{7,5},{8,10},{9,11},{10,... | collective-permute-start | bytes 221192 | tf_op jit(solution)/shard_map/ppermute | solution.py:48
  109.9 0.9 bitcast_dynamic-update-slice_fusion.15
  110.8 2.8 %copy.42 = bf16[48,96,128]{1,0,2:T(8,128)(2,1)} copy(bf16[48,96,128]{2,1,0:T(8,128)(2,1)} %bitcast.185) | data formatting | bytes 2359296 | tf_op jit(solution)/shard_map/optimization_barrier | solution.py:169
  113.6 0.9 bitcast_dynamic-update-slice_fusion.14
  114.8 2.1 %collective-permute-start.9 = (bf16[2,6,48,128]{3,2,1,0:T(8,128)(2,1)S(1)}, bf16[2,6,48,128]{3,2,1,0:T(8,128)(2,1)S(1)}, u32[]{:S(2)}, u32[]{:S(2)}) collective-permute-start(bf16[2,6,48,128]{3,2,1,0:T(8,128)(2,1)S(1)} %bitcast_dynamic-update-slice_fusion.14), channel_id=1, source_target_pairs={{0,4},{1,5},{2,6},{3,7},{4,0},{5,1},{6,2},{7,3},{8,12},{9,13},{10,... | collective-permute-start | bytes 442376 | tf_op jit(solution)/shard_map/ppermute | solution.py:48
  116.8 2.0 %collective-permute-start.10 = (bf16[2,6,48,128]{3,2,1,0:T(8,128)(2,1)S(1)}, bf16[2,6,48,128]{3,2,1,0:T(8,128)(2,1)S(1)}, u32[]{:S(2)}, u32[]{:S(2)}) collective-permute-start(bf16[2,6,48,128]{3,2,1,0:T(8,128)(2,1)S(1)} %bitcast_dynamic-update-slice_fusion.14), channel_id=1, source_target_pairs={{0,12},{1,13},{2,14},{3,15},{4,8},{5,9},{6,10},{7,11},{8,4},{9,5},... | collective-permute-start | bytes 442376 | tf_op jit(solution)/shard_map/ppermute | solution.py:48
  118.8 2.3 %fusion.102 = (f32[48,48]{1,0:T(8,128)S(1)}, f32[128,48,48]{2,1,0:T(8,128)S(1)}) fusion(bf16[128,48,96]{2,1,0:T(8,128)(2,1)} %bitcast.181, bf16[48,96,128]{1,0,2:T(8,128)(2,1)S(1)} %copy.40), kind=kOutput, calls=%fused_computation.187 | convolution fusion | flops 56915712 | bytes 3548160 | tf_op jit(solution)/shard_map/hik,jkh->hij/dot_general | solution.py:166
  123.1 0.6 copy-done.3
  123.7 0.8 convert_reduce_fusion
  124.6 0.7 fusion.23
  125.3 0.8 fusion.26
  126.7 1.6 %pad_maximum_fusion = f32[2,48,48,128]{3,2,1,0:T(8,128)} fusion(f32[1,48,48,128]{3,2,1,0:T(8,128)S(1)} %convert_bitcast_fusion, f32[1,48,48,128]{3,2,1,0:T(8,128)S(1)} %bitcast.187), kind=kLoop, calls=%fused_computation.12 | loop fusion | flops 589824 | bytes 4718592 | tf_op jit(solution)/shard_map/stack | solution.py:175
  128.7 1.0 copy-done.2
  129.7 2.4 %copy.47 = bf16[96,48,128]{0,1,2:T(8,128)(2,1)S(1)} copy(bf16[96,48,128]{2,1,0:T(8,128)(2,1)} %bitcast.183) | data formatting | bytes 2359296 | tf_op jit(solution)/shard_map/reshape;reshape | solution.py:172
  132.1 3.8 %all-to-all-done.2 = bf16[16,6,48,128]{3,2,1,0:T(8,128)(2,1)S(1)} async-done(((bf16[16,6,48,128]{3,2,1,0:T(8,128)(2,1)}), bf16[16,6,48,128]{3,2,1,0:T(8,128)(2,1)S(1)}, u32[]{:S(2)}, u32[]{:S(2)}) %all-to-all-start.2) | async-done | bytes 1179680 | tf_op jit(solution)/shard_map/all_to_all | solution.py:163
  135.9 2.0 %copy.48 = bf16[96,48,128]{0,1,2:T(8,128)(2,1)} copy(bf16[96,48,128]{2,1,0:T(8,128)(2,1)S(1)} %bitcast.182) | data formatting | bytes 2359296 | tf_op jit(solution)/shard_map/reshape | solution.py:163
  137.9 2.3 %fusion.103 = (f32[48,48]{1,0:T(8,128)S(1)}, f32[128,48,48]{2,1,0:T(8,128)S(1)}) fusion(bf16[96,48,128]{0,1,2:T(8,128)(2,1)S(1)} %copy.47, bf16[96,48,128]{0,1,2:T(8,128)(2,1)} %copy.48), kind=kOutput, calls=%fused_computation.188 | convolution fusion | flops 56915712 | bytes 3548160 | tf_op jit(solution)/shard_map/kih,kjh->hij/dot_general | solution.py:177
  141.5 1.1 copy-done.1
  142.6 1.4 fusion.20
  (162 shorter events, 11.0 us)
Async XLA Ops:
  0.0 29.9 %copy-start = (bf16[48,48,128]{2,1,0:T(8,128)(2,1)S(1)}, bf16[48,48,128]{2,1,0:T(8,128)(2,1)}, u32[]{:S(2)}) copy-start(bf16[48,48,128]{2,1,0:T(8,128)(2,1)} %param.11) | copy-start | bytes 1769476
  0.0 7.6 %copy-start.26 = (s32[2,2]{1,0:T(2,128)S(1)}, s32[2,2]{1,0:T(2,128)}, u32[]{:S(2)}) copy-start(s32[2,2]{1,0:T(2,128)} %param.13) | copy-start | bytes 52
  0.0 9.6 %copy-start.25 = (s32[768]{0:T(1024)S(1)}, s32[768]{0:T(1024)}, u32[]{:S(2)}) copy-start(s32[768]{0:T(1024)} %param.12) | copy-start | bytes 9220
  0.0 11.4 %copy-start.30 = (f32[2,128]{1,0:T(2,128)S(1)}, f32[2,128]{1,0:T(2,128)}, u32[]{:S(2)}) copy-start(f32[2,128]{1,0:T(2,128)} %param.14) | copy-start | bytes 3076
  0.0 11.4 %copy-start.29 = (f32[2,128]{1,0:T(2,128)S(1)}, f32[2,128]{1,0:T(2,128)}, u32[]{:S(2)}) copy-start(f32[2,128]{1,0:T(2,128)} %param.15) | copy-start | bytes 3076
  0.0 16.7 %copy-start.7 = (bf16[2,128,256]{2,1,0:T(8,128)(2,1)S(1)}, bf16[2,128,256]{2,1,0:T(8,128)(2,1)}, u32[]{:S(2)}) copy-start(bf16[2,128,256]{2,1,0:T(8,128)(2,1)} %param.16) | copy-start | bytes 393220
  0.0 16.8 %copy-start.10 = (bf16[2,128,256]{2,1,0:T(8,128)(2,1)S(1)}, bf16[2,128,256]{2,1,0:T(8,128)(2,1)}, u32[]{:S(2)}) copy-start(bf16[2,128,256]{2,1,0:T(8,128)(2,1)} %param.17) | copy-start | bytes 393220
  0.1 18.3 %all-to-all-start = ((bf16[16,3,48,128]{3,2,1,0:T(8,128)(2,1)}), bf16[16,3,48,128]{3,2,1,0:T(8,128)(2,1)S(1)}, u32[]{:S(2)}, u32[]{:S(2)}) async-start(bf16[16,3,48,128]{3,2,1,0:T(8,128)(2,1)} %bitcast.178), calls=%async_computation | async-start | bytes 1179648 | tf_op jit(solution)/shard_map/all_to_all | solution.py:131
  12.0 19.8 %copy-start.12 = (f32[128]{0:T(128)}, f32[128]{0:T(128)S(1)}, u32[]{:S(2)}) copy-start(f32[128]{0:T(128)S(1)} %get-tuple-element.87) | copy-start | bytes 1540
  12.0 19.8 %copy-start.14 = (f32[128]{0:T(128)}, f32[128]{0:T(128)S(1)}, u32[]{:S(2)}) copy-start(f32[128]{0:T(128)S(1)} %get-tuple-element.104) | copy-start | bytes 1540
  18.9 14.8 %collective-permute-start = (bf16[3,96,128]{2,1,0:T(8,128)(2,1)S(1)}, bf16[3,96,128]{2,1,0:T(8,128)(2,1)S(1)}, u32[]{:S(2)}, u32[]{:S(2)}) collective-permute-start(bf16[3,96,128]{2,1,0:T(8,128)(2,1)S(1)} %fusion.69), channel_id=1, source_target_pairs={{0,0},{1,16},{2,32},{3,48},{4,64},{5,80},{6,96},{7,112},{8,128},{9... | collective-permute-start | bytes 221192 | tf_op jit(solution)/shard_map/ppermute | solution.py:73
  30.3 1.7 %copy-start.33 = (bf16[2,128,128]{2,1,0:T(8,128)(2,1)S(1)}, bf16[2,128,128]{2,1,0:T(8,128)(2,1)}, u32[]{:S(2)}) copy-start(bf16[2,128,128]{2,1,0:T(8,128)(2,1)} %param.21) | copy-start | bytes 196612
  35.7 49.8 %all-to-all-start.1 = ((bf16[16,3,144,128]{3,2,1,0:T(8,128)(2,1)}), bf16[16,3,144,128]{3,2,1,0:T(8,128)(2,1)S(1)}, u32[]{:S(2)}, u32[]{:S(2)}) async-start(bf16[16,3,144,128]{3,2,1,0:T(8,128)(2,1)} %pad_maximum_fusion.1), calls=%async_computation.1 | async-start | bytes 3538944 | tf_op jit(solution)/shard_map/all_to_all | solution.py:148
  41.8 7.5 %collective-permute-start.1 = (bf16[2,3,96,128]{3,2,1,0:T(8,128)(2,1)S(1)}, bf16[2,3,96,128]{3,2,1,0:T(8,128)(2,1)S(1)}, u32[]{:S(2)}, u32[]{:S(2)}) collective-permute-start(bf16[2,3,96,128]{3,2,1,0:T(8,128)(2,1)S(1)} %pad_maximum_fusion.2), channel_id=1, source_target_pairs={{0,2},{1,3},{2,0},{3,1},{4,6},{5,7},{6,4},{7,5},{8,10},{9,11},{10,... | collective-permute-start | bytes 442376 | tf_op jit(solution)/shard_map/ppermute | solution.py:48
  49.3 13.4 %collective-permute-start.2 = (bf16[2,2,3,96,128]{4,3,2,0,1:T(8,128)(2,1)S(1)}, bf16[2,2,3,96,128]{4,3,2,0,1:T(8,128)(2,1)S(1)}, u32[]{:S(2)}, u32[]{:S(2)}) collective-permute-start(bf16[2,2,3,96,128]{4,3,2,0,1:T(8,128)(2,1)S(1)} %bitcast_dynamic-update-slice_fusion.8), channel_id=1, source_target_pairs={{0,8},{1,9},{2,10},{3,11},{4,12},{5,13},{6,14},{7,15},{8,0},{9,1},... | collective-permute-start | bytes 884744 | tf_op jit(solution)/shard_map/ppermute | solution.py:48
  54.8 13.7 %collective-permute-start.3 = (bf16[2,2,3,96,128]{4,3,2,0,1:T(8,128)(2,1)S(1)}, bf16[2,2,3,96,128]{4,3,2,0,1:T(8,128)(2,1)S(1)}, u32[]{:S(2)}, u32[]{:S(2)}) collective-permute-start(bf16[2,2,3,96,128]{4,3,2,0,1:T(8,128)(2,1)S(1)} %bitcast_dynamic-update-slice_fusion.8), channel_id=1, source_target_pairs={{0,4},{1,5},{2,6},{3,7},{4,0},{5,1},{6,2},{7,3},{8,12},{9,13},{10,... | collective-permute-start | bytes 884744 | tf_op jit(solution)/shard_map/ppermute | solution.py:48
  55.7 12.8 %collective-permute-start.4 = (bf16[2,2,3,96,128]{4,3,2,0,1:T(8,128)(2,1)S(1)}, bf16[2,2,3,96,128]{4,3,2,0,1:T(8,128)(2,1)S(1)}, u32[]{:S(2)}, u32[]{:S(2)}) collective-permute-start(bf16[2,2,3,96,128]{4,3,2,0,1:T(8,128)(2,1)S(1)} %bitcast_dynamic-update-slice_fusion.8), channel_id=1, source_target_pairs={{0,12},{1,13},{2,14},{3,15},{4,8},{5,9},{6,10},{7,11},{8,4},{9,5},... | collective-permute-start | bytes 884744 | tf_op jit(solution)/shard_map/ppermute | solution.py:48
  55.9 16.6 %copy-start.31 = (f32[2,128]{1,0:T(2,128)S(1)}, f32[2,128]{1,0:T(2,128)}, u32[]{:S(2)}) copy-start(f32[2,128]{1,0:T(2,128)} %param.19) | copy-start | bytes 3076
  55.9 16.6 %copy-start.32 = (f32[2,128]{1,0:T(2,128)S(1)}, f32[2,128]{1,0:T(2,128)}, u32[]{:S(2)}) copy-start(f32[2,128]{1,0:T(2,128)} %param.18) | copy-start | bytes 3076
  68.6 5.2 %collective-permute-start.5 = (bf16[4,2,2,3,96,128]{5,4,3,1,0,2:T(8,128)(2,1)S(1)}, bf16[4,2,2,3,96,128]{5,4,3,1,0,2:T(8,128)(2,1)}, u32[]{:S(2)}, u32[]{:S(2)}) collective-permute-start(bf16[4,2,2,3,96,128]{5,4,3,1,0,2:T(8,128)(2,1)S(1)} %bitcast_dynamic-update-slice_fusion.7), channel_id=1, source_target_pairs={{0,1},{1,0},{2,3},{3,2},{4,5},{5,4},{6,7},{7,6},{8,9},{9,8},{10,11... | collective-permute-start | bytes 3538952 | tf_op jit(solution)/shard_map/ppermute | solution.py:48
  86.3 1.0 copy-start.6
  87.3 2.1 %copy-start.4 = (bf16[3,48,128]{2,1,0:T(8,128)(2,1)S(1)}, bf16[3,48,128]{2,1,0:T(8,128)(2,1)}, u32[]{:S(2)}) copy-start(bf16[3,48,128]{2,1,0:T(8,128)(2,1)} %get-tuple-element.42) | copy-start | bytes 110596
  87.3 2.1 %copy-start.5 = (bf16[3,48,128]{2,1,0:T(8,128)(2,1)S(1)}, bf16[3,48,128]{2,1,0:T(8,128)(2,1)}, u32[]{:S(2)}) copy-start(bf16[3,48,128]{2,1,0:T(8,128)(2,1)} %get-tuple-element.41) | copy-start | bytes 110596
  87.3 2.4 %copy-start.13 = (f32[128]{0:T(128)S(1)}, f32[128]{0:T(128)}, u32[]{:S(2)}) copy-start(f32[128]{0:T(128)} %copy-done.12) | copy-start | bytes 1540
  87.3 2.4 %copy-start.15 = (f32[128]{0:T(128)S(1)}, f32[128]{0:T(128)}, u32[]{:S(2)}) copy-start(f32[128]{0:T(128)} %copy-done.14) | copy-start | bytes 1540
  87.4 2.6 %copy-start.34 = (bf16[2,128,128]{2,1,0:T(8,128)(2,1)S(1)}, bf16[2,128,128]{2,1,0:T(8,128)(2,1)}, u32[]{:S(2)}) copy-start(bf16[2,128,128]{2,1,0:T(8,128)(2,1)} %param.21) | copy-start | bytes 196612
  89.2 0.9 copy-start.21
  89.2 0.9 copy-start.23
  89.3 1.3 copy-start.9
  89.8 1.3 copy-start.17
  89.8 1.3 copy-start.19
  90.0 1.3 copy-start.11
  90.5 1.0 copy-start.8
  90.5 1.0 copy-start.16
  91.7 14.0 %collective-permute-start.6 = (bf16[6,48,128]{2,1,0:T(8,128)(2,1)S(1)}, bf16[6,48,128]{2,1,0:T(8,128)(2,1)}, u32[]{:S(2)}, u32[]{:S(2)}) collective-permute-start(bf16[6,48,128]{2,1,0:T(8,128)(2,1)S(1)} %get-tuple-element.70), channel_id=1, source_target_pairs={{0,0},{1,16},{2,32},{3,48},{4,64},{5,80},{6,96},{7,112},{8,128},{9... | collective-permute-start | bytes 221192 | tf_op jit(solution)/shard_map/ppermute | solution.py:73
  100.2 35.8 %all-to-all-start.2 = ((bf16[16,6,48,128]{3,2,1,0:T(8,128)(2,1)}), bf16[16,6,48,128]{3,2,1,0:T(8,128)(2,1)S(1)}, u32[]{:S(2)}, u32[]{:S(2)}) async-start(bf16[16,6,48,128]{3,2,1,0:T(8,128)(2,1)} %broadcast_in_dim.23), calls=%async_computation.2 | async-start | bytes 2359296 | tf_op jit(solution)/shard_map/all_to_all | solution.py:163
  105.8 7.8 %collective-permute-start.7 = (bf16[6,48,128]{2,1,0:T(8,128)(2,1)}, bf16[6,48,128]{2,1,0:T(8,128)(2,1)}, u32[]{:S(2)}, u32[]{:S(2)}) collective-permute-start(bf16[6,48,128]{2,1,0:T(8,128)(2,1)} %collective-permute-done.6), channel_id=1, source_target_pairs={{0,2},{1,3},{2,0},{3,1},{4,6},{5,7},{6,4},{7,5},{8,10},{9,11},{10,... | collective-permute-start | bytes 221192 | tf_op jit(solution)/shard_map/ppermute | solution.py:48
  114.5 8.1 %collective-permute-start.8 = (bf16[2,6,48,128]{3,2,1,0:T(8,128)(2,1)S(1)}, bf16[2,6,48,128]{3,2,1,0:T(8,128)(2,1)S(1)}, u32[]{:S(2)}, u32[]{:S(2)}) collective-permute-start(bf16[2,6,48,128]{3,2,1,0:T(8,128)(2,1)S(1)} %bitcast_dynamic-update-slice_fusion.14), channel_id=1, source_target_pairs={{0,8},{1,9},{2,10},{3,11},{4,12},{5,13},{6,14},{7,15},{8,0},{9,1},... | collective-permute-start | bytes 442376 | tf_op jit(solution)/shard_map/ppermute | solution.py:48
  114.8 7.9 %collective-permute-start.9 = (bf16[2,6,48,128]{3,2,1,0:T(8,128)(2,1)S(1)}, bf16[2,6,48,128]{3,2,1,0:T(8,128)(2,1)S(1)}, u32[]{:S(2)}, u32[]{:S(2)}) collective-permute-start(bf16[2,6,48,128]{3,2,1,0:T(8,128)(2,1)S(1)} %bitcast_dynamic-update-slice_fusion.14), channel_id=1, source_target_pairs={{0,4},{1,5},{2,6},{3,7},{4,0},{5,1},{6,2},{7,3},{8,12},{9,13},{10,... | collective-permute-start | bytes 442376 | tf_op jit(solution)/shard_map/ppermute | solution.py:48
  116.8 6.1 %collective-permute-start.10 = (bf16[2,6,48,128]{3,2,1,0:T(8,128)(2,1)S(1)}, bf16[2,6,48,128]{3,2,1,0:T(8,128)(2,1)S(1)}, u32[]{:S(2)}, u32[]{:S(2)}) collective-permute-start(bf16[2,6,48,128]{3,2,1,0:T(8,128)(2,1)S(1)} %bitcast_dynamic-update-slice_fusion.14), channel_id=1, source_target_pairs={{0,12},{1,13},{2,14},{3,15},{4,8},{5,9},{6,10},{7,11},{8,4},{9,5},... | collective-permute-start | bytes 442376 | tf_op jit(solution)/shard_map/ppermute | solution.py:48
  121.2 0.7 copy-start.22
  122.5 1.3 copy-start.3
  123.0 5.6 %collective-permute-start.11 = (bf16[4,2,6,48,128]{4,3,2,1,0:T(8,128)(2,1)S(1)}, bf16[4,2,6,48,128]{4,3,2,1,0:T(8,128)(2,1)S(1)}, u32[]{:S(2)}, u32[]{:S(2)}) collective-permute-start(bf16[4,2,6,48,128]{4,3,2,1,0:T(8,128)(2,1)S(1)} %bitcast_dynamic-update-slice_fusion.10), channel_id=1, source_target_pairs={{0,1},{1,0},{2,3},{3,2},{4,5},{5,4},{6,7},{7,6},{8,9},{9,8},{10,11... | collective-permute-start | bytes 1769480 | tf_op jit(solution)/shard_map/ppermute | solution.py:48
  123.7 1.6 %copy-start.18 = (f32[128]{0:T(128)S(1)}, f32[128]{0:T(128)}, u32[]{:S(2)}) copy-start(f32[128]{0:T(128)} %get-tuple-element.86) | copy-start | bytes 1540
  123.7 1.6 %copy-start.20 = (f32[128]{0:T(128)S(1)}, f32[128]{0:T(128)}, u32[]{:S(2)}) copy-start(f32[128]{0:T(128)} %get-tuple-element.105) | copy-start | bytes 1540
  124.6 1.6 %copy-start.35 = (bf16[2,128,128]{2,1,0:T(8,128)(2,1)S(1)}, bf16[2,128,128]{2,1,0:T(8,128)(2,1)}, u32[]{:S(2)}) copy-start(bf16[2,128,128]{2,1,0:T(8,128)(2,1)} %param.21) | copy-start | bytes 196612
  128.6 1.0 copy-start.2
  140.9 1.7 %copy-start.1 = (f32[2,48,48,128]{3,2,1,0:T(8,128)S(1)}, f32[2,48,48,128]{3,2,1,0:T(8,128)}, u32[]{:S(2)}) copy-start(f32[2,48,48,128]{3,2,1,0:T(8,128)} %pad_maximum_fusion) | copy-start | bytes 7077892
  (3 other events, 1.9 us)

commit v3 on v2

--- a/solution.py
+++ b/solution.py
@@ -138,12 +138,14 @@
     source, band = lax.optimization_barrier((pair_rep, band))
     gate = gate_of(norm_in(source, 0), 0)
     left_own = gate_project(band, band_keep, w_proj[0][:, :hidden], w_gate[0][:, :hidden])
-    moved, gate, left_own = lax.optimization_barrier((moved, gate, left_own))
+    rows = pair_rep.reshape(n, part, tile, width)
+    chunks = jnp.pad(rows, ((0, 0), (0, 0), (2 * tile, 0), (0, 0)))
+    moved, gate, left_own, chunks = lax.optimization_barrier((moved, gate, left_own, chunks))
     gated = gate_project(moved, moved_keep, w_proj[0], w_gate[0])
     left_moved, right_moved = gated[..., :hidden], gated[..., hidden:]
 
-    rows = pair_rep.reshape(n, part, tile, width)
-    chunks = jnp.concatenate([jnp.broadcast_to(right_moved, (n,) + right_moved.shape), rows], axis=2)
+    spread = jnp.broadcast_to(right_moved, (n,) + right_moved.shape)
+    chunks = lax.dynamic_update_slice(chunks, spread, (0, 0, 0, 0))
     chunks, left_own = lax.optimization_barrier((chunks, left_own))
     chunks = lax.all_to_all(chunks, "row", 0, 0, tiled=True)
     rows = pick(chunks[:, :, 2 * tile :], 1)

time: 145 us -> 146 us (level)
  waiting for transfers between devices: 33.3 us -> 28.7 us
  starting transfers between devices: 52.2 us -> 56.4 us
  local copies, waits for them, and re-layouts: 24.1 us -> 25.9 us
    all_to_all x1, waiting for transfers between devices: 7.43 us -> 4.63 us  [body(): chunks = lax.all_to_all(chunks, 'row', 0, 0, tiled=True)]
    ppermute x10, starting transfers between devices: 16 us -> 18.6 us  [swap(): return lax.ppermute(x, axis, [(p, p ^ bits) for p in range(n)])]
    ppermute x2, starting transfers between devices: 18.2 us -> 20.6 us  [transpose_devices(): return lax.ppermute(x, ('row', 'col'), pairs)]
    all_to_all x1, starting transfers between devices: 6.12 us -> 4.38 us  [body(): chunks = lax.all_to_all(chunks, 'row', 0, 0, tiled=True)]
  transfers between devices with their start and end apart: 15 -> 15, of which waited for: 8 -> 8; matrix products, arithmetic and copies ran while one was open for 20% -> 21% of each run, Pallas kernels for 0% -> 0%
where the time goes in v3:
time: 146 us; the launch traced here: 144 us
  starting transfers between devices  56.4 us (39%)
  waiting for transfers between devices  28.7 us (20%)
  local copies, waits for them, and re-layouts  25.9 us (18%)
  matrix products  12.4 us (8%)
  between operations  11.4 us (8%)
  other arithmetic  9.3 us (6%)
    ppermute x2, starting transfers between devices, transpose_devices(): return lax.ppermute(x, ('row', 'col'), pairs)  20.6 us
    ppermute x10, waiting for transfers between devices, swap(): return lax.ppermute(x, axis, [(p, p ^ bits) for p in range(n)])  18.8 us
    ppermute x10, starting transfers between devices, swap(): return lax.ppermute(x, axis, [(p, p ^ bits) for p in range(n)])  18.6 us
    all_to_all x1, starting transfers between devices, body(): lax.all_to_all(pair_rep.reshape(n, part, tile, width), 'col', 0, 0, tiled...  7.6 us
    all_to_all x1, starting transfers between devices, body(): lax.all_to_all(copies, 'row', 0, 0, tiled=True)  5.22 us
    all_to_all x1, waiting for transfers between devices, body(): lax.all_to_all(copies, 'row', 0, 0, tiled=True)  5.12 us
    all_to_all x1, waiting for transfers between devices, body(): chunks = lax.all_to_all(chunks, 'row', 0, 0, tiled=True)  4.63 us
    all_to_all x1, starting transfers between devices, body(): chunks = lax.all_to_all(chunks, 'row', 0, 0, tiled=True)  4.38 us
  transfers between devices with their start and end apart: 15, of which 8 were waited for; matrix products, arithmetic and copies ran while one was open for 21% of the time, Pallas kernels for 0%

profile of v3, /device:TPU:4, one launch (start us, length us, event | category | flops | bytes accessed | tf_op | source)
XLA Modules:
  0.0 144.0 jit_solution(6557959816369416219)
XLA Ops:
  0.0 7.6 %all-to-all-start = ((bf16[16,3,48,128]{3,2,1,0:T(8,128)(2,1)}), bf16[16,3,48,128]{3,2,1,0:T(8,128)(2,1)S(1)}, u32[]{:S(2)}, u32[]{:S(2)}) async-start(bf16[16,3,48,128]{3,2,1,0:T(8,128)(2,1)} %bitcast.178), calls=%async_computation | async-start | bytes 1179648 | tf_op jit(solution)/shard_map/all_to_all | solution.py:131
  7.6 0.7 fusion.99
  11.4 0.6 slice_bitcast_fusion.7
  14.8 0.7 mul.302
  15.4 1.4 pad.4
  18.8 11.0 %collective-permute-start = (bf16[3,96,128]{2,1,0:T(8,128)(2,1)S(1)}, bf16[3,96,128]{2,1,0:T(8,128)(2,1)S(1)}, u32[]{:S(2)}, u32[]{:S(2)}) collective-permute-start(bf16[3,96,128]{2,1,0:T(8,128)(2,1)S(1)} %fusion.69), channel_id=1, source_target_pairs={{0,0},{1,16},{2,32},{3,48},{4,64},{5,80},{6,96},{7,112},{8,128},{9... | collective-permute-start | bytes 221192 | tf_op jit(solution)/shard_map/ppermute | solution.py:73
  30.3 0.7 fusion.27
  31.0 0.8 fusion.30
  32.0 1.5 %fusion.5 = f32[2304,128]{1,0:T(8,128)} fusion(bf16[2304,128]{1,0:T(8,128)(2,1)S(1)} %bitcast.190, bf16[2,128,128]{2,1,0:T(8,128)(2,1)S(1)} %copy-done.33), kind=kOutput, calls=%fused_computation.7 | convolution fusion | flops 76382208 | bytes 1802240 | tf_op jit(solution)/shard_map/dot_general | solution.py:26
  34.1 1.2 broadcast_dynamic-update-slice_fusion
  35.4 4.4 %all-to-all-start.1 = ((bf16[16,3,144,128]{3,2,1,0:T(8,128)(2,1)}), bf16[16,3,144,128]{3,2,1,0:T(8,128)(2,1)S(1)}, u32[]{:S(2)}, u32[]{:S(2)}) async-start(bf16[16,3,144,128]{3,2,1,0:T(8,128)(2,1)} %broadcast_dynamic-update-slice_fusion), calls=%async_computation.1 | async-start | bytes 3538944 | tf_op jit(solution)/shard_map/all_to_all | solution.py:150
  39.8 4.3 %collective-permute-start.1 = (bf16[2,3,96,128]{3,2,1,0:T(8,128)(2,1)S(1)}, bf16[2,3,96,128]{3,2,1,0:T(8,128)(2,1)S(1)}, u32[]{:S(2)}, u32[]{:S(2)}) collective-permute-start(bf16[2,3,96,128]{3,2,1,0:T(8,128)(2,1)S(1)} %pad_maximum_fusion.1), channel_id=1, source_target_pairs={{0,2},{1,3},{2,0},{3,1},{4,6},{5,7},{6,4},{7,5},{8,10},{9,11},{10,... | collective-permute-start | bytes 442376 | tf_op jit(solution)/shard_map/ppermute | solution.py:48
  44.1 5.7 %collective-permute-done.1 = bf16[2,3,96,128]{3,2,1,0:T(8,128)(2,1)S(1)} collective-permute-done((bf16[2,3,96,128]{3,2,1,0:T(8,128)(2,1)S(1)}, bf16[2,3,96,128]{3,2,1,0:T(8,128)(2,1)S(1)}, u32[]{:S(2)}, u32[]{:S(2)}) %collective-permute-start.1) | collective-permute-done | bytes 147488 | tf_op jit(solution)/shard_map/ppermute | solution.py:48
  49.9 6.0 %collective-permute-start.2 = (bf16[2,2,3,96,128]{4,3,2,0,1:T(8,128)(2,1)S(1)}, bf16[2,2,3,96,128]{4,3,2,0,1:T(8,128)(2,1)S(1)}, u32[]{:S(2)}, u32[]{:S(2)}) collective-permute-start(bf16[2,2,3,96,128]{4,3,2,0,1:T(8,128)(2,1)S(1)} %bitcast_dynamic-update-slice_fusion.8), channel_id=1, source_target_pairs={{0,8},{1,9},{2,10},{3,11},{4,12},{5,13},{6,14},{7,15},{8,0},{9,1},... | collective-permute-start | bytes 884744 | tf_op jit(solution)/shard_map/ppermute | solution.py:48
  55.9 0.7 collective-permute-start.4
  56.9 7.0 %collective-permute-done.2 = bf16[2,2,3,96,128]{4,3,2,0,1:T(8,128)(2,1)S(1)} collective-permute-done((bf16[2,2,3,96,128]{4,3,2,0,1:T(8,128)(2,1)S(1)}, bf16[2,2,3,96,128]{4,3,2,0,1:T(8,128)(2,1)S(1)}, u32[]{:S(2)}, u32[]{:S(2)}) %collective-permute-start.2) | collective-permute-done | bytes 294944 | tf_op jit(solution)/shard_map/ppermute | solution.py:48
  63.9 5.1 %collective-permute-done.3 = bf16[2,2,3,96,128]{4,3,2,0,1:T(8,128)(2,1)S(1)} collective-permute-done((bf16[2,2,3,96,128]{4,3,2,0,1:T(8,128)(2,1)S(1)}, bf16[2,2,3,96,128]{4,3,2,0,1:T(8,128)(2,1)S(1)}, u32[]{:S(2)}, u32[]{:S(2)}) %collective-permute-start.3) | collective-permute-done | bytes 294944 | tf_op jit(solution)/shard_map/ppermute | solution.py:48
  73.1 0.6 slice_bitcast_fusion.5
  74.4 1.4 bitcast_dynamic-update-slice_fusion.1
  75.8 1.2 fusion.97
  77.0 0.8 copy.38
  77.8 0.8 copy.39
  78.6 4.6 %all-to-all-done.1 = bf16[16,3,144,128]{3,2,1,0:T(8,128)(2,1)S(1)} async-done(((bf16[16,3,144,128]{3,2,1,0:T(8,128)(2,1)}), bf16[16,3,144,128]{3,2,1,0:T(8,128)(2,1)S(1)}, u32[]{:S(2)}, u32[]{:S(2)}) %all-to-all-start.1) | async-done | bytes 1769504 | tf_op jit(solution)/shard_map/all_to_all | solution.py:150
  83.3 0.6 dynamic-slice_bitcast_fusion
  84.0 1.0 copy.40
  85.1 1.9 %fusion.100 = (f32[6,48]{1,0:T(8,128)S(1)}, f32[128,6,48]{2,1,0:T(8,128)S(1)}) fusion(bf16[48,96,128]{1,0,2:T(8,128)(2,1)S(1)} %copy.40, bf16[3,96,128]{1,0,2:T(4,128)(2,1)} %bitcast.193, bf16[3,96,128]{1,0,2:T(4,128)(2,1)S(1)} %bitcast.192), kind=kOutput, calls=%fused_computation.185 | convolution fusion | flops 7409376 | bytes 1475712 | tf_op jit(solution)/shard_map/ikh,jkh->hij/dot_general | solution.py:159
  89.5 9.6 %collective-permute-start.6 = (bf16[6,48,128]{2,1,0:T(8,128)(2,1)S(1)}, bf16[6,48,128]{2,1,0:T(8,128)(2,1)}, u32[]{:S(2)}, u32[]{:S(2)}) collective-permute-start(bf16[6,48,128]{2,1,0:T(8,128)(2,1)S(1)} %get-tuple-element.72), channel_id=1, source_target_pairs={{0,0},{1,16},{2,32},{3,48},{4,64},{5,80},{6,96},{7,112},{8,128},{9... | collective-permute-start | bytes 221192 | tf_op jit(solution)/shard_map/ppermute | solution.py:73
  99.1 1.2 broadcast_in_dim.23
  100.3 5.2 %all-to-all-start.2 = ((bf16[16,6,48,128]{3,2,1,0:T(8,128)(2,1)}), bf16[16,6,48,128]{3,2,1,0:T(8,128)(2,1)S(1)}, u32[]{:S(2)}, u32[]{:S(2)}) async-start(bf16[16,6,48,128]{3,2,1,0:T(8,128)(2,1)} %broadcast_in_dim.23), calls=%async_computation.2 | async-start | bytes 2359296 | tf_op jit(solution)/shard_map/all_to_all | solution.py:165
  105.5 3.0 %collective-permute-start.7 = (bf16[6,48,128]{2,1,0:T(8,128)(2,1)}, bf16[6,48,128]{2,1,0:T(8,128)(2,1)}, u32[]{:S(2)}, u32[]{:S(2)}) collective-permute-start(bf16[6,48,128]{2,1,0:T(8,128)(2,1)} %collective-permute-done.6), channel_id=1, source_target_pairs={{0,2},{1,3},{2,0},{3,1},{4,6},{5,7},{6,4},{7,5},{8,10},{9,11},{10,... | collective-permute-start | bytes 221192 | tf_op jit(solution)/shard_map/ppermute | solution.py:48
  108.6 0.9 bitcast_dynamic-update-slice_fusion.15
  109.5 2.8 %copy.42 = bf16[48,96,128]{1,0,2:T(8,128)(2,1)} copy(bf16[48,96,128]{2,1,0:T(8,128)(2,1)} %bitcast.185) | data formatting | bytes 2359296 | tf_op jit(solution)/shard_map/optimization_barrier | solution.py:171
  112.3 0.9 bitcast_dynamic-update-slice_fusion.14
  113.2 0.9 collective-permute-start.8
  114.1 3.1 %collective-permute-start.9 = (bf16[2,6,48,128]{3,2,1,0:T(8,128)(2,1)S(1)}, bf16[2,6,48,128]{3,2,1,0:T(8,128)(2,1)S(1)}, u32[]{:S(2)}, u32[]{:S(2)}) collective-permute-start(bf16[2,6,48,128]{3,2,1,0:T(8,128)(2,1)S(1)} %bitcast_dynamic-update-slice_fusion.14), channel_id=1, source_target_pairs={{0,4},{1,5},{2,6},{3,7},{4,0},{5,1},{6,2},{7,3},{8,12},{9,13},{10,... | collective-permute-start | bytes 442376 | tf_op jit(solution)/shard_map/ppermute | solution.py:48
  117.5 2.3 %fusion.102 = (f32[48,48]{1,0:T(8,128)S(1)}, f32[128,48,48]{2,1,0:T(8,128)S(1)}) fusion(bf16[128,48,96]{2,1,0:T(8,128)(2,1)} %bitcast.181, bf16[48,96,128]{1,0,2:T(8,128)(2,1)S(1)} %copy.40), kind=kOutput, calls=%fused_computation.187 | convolution fusion | flops 56915712 | bytes 3548160 | tf_op jit(solution)/shard_map/hik,jkh->hij/dot_general | solution.py:168
  122.5 0.8 convert_reduce_fusion
  123.3 0.7 fusion.23
  124.1 0.8 fusion.26
  125.4 1.6 %pad_maximum_fusion = f32[2,48,48,128]{3,2,1,0:T(8,128)} fusion(f32[1,48,48,128]{3,2,1,0:T(8,128)S(1)} %convert_bitcast_fusion, f32[1,48,48,128]{3,2,1,0:T(8,128)S(1)} %bitcast.187), kind=kLoop, calls=%fused_computation.12 | loop fusion | flops 589824 | bytes 4718592 | tf_op jit(solution)/shard_map/stack | solution.py:177
  127.4 1.0 copy-done.2
  128.4 2.4 %copy.47 = bf16[96,48,128]{0,1,2:T(8,128)(2,1)S(1)} copy(bf16[96,48,128]{2,1,0:T(8,128)(2,1)} %bitcast.183) | data formatting | bytes 2359296 | tf_op jit(solution)/shard_map/reshape;reshape | solution.py:174
  130.8 5.1 %all-to-all-done.2 = bf16[16,6,48,128]{3,2,1,0:T(8,128)(2,1)S(1)} async-done(((bf16[16,6,48,128]{3,2,1,0:T(8,128)(2,1)}), bf16[16,6,48,128]{3,2,1,0:T(8,128)(2,1)S(1)}, u32[]{:S(2)}, u32[]{:S(2)}) %all-to-all-start.2) | async-done | bytes 1179680 | tf_op jit(solution)/shard_map/all_to_all | solution.py:165
  135.9 2.0 %copy.48 = bf16[96,48,128]{0,1,2:T(8,128)(2,1)} copy(bf16[96,48,128]{2,1,0:T(8,128)(2,1)S(1)} %bitcast.182) | data formatting | bytes 2359296 | tf_op jit(solution)/shard_map/reshape | solution.py:165
  138.0 2.3 %fusion.103 = (f32[48,48]{1,0:T(8,128)S(1)}, f32[128,48,48]{2,1,0:T(8,128)S(1)}) fusion(bf16[96,48,128]{0,1,2:T(8,128)(2,1)S(1)} %copy.47, bf16[96,48,128]{0,1,2:T(8,128)(2,1)} %copy.48), kind=kOutput, calls=%fused_computation.188 | convolution fusion | flops 56915712 | bytes 3548160 | tf_op jit(solution)/shard_map/kih,kjh->hij/dot_general | solution.py:179
  141.0 0.6 add_convert_fusion
  141.6 1.1 copy-done.1
  142.6 1.4 fusion.20
  (162 shorter events, 10.4 us)
Async XLA Ops:
  0.0 15.4 %copy-start = (bf16[48,48,128]{2,1,0:T(8,128)(2,1)S(1)}, bf16[48,48,128]{2,1,0:T(8,128)(2,1)}, u32[]{:S(2)}) copy-start(bf16[48,48,128]{2,1,0:T(8,128)(2,1)} %param.11) | copy-start | bytes 1769476
  0.0 7.6 %copy-start.26 = (s32[2,2]{1,0:T(2,128)S(1)}, s32[2,2]{1,0:T(2,128)}, u32[]{:S(2)}) copy-start(s32[2,2]{1,0:T(2,128)} %param.13) | copy-start | bytes 52
  0.0 9.6 %copy-start.25 = (s32[768]{0:T(1024)S(1)}, s32[768]{0:T(1024)}, u32[]{:S(2)}) copy-start(s32[768]{0:T(1024)} %param.12) | copy-start | bytes 9220
  0.0 11.4 %copy-start.30 = (f32[2,128]{1,0:T(2,128)S(1)}, f32[2,128]{1,0:T(2,128)}, u32[]{:S(2)}) copy-start(f32[2,128]{1,0:T(2,128)} %param.14) | copy-start | bytes 3076
  0.0 11.4 %copy-start.29 = (f32[2,128]{1,0:T(2,128)S(1)}, f32[2,128]{1,0:T(2,128)}, u32[]{:S(2)}) copy-start(f32[2,128]{1,0:T(2,128)} %param.15) | copy-start | bytes 3076
  0.0 18.3 %all-to-all-start = ((bf16[16,3,48,128]{3,2,1,0:T(8,128)(2,1)}), bf16[16,3,48,128]{3,2,1,0:T(8,128)(2,1)S(1)}, u32[]{:S(2)}, u32[]{:S(2)}) async-start(bf16[16,3,48,128]{3,2,1,0:T(8,128)(2,1)} %bitcast.178), calls=%async_computation | async-start | bytes 1179648 | tf_op jit(solution)/shard_map/all_to_all | solution.py:131
  12.0 19.0 %copy-start.12 = (f32[128]{0:T(128)}, f32[128]{0:T(128)S(1)}, u32[]{:S(2)}) copy-start(f32[128]{0:T(128)S(1)} %get-tuple-element.89) | copy-start | bytes 1540
  12.0 19.0 %copy-start.14 = (f32[128]{0:T(128)}, f32[128]{0:T(128)S(1)}, u32[]{:S(2)}) copy-start(f32[128]{0:T(128)S(1)} %get-tuple-element.106) | copy-start | bytes 1540
  15.4 2.7 %copy-start.7 = (bf16[2,128,256]{2,1,0:T(8,128)(2,1)S(1)}, bf16[2,128,256]{2,1,0:T(8,128)(2,1)}, u32[]{:S(2)}) copy-start(bf16[2,128,256]{2,1,0:T(8,128)(2,1)} %param.16) | copy-start | bytes 393220
  15.4 2.8 %copy-start.10 = (bf16[2,128,256]{2,1,0:T(8,128)(2,1)S(1)}, bf16[2,128,256]{2,1,0:T(8,128)(2,1)}, u32[]{:S(2)}) copy-start(bf16[2,128,256]{2,1,0:T(8,128)(2,1)} %param.17) | copy-start | bytes 393220
  18.8 14.8 %collective-permute-start = (bf16[3,96,128]{2,1,0:T(8,128)(2,1)S(1)}, bf16[3,96,128]{2,1,0:T(8,128)(2,1)S(1)}, u32[]{:S(2)}, u32[]{:S(2)}) collective-permute-start(bf16[3,96,128]{2,1,0:T(8,128)(2,1)S(1)} %fusion.69), channel_id=1, source_target_pairs={{0,0},{1,16},{2,32},{3,48},{4,64},{5,80},{6,96},{7,112},{8,128},{9... | collective-permute-start | bytes 221192 | tf_op jit(solution)/shard_map/ppermute | solution.py:73
  30.2 1.7 %copy-start.33 = (bf16[2,128,128]{2,1,0:T(8,128)(2,1)S(1)}, bf16[2,128,128]{2,1,0:T(8,128)(2,1)}, u32[]{:S(2)}) copy-start(bf16[2,128,128]{2,1,0:T(8,128)(2,1)} %param.21) | copy-start | bytes 196612
  35.4 47.9 %all-to-all-start.1 = ((bf16[16,3,144,128]{3,2,1,0:T(8,128)(2,1)}), bf16[16,3,144,128]{3,2,1,0:T(8,128)(2,1)S(1)}, u32[]{:S(2)}, u32[]{:S(2)}) async-start(bf16[16,3,144,128]{3,2,1,0:T(8,128)(2,1)} %broadcast_dynamic-update-slice_fusion), calls=%async_computation.1 | async-start | bytes 3538944 | tf_op jit(solution)/shard_map/all_to_all | solution.py:150
  39.8 10.1 %collective-permute-start.1 = (bf16[2,3,96,128]{3,2,1,0:T(8,128)(2,1)S(1)}, bf16[2,3,96,128]{3,2,1,0:T(8,128)(2,1)S(1)}, u32[]{:S(2)}, u32[]{:S(2)}) collective-permute-start(bf16[2,3,96,128]{3,2,1,0:T(8,128)(2,1)S(1)} %pad_maximum_fusion.1), channel_id=1, source_target_pairs={{0,2},{1,3},{2,0},{3,1},{4,6},{5,7},{6,4},{7,5},{8,10},{9,11},{10,... | collective-permute-start | bytes 442376 | tf_op jit(solution)/shard_map/ppermute | solution.py:48
  49.9 14.0 %collective-permute-start.2 = (bf16[2,2,3,96,128]{4,3,2,0,1:T(8,128)(2,1)S(1)}, bf16[2,2,3,96,128]{4,3,2,0,1:T(8,128)(2,1)S(1)}, u32[]{:S(2)}, u32[]{:S(2)}) collective-permute-start(bf16[2,2,3,96,128]{4,3,2,0,1:T(8,128)(2,1)S(1)} %bitcast_dynamic-update-slice_fusion.8), channel_id=1, source_target_pairs={{0,8},{1,9},{2,10},{3,11},{4,12},{5,13},{6,14},{7,15},{8,0},{9,1},... | collective-permute-start | bytes 884744 | tf_op jit(solution)/shard_map/ppermute | solution.py:48
  55.9 13.1 %collective-permute-start.3 = (bf16[2,2,3,96,128]{4,3,2,0,1:T(8,128)(2,1)S(1)}, bf16[2,2,3,96,128]{4,3,2,0,1:T(8,128)(2,1)S(1)}, u32[]{:S(2)}, u32[]{:S(2)}) collective-permute-start(bf16[2,2,3,96,128]{4,3,2,0,1:T(8,128)(2,1)S(1)} %bitcast_dynamic-update-slice_fusion.8), channel_id=1, source_target_pairs={{0,4},{1,5},{2,6},{3,7},{4,0},{5,1},{6,2},{7,3},{8,12},{9,13},{10,... | collective-permute-start | bytes 884744 | tf_op jit(solution)/shard_map/ppermute | solution.py:48
  55.9 13.2 %collective-permute-start.4 = (bf16[2,2,3,96,128]{4,3,2,0,1:T(8,128)(2,1)S(1)}, bf16[2,2,3,96,128]{4,3,2,0,1:T(8,128)(2,1)S(1)}, u32[]{:S(2)}, u32[]{:S(2)}) collective-permute-start(bf16[2,2,3,96,128]{4,3,2,0,1:T(8,128)(2,1)S(1)} %bitcast_dynamic-update-slice_fusion.8), channel_id=1, source_target_pairs={{0,12},{1,13},{2,14},{3,15},{4,8},{5,9},{6,10},{7,11},{8,4},{9,5},... | collective-permute-start | bytes 884744 | tf_op jit(solution)/shard_map/ppermute | solution.py:48
  56.8 16.3 %copy-start.31 = (f32[2,128]{1,0:T(2,128)S(1)}, f32[2,128]{1,0:T(2,128)}, u32[]{:S(2)}) copy-start(f32[2,128]{1,0:T(2,128)} %param.19) | copy-start | bytes 3076
  56.8 16.3 %copy-start.32 = (f32[2,128]{1,0:T(2,128)S(1)}, f32[2,128]{1,0:T(2,128)}, u32[]{:S(2)}) copy-start(f32[2,128]{1,0:T(2,128)} %param.18) | copy-start | bytes 3076
  69.1 5.2 %collective-permute-start.5 = (bf16[4,2,2,3,96,128]{5,4,3,1,0,2:T(8,128)(2,1)S(1)}, bf16[4,2,2,3,96,128]{5,4,3,1,0,2:T(8,128)(2,1)}, u32[]{:S(2)}, u32[]{:S(2)}) collective-permute-start(bf16[4,2,2,3,96,128]{5,4,3,1,0,2:T(8,128)(2,1)S(1)} %bitcast_dynamic-update-slice_fusion.7), channel_id=1, source_target_pairs={{0,1},{1,0},{2,3},{3,2},{4,5},{5,4},{6,7},{7,6},{8,9},{9,8},{10,11... | collective-permute-start | bytes 3538952 | tf_op jit(solution)/shard_map/ppermute | solution.py:48
  84.0 1.0 copy-start.6
  85.1 2.1 %copy-start.4 = (bf16[3,48,128]{2,1,0:T(8,128)(2,1)S(1)}, bf16[3,48,128]{2,1,0:T(8,128)(2,1)}, u32[]{:S(2)}) copy-start(bf16[3,48,128]{2,1,0:T(8,128)(2,1)} %get-tuple-element.44) | copy-start | bytes 110596
  85.1 2.1 %copy-start.5 = (bf16[3,48,128]{2,1,0:T(8,128)(2,1)S(1)}, bf16[3,48,128]{2,1,0:T(8,128)(2,1)}, u32[]{:S(2)}) copy-start(bf16[3,48,128]{2,1,0:T(8,128)(2,1)} %get-tuple-element.43) | copy-start | bytes 110596
  85.1 2.4 %copy-start.13 = (f32[128]{0:T(128)S(1)}, f32[128]{0:T(128)}, u32[]{:S(2)}) copy-start(f32[128]{0:T(128)} %copy-done.12) | copy-start | bytes 1540
  85.1 2.4 %copy-start.15 = (f32[128]{0:T(128)S(1)}, f32[128]{0:T(128)}, u32[]{:S(2)}) copy-start(f32[128]{0:T(128)} %copy-done.14) | copy-start | bytes 1540
  85.1 2.6 %copy-start.34 = (bf16[2,128,128]{2,1,0:T(8,128)(2,1)S(1)}, bf16[2,128,128]{2,1,0:T(8,128)(2,1)}, u32[]{:S(2)}) copy-start(bf16[2,128,128]{2,1,0:T(8,128)(2,1)} %param.21) | copy-start | bytes 196612
  87.0 0.9 copy-start.21
  87.0 0.9 copy-start.23
  87.0 1.3 copy-start.9
  87.5 1.3 copy-start.17
  87.5 1.3 copy-start.19
  87.7 1.3 copy-start.11
  88.3 1.0 copy-start.8
  88.3 1.0 copy-start.16
  89.5 16.0 %collective-permute-start.6 = (bf16[6,48,128]{2,1,0:T(8,128)(2,1)S(1)}, bf16[6,48,128]{2,1,0:T(8,128)(2,1)}, u32[]{:S(2)}, u32[]{:S(2)}) collective-permute-start(bf16[6,48,128]{2,1,0:T(8,128)(2,1)S(1)} %get-tuple-element.72), channel_id=1, source_target_pairs={{0,0},{1,16},{2,32},{3,48},{4,64},{5,80},{6,96},{7,112},{8,128},{9... | collective-permute-start | bytes 221192 | tf_op jit(solution)/shard_map/ppermute | solution.py:73
  100.3 35.7 %all-to-all-start.2 = ((bf16[16,6,48,128]{3,2,1,0:T(8,128)(2,1)}), bf16[16,6,48,128]{3,2,1,0:T(8,128)(2,1)S(1)}, u32[]{:S(2)}, u32[]{:S(2)}) async-start(bf16[16,6,48,128]{3,2,1,0:T(8,128)(2,1)} %broadcast_in_dim.23), calls=%async_computation.2 | async-start | bytes 2359296 | tf_op jit(solution)/shard_map/all_to_all | solution.py:165
  105.5 6.8 %collective-permute-start.7 = (bf16[6,48,128]{2,1,0:T(8,128)(2,1)}, bf16[6,48,128]{2,1,0:T(8,128)(2,1)}, u32[]{:S(2)}, u32[]{:S(2)}) collective-permute-start(bf16[6,48,128]{2,1,0:T(8,128)(2,1)} %collective-permute-done.6), channel_id=1, source_target_pairs={{0,2},{1,3},{2,0},{3,1},{4,6},{5,7},{6,4},{7,5},{8,10},{9,11},{10,... | collective-permute-start | bytes 221192 | tf_op jit(solution)/shard_map/ppermute | solution.py:48
  113.2 8.1 %collective-permute-start.8 = (bf16[2,6,48,128]{3,2,1,0:T(8,128)(2,1)S(1)}, bf16[2,6,48,128]{3,2,1,0:T(8,128)(2,1)S(1)}, u32[]{:S(2)}, u32[]{:S(2)}) collective-permute-start(bf16[2,6,48,128]{3,2,1,0:T(8,128)(2,1)S(1)} %bitcast_dynamic-update-slice_fusion.14), channel_id=1, source_target_pairs={{0,8},{1,9},{2,10},{3,11},{4,12},{5,13},{6,14},{7,15},{8,0},{9,1},... | collective-permute-start | bytes 442376 | tf_op jit(solution)/shard_map/ppermute | solution.py:48
  114.1 7.8 %collective-permute-start.9 = (bf16[2,6,48,128]{3,2,1,0:T(8,128)(2,1)S(1)}, bf16[2,6,48,128]{3,2,1,0:T(8,128)(2,1)S(1)}, u32[]{:S(2)}, u32[]{:S(2)}) collective-permute-start(bf16[2,6,48,128]{3,2,1,0:T(8,128)(2,1)S(1)} %bitcast_dynamic-update-slice_fusion.14), channel_id=1, source_target_pairs={{0,4},{1,5},{2,6},{3,7},{4,0},{5,1},{6,2},{7,3},{8,12},{9,13},{10,... | collective-permute-start | bytes 442376 | tf_op jit(solution)/shard_map/ppermute | solution.py:48
  117.2 5.1 %collective-permute-start.10 = (bf16[2,6,48,128]{3,2,1,0:T(8,128)(2,1)S(1)}, bf16[2,6,48,128]{3,2,1,0:T(8,128)(2,1)S(1)}, u32[]{:S(2)}, u32[]{:S(2)}) collective-permute-start(bf16[2,6,48,128]{3,2,1,0:T(8,128)(2,1)S(1)} %bitcast_dynamic-update-slice_fusion.14), channel_id=1, source_target_pairs={{0,12},{1,13},{2,14},{3,15},{4,8},{5,9},{6,10},{7,11},{8,4},{9,5},... | collective-permute-start | bytes 442376 | tf_op jit(solution)/shard_map/ppermute | solution.py:48
  119.9 0.7 copy-start.22
  121.2 1.3 copy-start.3
  122.4 4.9 %collective-permute-start.11 = (bf16[4,2,6,48,128]{4,3,2,1,0:T(8,128)(2,1)S(1)}, bf16[4,2,6,48,128]{4,3,2,1,0:T(8,128)(2,1)S(1)}, u32[]{:S(2)}, u32[]{:S(2)}) collective-permute-start(bf16[4,2,6,48,128]{4,3,2,1,0:T(8,128)(2,1)S(1)} %bitcast_dynamic-update-slice_fusion.10), channel_id=1, source_target_pairs={{0,1},{1,0},{2,3},{3,2},{4,5},{5,4},{6,7},{7,6},{8,9},{9,8},{10,11... | collective-permute-start | bytes 1769480 | tf_op jit(solution)/shard_map/ppermute | solution.py:48
  122.5 1.6 %copy-start.18 = (f32[128]{0:T(128)S(1)}, f32[128]{0:T(128)}, u32[]{:S(2)}) copy-start(f32[128]{0:T(128)} %get-tuple-element.88) | copy-start | bytes 1540
  122.5 1.6 %copy-start.20 = (f32[128]{0:T(128)S(1)}, f32[128]{0:T(128)}, u32[]{:S(2)}) copy-start(f32[128]{0:T(128)} %get-tuple-element.107) | copy-start | bytes 1540
  123.3 1.6 %copy-start.35 = (bf16[2,128,128]{2,1,0:T(8,128)(2,1)S(1)}, bf16[2,128,128]{2,1,0:T(8,128)(2,1)}, u32[]{:S(2)}) copy-start(bf16[2,128,128]{2,1,0:T(8,128)(2,1)} %param.21) | copy-start | bytes 196612
  127.4 1.0 copy-start.2
  141.0 1.7 %copy-start.1 = (f32[2,48,48,128]{3,2,1,0:T(8,128)S(1)}, f32[2,48,48,128]{3,2,1,0:T(8,128)}, u32[]{:S(2)}) copy-start(f32[2,48,48,128]{3,2,1,0:T(8,128)} %pad_maximum_fusion) | copy-start | bytes 7077892
  (3 other events, 1.9 us)

commit v4 on v2

--- a/solution.py
+++ b/solution.py
@@ -151,8 +151,10 @@
     rows = jnp.concatenate(rows, axis=0)
     right = chunks[:, :, : 2 * tile].reshape(tile, 2 * tile, hidden)
     lefts, _ = gather_col(jnp.stack([left_own, left_moved]), places)
-    left = lefts[:, 0].reshape(tile, 2 * tile, hidden)
+    left = lefts[:, 0].reshape(tile, 2 * tile, hidden).transpose(2, 0, 1)
+    left = with_layout_constraint(left, Layout(major_to_minor=(0, 1, 2)))
     left_rows = jnp.concatenate(pick(lefts[:, 1], 1), axis=0)
+    left, left_rows = lax.optimization_barrier((left, left_rows))
 
     contracted = jnp.einsum("ikh,jkh->hij", left_rows, right, preferred_element_type=jnp.float32)
     scaled = scale(spread_of(contracted), 0)
@@ -167,7 +169,6 @@
         return scale(spread_of(contracted), 0)
 
     next_left, left = lax.optimization_barrier((next_left, left))
-    left = with_layout_constraint(left.transpose(2, 0, 1), Layout(major_to_minor=(0, 1, 2)))
     next_left, scaled = gather_col(next_left, places, left, main_tile)
     next_left = next_left.reshape(2 * tile, tile, hidden)
     current = finish(pair_rep, scaled, gate, w_out[0])

time: 145 us -> 147 us (1.014)
  waiting for transfers between devices: 33.3 us -> 36.6 us
  local copies, waits for them, and re-layouts: 24.1 us -> 21.6 us
    all_to_all x1, waiting for transfers between devices: 7.43 us -> 12.6 us  [body(): chunks = lax.all_to_all(chunks, 'row', 0, 0, tiled=True)]
    ppermute x10, waiting for transfers between devices: 19.1 us -> 15.1 us  [swap(): return lax.ppermute(x, axis, [(p, p ^ bits) for p in range(n)])]
    all_to_all x1, waiting for transfers between devices: 3.85 us -> 6.86 us  [body(): lax.all_to_all(copies, 'row', 0, 0, tiled=True)]
    ppermute x10, starting transfers between devices: 16 us -> 18.5 us  [swap(): return lax.ppermute(x, axis, [(p, p ^ bits) for p in range(n)])]
    all_to_all x1, starting transfers between devices: 6.12 us -> 3.71 us  [body(): chunks = lax.all_to_all(chunks, 'row', 0, 0, tiled=True)]
    optimization_barrier x1, local copies, waits for them, and re-layouts: 2.8 us -> 0.88 us  [body(): left, left_rows = lax.optimization_barrier((left, left_rows))]
    ppermute x2, starting transfers between devices: 18.2 us -> 20.1 us  [transpose_devices(): return lax.ppermute(x, ('row', 'col'), pairs)]
    another operation x0 -> x1, local copies, waits for them, and re-layouts: none -> 1.82 us  [body(): left = lefts[:, 0].reshape(tile, 2 * tile, hidden).transpose(2, 0, 1)]
  transfers between devices with their start and end apart: 15 -> 15, of which waited for: 8 -> 9; matrix products, arithmetic and copies ran while one was open for 20% -> 18% of each run, Pallas kernels for 0% -> 0%
where the time goes in v4:
time: 147 us; the launch traced here: 146 us
  starting transfers between devices  53.5 us (36%)
  waiting for transfers between devices  36.6 us (25%)
  local copies, waits for them, and re-layouts  21.6 us (15%)
  matrix products  12.4 us (8%)
  between operations  11.1 us (8%)
  other arithmetic  10.7 us (7%)
    ppermute x2, starting transfers between devices, transpose_devices(): return lax.ppermute(x, ('row', 'col'), pairs)  20.1 us
    ppermute x10, starting transfers between devices, swap(): return lax.ppermute(x, axis, [(p, p ^ bits) for p in range(n)])  18.5 us
    ppermute x10, waiting for transfers between devices, swap(): return lax.ppermute(x, axis, [(p, p ^ bits) for p in range(n)])  15.1 us
    all_to_all x1, waiting for transfers between devices, body(): chunks = lax.all_to_all(chunks, 'row', 0, 0, tiled=True)  12.6 us
    all_to_all x1, starting transfers between devices, body(): lax.all_to_all(pair_rep.reshape(n, part, tile, width), 'col', 0, 0, tiled...  7.6 us
    all_to_all x1, waiting for transfers between devices, body(): lax.all_to_all(copies, 'row', 0, 0, tiled=True)  6.86 us
    all_to_all x1, starting transfers between devices, body(): chunks = lax.all_to_all(chunks, 'row', 0, 0, tiled=True)  3.71 us
    all_to_all x1, starting transfers between devices, body(): lax.all_to_all(copies, 'row', 0, 0, tiled=True)  3.7 us
  transfers between devices with their start and end apart: 15, of which 9 were waited for; matrix products, arithmetic and copies ran while one was open for 18% of the time, Pallas kernels for 0%

profile of v4, /device:TPU:4, one launch (start us, length us, event | category | flops | bytes accessed | tf_op | source)
XLA Modules:
  0.0 145.9 jit_solution(2682133667603248826)
XLA Ops:
  0.1 7.6 %all-to-all-start = ((bf16[16,3,48,128]{3,2,1,0:T(8,128)(2,1)}), bf16[16,3,48,128]{3,2,1,0:T(8,128)(2,1)S(1)}, u32[]{:S(2)}, u32[]{:S(2)}) async-start(bf16[16,3,48,128]{3,2,1,0:T(8,128)(2,1)} %bitcast.181), calls=%async_computation | async-start | bytes 1179648 | tf_op jit(solution)/shard_map/all_to_all | solution.py:131
  7.7 0.7 fusion.94
  11.4 0.6 slice_bitcast_fusion.7
  16.3 2.0 %all-to-all-done = bf16[16,3,48,128]{3,2,1,0:T(8,128)(2,1)S(1)} async-done(((bf16[16,3,48,128]{3,2,1,0:T(8,128)(2,1)}), bf16[16,3,48,128]{3,2,1,0:T(8,128)(2,1)S(1)}, u32[]{:S(2)}, u32[]{:S(2)}) %all-to-all-start) | async-done | bytes 589856 | tf_op jit(solution)/shard_map/all_to_all | solution.py:131
  18.9 11.0 %collective-permute-start = (bf16[3,96,128]{2,1,0:T(8,128)(2,1)S(1)}, bf16[3,96,128]{2,1,0:T(8,128)(2,1)S(1)}, u32[]{:S(2)}, u32[]{:S(2)}) collective-permute-start(bf16[3,96,128]{2,1,0:T(8,128)(2,1)S(1)} %fusion.65), channel_id=1, source_target_pairs={{0,0},{1,16},{2,32},{3,48},{4,64},{5,80},{6,96},{7,112},{8,128},{9... | collective-permute-start | bytes 221192 | tf_op jit(solution)/shard_map/ppermute | solution.py:73
  30.3 0.7 fusion.27
  31.0 0.8 fusion.30
  32.0 1.5 %fusion.5 = f32[2304,128]{1,0:T(8,128)} fusion(bf16[2304,128]{1,0:T(8,128)(2,1)S(1)} %bitcast.193, bf16[2,128,128]{2,1,0:T(8,128)(2,1)S(1)} %copy-done.25), kind=kOutput, calls=%fused_computation.7 | convolution fusion | flops 76382208 | bytes 1802240 | tf_op jit(solution)/shard_map/dot_general | solution.py:26
  34.3 1.4 pad_maximum_fusion.1
  35.7 2.6 %collective-permute-start.1 = (bf16[2,3,96,128]{3,2,1,0:T(8,128)(2,1)S(1)}, bf16[2,3,96,128]{3,2,1,0:T(8,128)(2,1)S(1)}, u32[]{:S(2)}, u32[]{:S(2)}) collective-permute-start(bf16[2,3,96,128]{3,2,1,0:T(8,128)(2,1)S(1)} %pad_maximum_fusion.2), channel_id=1, source_target_pairs={{0,2},{1,3},{2,0},{3,1},{4,6},{5,7},{6,4},{7,5},{8,10},{9,11},{10,... | collective-permute-start | bytes 442376 | tf_op jit(solution)/shard_map/ppermute | solution.py:48
  38.3 3.7 %all-to-all-start.1 = ((bf16[16,3,144,128]{3,2,1,0:T(8,128)(2,1)}), bf16[16,3,144,128]{3,2,1,0:T(8,128)(2,1)S(1)}, u32[]{:S(2)}, u32[]{:S(2)}) async-start(bf16[16,3,144,128]{3,2,1,0:T(8,128)(2,1)} %pad_maximum_fusion.1), calls=%async_computation.1 | async-start | bytes 3538944 | tf_op jit(solution)/shard_map/all_to_all | solution.py:148
  42.1 1.2 collective-permute-done.1
  43.3 5.4 %collective-permute-start.2 = (bf16[2,2,3,96,128]{4,3,2,0,1:T(8,128)(2,1)S(1)}, bf16[2,2,3,96,128]{4,3,2,0,1:T(8,128)(2,1)S(1)}, u32[]{:S(2)}, u32[]{:S(2)}) collective-permute-start(bf16[2,2,3,96,128]{4,3,2,0,1:T(8,128)(2,1)S(1)} %bitcast_dynamic-update-slice_fusion.8), channel_id=1, source_target_pairs={{0,8},{1,9},{2,10},{3,11},{4,12},{5,13},{6,14},{7,15},{8,0},{9,1},... | collective-permute-start | bytes 884744 | tf_op jit(solution)/shard_map/ppermute | solution.py:48
  48.7 0.7 collective-permute-start.4
  49.6 7.1 %collective-permute-done.2 = bf16[2,2,3,96,128]{4,3,2,0,1:T(8,128)(2,1)S(1)} collective-permute-done((bf16[2,2,3,96,128]{4,3,2,0,1:T(8,128)(2,1)S(1)}, bf16[2,2,3,96,128]{4,3,2,0,1:T(8,128)(2,1)S(1)}, u32[]{:S(2)}, u32[]{:S(2)}) %collective-permute-start.2) | collective-permute-done | bytes 294944 | tf_op jit(solution)/shard_map/ppermute | solution.py:48
  56.7 3.9 %collective-permute-done.3 = bf16[2,2,3,96,128]{4,3,2,0,1:T(8,128)(2,1)S(1)} collective-permute-done((bf16[2,2,3,96,128]{4,3,2,0,1:T(8,128)(2,1)S(1)}, bf16[2,2,3,96,128]{4,3,2,0,1:T(8,128)(2,1)S(1)}, u32[]{:S(2)}, u32[]{:S(2)}) %collective-permute-start.3) | collective-permute-done | bytes 294944 | tf_op jit(solution)/shard_map/ppermute | solution.py:48
  64.8 1.3 slice_bitcast_fusion.5
  66.8 1.4 bitcast_dynamic-update-slice_fusion.1
  68.2 1.2 fusion.92
  69.4 1.8 %copy.54 = bf16[48,96,128]{1,0,2:T(8,128)(2,1)} copy(bf16[48,96,128]{2,1,0:T(8,128)(2,1)S(1)} %bitcast.188) | data formatting | bytes 2359296 | tf_op jit(solution)/shard_map/reshape;squeeze | solution.py:154
  71.2 0.9 dynamic-slice_bitcast_fusion.1
  72.2 0.9 copy.55
  73.1 12.6 %all-to-all-done.1 = bf16[16,3,144,128]{3,2,1,0:T(8,128)(2,1)S(1)} async-done(((bf16[16,3,144,128]{3,2,1,0:T(8,128)(2,1)}), bf16[16,3,144,128]{3,2,1,0:T(8,128)(2,1)S(1)}, u32[]{:S(2)}, u32[]{:S(2)}) %all-to-all-start.1) | async-done | bytes 1769504 | tf_op jit(solution)/shard_map/all_to_all | solution.py:148
  85.7 0.7 dynamic-slice_bitcast_fusion.2
  86.4 1.0 copy.56
  87.5 1.9 %fusion.95 = (f32[6,48]{1,0:T(8,128)S(1)}, f32[128,6,48]{2,1,0:T(8,128)S(1)}) fusion(bf16[6,96,128]{1,0,2:T(8,128)(2,1)} %copy.55, bf16[48,96,128]{1,0,2:T(8,128)(2,1)S(1)} %copy.56), kind=kOutput, calls=%fused_computation.181 | convolution fusion | flops 7114464 | bytes 1475712 | tf_op jit(solution)/shard_map/ikh,jkh->hij/dot_general | solution.py:159
  91.8 9.0 %collective-permute-start.6 = (bf16[6,48,128]{2,1,0:T(8,128)(2,1)S(1)}, bf16[6,48,128]{2,1,0:T(8,128)(2,1)S(1)}, u32[]{:S(2)}, u32[]{:S(2)}) collective-permute-start(bf16[6,48,128]{2,1,0:T(8,128)(2,1)S(1)} %get-tuple-element.74), channel_id=1, source_target_pairs={{0,0},{1,16},{2,32},{3,48},{4,64},{5,80},{6,96},{7,112},{8,128},{9... | collective-permute-start | bytes 221192 | tf_op jit(solution)/shard_map/ppermute | solution.py:73
  100.9 1.2 broadcast_in_dim.23
  102.1 3.7 %all-to-all-start.2 = ((bf16[16,6,48,128]{3,2,1,0:T(8,128)(2,1)}), bf16[16,6,48,128]{3,2,1,0:T(8,128)(2,1)S(1)}, u32[]{:S(2)}, u32[]{:S(2)}) async-start(bf16[16,6,48,128]{3,2,1,0:T(8,128)(2,1)} %broadcast_in_dim.23), calls=%async_computation.2 | async-start | bytes 2359296 | tf_op jit(solution)/shard_map/all_to_all | solution.py:165
  105.8 5.2 %collective-permute-start.7 = (bf16[6,48,128]{2,1,0:T(8,128)(2,1)S(1)}, bf16[6,48,128]{2,1,0:T(8,128)(2,1)S(1)}, u32[]{:S(2)}, u32[]{:S(2)}) collective-permute-start(bf16[6,48,128]{2,1,0:T(8,128)(2,1)S(1)} %collective-permute-done.6), channel_id=1, source_target_pairs={{0,2},{1,3},{2,0},{3,1},{4,6},{5,7},{6,4},{7,5},{8,10},{9,11},{10,... | collective-permute-start | bytes 221192 | tf_op jit(solution)/shard_map/ppermute | solution.py:48
  111.1 2.3 %collective-permute-done.7 = bf16[6,48,128]{2,1,0:T(8,128)(2,1)S(1)} collective-permute-done((bf16[6,48,128]{2,1,0:T(8,128)(2,1)S(1)}, bf16[6,48,128]{2,1,0:T(8,128)(2,1)S(1)}, u32[]{:S(2)}, u32[]{:S(2)}) %collective-permute-start.7) | collective-permute-done | bytes 73760 | tf_op jit(solution)/shard_map/ppermute | solution.py:48
  113.7 1.9 %collective-permute-start.9 = (bf16[2,6,48,128]{3,2,1,0:T(8,128)(2,1)S(1)}, bf16[2,6,48,128]{3,2,1,0:T(8,128)(2,1)S(1)}, u32[]{:S(2)}, u32[]{:S(2)}) collective-permute-start(bf16[2,6,48,128]{3,2,1,0:T(8,128)(2,1)S(1)} %bitcast_dynamic-update-slice_fusion.14), channel_id=1, source_target_pairs={{0,4},{1,5},{2,6},{3,7},{4,0},{5,1},{6,2},{7,3},{8,12},{9,13},{10,... | collective-permute-start | bytes 442376 | tf_op jit(solution)/shard_map/ppermute | solution.py:48
  115.6 2.1 %collective-permute-start.10 = (bf16[2,6,48,128]{3,2,1,0:T(8,128)(2,1)S(1)}, bf16[2,6,48,128]{3,2,1,0:T(8,128)(2,1)S(1)}, u32[]{:S(2)}, u32[]{:S(2)}) collective-permute-start(bf16[2,6,48,128]{3,2,1,0:T(8,128)(2,1)S(1)} %bitcast_dynamic-update-slice_fusion.14), channel_id=1, source_target_pairs={{0,12},{1,13},{2,14},{3,15},{4,8},{5,9},{6,10},{7,11},{8,4},{9,5},... | collective-permute-start | bytes 442376 | tf_op jit(solution)/shard_map/ppermute | solution.py:48
  117.8 2.3 %fusion.97 = (f32[48,48]{1,0:T(8,128)S(1)}, f32[128,48,48]{2,1,0:T(8,128)S(1)}) fusion(bf16[128,48,96]{2,1,0:T(8,128)(2,1)} %bitcast.184, bf16[48,96,128]{1,0,2:T(8,128)(2,1)S(1)} %copy.56), kind=kOutput, calls=%fused_computation.183 | convolution fusion | flops 56915712 | bytes 3548160 | tf_op jit(solution)/shard_map/hik,jkh->hij/dot_general | solution.py:168
  120.8 0.6 add_convert_fusion.1
  122.0 0.6 copy-done.3
  122.6 0.8 convert_reduce_fusion
  123.5 0.7 fusion.23
  124.2 0.8 fusion.26
  125.6 1.6 %pad_maximum_fusion = f32[2,48,48,128]{3,2,1,0:T(8,128)} fusion(f32[1,48,48,128]{3,2,1,0:T(8,128)S(1)} %convert_bitcast_fusion, f32[1,48,48,128]{3,2,1,0:T(8,128)S(1)} %bitcast.190), kind=kLoop, calls=%fused_computation.12 | loop fusion | flops 589824 | bytes 4718592 | tf_op jit(solution)/shard_map/stack | solution.py:176
  127.5 1.0 copy-done.2
  128.6 2.4 %copy.62 = bf16[96,48,128]{0,1,2:T(8,128)(2,1)S(1)} copy(bf16[96,48,128]{2,1,0:T(8,128)(2,1)} %bitcast.186) | data formatting | bytes 2359296 | tf_op jit(solution)/shard_map/reshape;reshape | solution.py:173
  130.9 6.9 %all-to-all-done.2 = bf16[16,6,48,128]{3,2,1,0:T(8,128)(2,1)S(1)} async-done(((bf16[16,6,48,128]{3,2,1,0:T(8,128)(2,1)}), bf16[16,6,48,128]{3,2,1,0:T(8,128)(2,1)S(1)}, u32[]{:S(2)}, u32[]{:S(2)}) %all-to-all-start.2) | async-done | bytes 1179680 | tf_op jit(solution)/shard_map/all_to_all | solution.py:165
  137.8 2.0 %copy.63 = bf16[96,48,128]{0,1,2:T(8,128)(2,1)} copy(bf16[96,48,128]{2,1,0:T(8,128)(2,1)S(1)} %bitcast.185) | data formatting | bytes 2359296 | tf_op jit(solution)/shard_map/reshape | solution.py:165
  139.8 2.3 %fusion.98 = (f32[48,48]{1,0:T(8,128)S(1)}, f32[128,48,48]{2,1,0:T(8,128)S(1)}) fusion(bf16[96,48,128]{0,1,2:T(8,128)(2,1)S(1)} %copy.62, bf16[96,48,128]{0,1,2:T(8,128)(2,1)} %copy.63), kind=kOutput, calls=%fused_computation.184 | convolution fusion | flops 56915712 | bytes 3548160 | tf_op jit(solution)/shard_map/kih,kjh->hij/dot_general | solution.py:178
  142.9 0.6 add_convert_fusion
  143.4 1.1 copy-done.1
  144.5 1.4 fusion.20
  (146 shorter events, 9.7 us)
Async XLA Ops:
  0.0 29.9 %copy-start = (bf16[48,48,128]{2,1,0:T(8,128)(2,1)S(1)}, bf16[48,48,128]{2,1,0:T(8,128)(2,1)}, u32[]{:S(2)}) copy-start(bf16[48,48,128]{2,1,0:T(8,128)(2,1)} %param.11) | copy-start | bytes 1769476
  0.0 7.6 %copy-start.20 = (s32[2,2]{1,0:T(2,128)S(1)}, s32[2,2]{1,0:T(2,128)}, u32[]{:S(2)}) copy-start(s32[2,2]{1,0:T(2,128)} %param.13) | copy-start | bytes 52
  0.0 9.7 %copy-start.19 = (s32[768]{0:T(1024)S(1)}, s32[768]{0:T(1024)}, u32[]{:S(2)}) copy-start(s32[768]{0:T(1024)} %param.12) | copy-start | bytes 9220
  0.0 11.4 %copy-start.24 = (f32[2,128]{1,0:T(2,128)S(1)}, f32[2,128]{1,0:T(2,128)}, u32[]{:S(2)}) copy-start(f32[2,128]{1,0:T(2,128)} %param.14) | copy-start | bytes 3076
  0.0 11.4 %copy-start.23 = (f32[2,128]{1,0:T(2,128)S(1)}, f32[2,128]{1,0:T(2,128)}, u32[]{:S(2)}) copy-start(f32[2,128]{1,0:T(2,128)} %param.15) | copy-start | bytes 3076
  0.0 16.2 %copy-start.6 = (bf16[2,128,256]{2,1,0:T(8,128)(2,1)S(1)}, bf16[2,128,256]{2,1,0:T(8,128)(2,1)}, u32[]{:S(2)}) copy-start(bf16[2,128,256]{2,1,0:T(8,128)(2,1)} %param.16) | copy-start | bytes 393220
  0.0 16.3 %copy-start.9 = (bf16[2,128,256]{2,1,0:T(8,128)(2,1)S(1)}, bf16[2,128,256]{2,1,0:T(8,128)(2,1)}, u32[]{:S(2)}) copy-start(bf16[2,128,256]{2,1,0:T(8,128)(2,1)} %param.17) | copy-start | bytes 393220
  0.1 18.3 %all-to-all-start = ((bf16[16,3,48,128]{3,2,1,0:T(8,128)(2,1)}), bf16[16,3,48,128]{3,2,1,0:T(8,128)(2,1)S(1)}, u32[]{:S(2)}, u32[]{:S(2)}) async-start(bf16[16,3,48,128]{3,2,1,0:T(8,128)(2,1)} %bitcast.181), calls=%async_computation | async-start | bytes 1179648 | tf_op jit(solution)/shard_map/all_to_all | solution.py:131
  12.0 79.2 %copy-start.11 = (f32[128]{0:T(128)}, f32[128]{0:T(128)S(1)}, u32[]{:S(2)}) copy-start(f32[128]{0:T(128)S(1)} %get-tuple-element.90) | copy-start | bytes 1540
  18.9 14.8 %collective-permute-start = (bf16[3,96,128]{2,1,0:T(8,128)(2,1)S(1)}, bf16[3,96,128]{2,1,0:T(8,128)(2,1)S(1)}, u32[]{:S(2)}, u32[]{:S(2)}) collective-permute-start(bf16[3,96,128]{2,1,0:T(8,128)(2,1)S(1)} %fusion.65), channel_id=1, source_target_pairs={{0,0},{1,16},{2,32},{3,48},{4,64},{5,80},{6,96},{7,112},{8,128},{9... | collective-permute-start | bytes 221192 | tf_op jit(solution)/shard_map/ppermute | solution.py:73
  30.3 1.7 %copy-start.25 = (bf16[2,128,128]{2,1,0:T(8,128)(2,1)S(1)}, bf16[2,128,128]{2,1,0:T(8,128)(2,1)}, u32[]{:S(2)}) copy-start(bf16[2,128,128]{2,1,0:T(8,128)(2,1)} %param.21) | copy-start | bytes 196612
  35.7 7.6 %collective-permute-start.1 = (bf16[2,3,96,128]{3,2,1,0:T(8,128)(2,1)S(1)}, bf16[2,3,96,128]{3,2,1,0:T(8,128)(2,1)S(1)}, u32[]{:S(2)}, u32[]{:S(2)}) collective-permute-start(bf16[2,3,96,128]{3,2,1,0:T(8,128)(2,1)S(1)} %pad_maximum_fusion.2), channel_id=1, source_target_pairs={{0,2},{1,3},{2,0},{3,1},{4,6},{5,7},{6,4},{7,5},{8,10},{9,11},{10,... | collective-permute-start | bytes 442376 | tf_op jit(solution)/shard_map/ppermute | solution.py:48
  38.3 47.4 %all-to-all-start.1 = ((bf16[16,3,144,128]{3,2,1,0:T(8,128)(2,1)}), bf16[16,3,144,128]{3,2,1,0:T(8,128)(2,1)S(1)}, u32[]{:S(2)}, u32[]{:S(2)}) async-start(bf16[16,3,144,128]{3,2,1,0:T(8,128)(2,1)} %pad_maximum_fusion.1), calls=%async_computation.1 | async-start | bytes 3538944 | tf_op jit(solution)/shard_map/all_to_all | solution.py:148
  43.3 13.4 %collective-permute-start.2 = (bf16[2,2,3,96,128]{4,3,2,0,1:T(8,128)(2,1)S(1)}, bf16[2,2,3,96,128]{4,3,2,0,1:T(8,128)(2,1)S(1)}, u32[]{:S(2)}, u32[]{:S(2)}) collective-permute-start(bf16[2,2,3,96,128]{4,3,2,0,1:T(8,128)(2,1)S(1)} %bitcast_dynamic-update-slice_fusion.8), channel_id=1, source_target_pairs={{0,8},{1,9},{2,10},{3,11},{4,12},{5,13},{6,14},{7,15},{8,0},{9,1},... | collective-permute-start | bytes 884744 | tf_op jit(solution)/shard_map/ppermute | solution.py:48
  48.7 11.9 %collective-permute-start.3 = (bf16[2,2,3,96,128]{4,3,2,0,1:T(8,128)(2,1)S(1)}, bf16[2,2,3,96,128]{4,3,2,0,1:T(8,128)(2,1)S(1)}, u32[]{:S(2)}, u32[]{:S(2)}) collective-permute-start(bf16[2,2,3,96,128]{4,3,2,0,1:T(8,128)(2,1)S(1)} %bitcast_dynamic-update-slice_fusion.8), channel_id=1, source_target_pairs={{0,4},{1,5},{2,6},{3,7},{4,0},{5,1},{6,2},{7,3},{8,12},{9,13},{10,... | collective-permute-start | bytes 884744 | tf_op jit(solution)/shard_map/ppermute | solution.py:48
  48.7 12.3 %collective-permute-start.4 = (bf16[2,2,3,96,128]{4,3,2,0,1:T(8,128)(2,1)S(1)}, bf16[2,2,3,96,128]{4,3,2,0,1:T(8,128)(2,1)S(1)}, u32[]{:S(2)}, u32[]{:S(2)}) collective-permute-start(bf16[2,2,3,96,128]{4,3,2,0,1:T(8,128)(2,1)S(1)} %bitcast_dynamic-update-slice_fusion.8), channel_id=1, source_target_pairs={{0,12},{1,13},{2,14},{3,15},{4,8},{5,9},{6,10},{7,11},{8,4},{9,5},... | collective-permute-start | bytes 884744 | tf_op jit(solution)/shard_map/ppermute | solution.py:48
  61.1 5.7 %collective-permute-start.5 = (bf16[4,2,2,3,96,128]{5,4,3,1,0,2:T(8,128)(2,1)S(1)}, bf16[4,2,2,3,96,128]{5,4,3,1,0,2:T(8,128)(2,1)}, u32[]{:S(2)}, u32[]{:S(2)}) collective-permute-start(bf16[4,2,2,3,96,128]{5,4,3,1,0,2:T(8,128)(2,1)S(1)} %bitcast_dynamic-update-slice_fusion.7), channel_id=1, source_target_pairs={{0,1},{1,0},{2,3},{3,2},{4,5},{5,4},{6,7},{7,6},{8,9},{9,8},{10,11... | collective-permute-start | bytes 3538952 | tf_op jit(solution)/shard_map/ppermute | solution.py:48
  87.4 2.1 %copy-start.4 = (bf16[3,48,128]{2,1,0:T(8,128)(2,1)S(1)}, bf16[3,48,128]{2,1,0:T(8,128)(2,1)}, u32[]{:S(2)}) copy-start(bf16[3,48,128]{2,1,0:T(8,128)(2,1)} %get-tuple-element.44) | copy-start | bytes 110596
  87.5 2.1 %copy-start.5 = (bf16[3,48,128]{2,1,0:T(8,128)(2,1)S(1)}, bf16[3,48,128]{2,1,0:T(8,128)(2,1)}, u32[]{:S(2)}) copy-start(bf16[3,48,128]{2,1,0:T(8,128)(2,1)} %get-tuple-element.43) | copy-start | bytes 110596
  87.5 2.6 %copy-start.26 = (bf16[2,128,128]{2,1,0:T(8,128)(2,1)S(1)}, bf16[2,128,128]{2,1,0:T(8,128)(2,1)}, u32[]{:S(2)}) copy-start(bf16[2,128,128]{2,1,0:T(8,128)(2,1)} %param.21) | copy-start | bytes 196612
  89.4 0.9 copy-start.15
  89.4 0.9 copy-start.17
  89.4 1.3 copy-start.8
  89.9 1.3 copy-start.13
  90.1 1.3 copy-start.10
  90.7 1.0 copy-start.7
  91.8 14.0 %collective-permute-start.6 = (bf16[6,48,128]{2,1,0:T(8,128)(2,1)S(1)}, bf16[6,48,128]{2,1,0:T(8,128)(2,1)S(1)}, u32[]{:S(2)}, u32[]{:S(2)}) collective-permute-start(bf16[6,48,128]{2,1,0:T(8,128)(2,1)S(1)} %get-tuple-element.74), channel_id=1, source_target_pairs={{0,0},{1,16},{2,32},{3,48},{4,64},{5,80},{6,96},{7,112},{8,128},{9... | collective-permute-start | bytes 221192 | tf_op jit(solution)/shard_map/ppermute | solution.py:73
  102.1 35.7 %all-to-all-start.2 = ((bf16[16,6,48,128]{3,2,1,0:T(8,128)(2,1)}), bf16[16,6,48,128]{3,2,1,0:T(8,128)(2,1)S(1)}, u32[]{:S(2)}, u32[]{:S(2)}) async-start(bf16[16,6,48,128]{3,2,1,0:T(8,128)(2,1)} %broadcast_in_dim.23), calls=%async_computation.2 | async-start | bytes 2359296 | tf_op jit(solution)/shard_map/all_to_all | solution.py:165
  105.8 7.6 %collective-permute-start.7 = (bf16[6,48,128]{2,1,0:T(8,128)(2,1)S(1)}, bf16[6,48,128]{2,1,0:T(8,128)(2,1)S(1)}, u32[]{:S(2)}, u32[]{:S(2)}) collective-permute-start(bf16[6,48,128]{2,1,0:T(8,128)(2,1)S(1)} %collective-permute-done.6), channel_id=1, source_target_pairs={{0,2},{1,3},{2,0},{3,1},{4,6},{5,7},{6,4},{7,5},{8,10},{9,11},{10,... | collective-permute-start | bytes 221192 | tf_op jit(solution)/shard_map/ppermute | solution.py:48
  113.4 8.1 %collective-permute-start.8 = (bf16[2,6,48,128]{3,2,1,0:T(8,128)(2,1)S(1)}, bf16[2,6,48,128]{3,2,1,0:T(8,128)(2,1)S(1)}, u32[]{:S(2)}, u32[]{:S(2)}) collective-permute-start(bf16[2,6,48,128]{3,2,1,0:T(8,128)(2,1)S(1)} %bitcast_dynamic-update-slice_fusion.14), channel_id=1, source_target_pairs={{0,8},{1,9},{2,10},{3,11},{4,12},{5,13},{6,14},{7,15},{8,0},{9,1},... | collective-permute-start | bytes 442376 | tf_op jit(solution)/shard_map/ppermute | solution.py:48
  113.7 7.8 %collective-permute-start.9 = (bf16[2,6,48,128]{3,2,1,0:T(8,128)(2,1)S(1)}, bf16[2,6,48,128]{3,2,1,0:T(8,128)(2,1)S(1)}, u32[]{:S(2)}, u32[]{:S(2)}) collective-permute-start(bf16[2,6,48,128]{3,2,1,0:T(8,128)(2,1)S(1)} %bitcast_dynamic-update-slice_fusion.14), channel_id=1, source_target_pairs={{0,4},{1,5},{2,6},{3,7},{4,0},{5,1},{6,2},{7,3},{8,12},{9,13},{10,... | collective-permute-start | bytes 442376 | tf_op jit(solution)/shard_map/ppermute | solution.py:48
  115.6 6.3 %collective-permute-start.10 = (bf16[2,6,48,128]{3,2,1,0:T(8,128)(2,1)S(1)}, bf16[2,6,48,128]{3,2,1,0:T(8,128)(2,1)S(1)}, u32[]{:S(2)}, u32[]{:S(2)}) collective-permute-start(bf16[2,6,48,128]{3,2,1,0:T(8,128)(2,1)S(1)} %bitcast_dynamic-update-slice_fusion.14), channel_id=1, source_target_pairs={{0,12},{1,13},{2,14},{3,15},{4,8},{5,9},{6,10},{7,11},{8,4},{9,5},... | collective-permute-start | bytes 442376 | tf_op jit(solution)/shard_map/ppermute | solution.py:48
  120.1 0.6 copy-start.16
  120.1 0.6 copy-start.18
  121.3 1.3 copy-start.3
  121.9 5.5 %collective-permute-start.11 = (bf16[4,2,6,48,128]{4,3,2,1,0:T(8,128)(2,1)S(1)}, bf16[4,2,6,48,128]{4,3,2,1,0:T(8,128)(2,1)S(1)}, u32[]{:S(2)}, u32[]{:S(2)}) collective-permute-start(bf16[4,2,6,48,128]{4,3,2,1,0:T(8,128)(2,1)S(1)} %bitcast_dynamic-update-slice_fusion.10), channel_id=1, source_target_pairs={{0,1},{1,0},{2,3},{3,2},{4,5},{5,4},{6,7},{7,6},{8,9},{9,8},{10,11... | collective-permute-start | bytes 1769480 | tf_op jit(solution)/shard_map/ppermute | solution.py:48
  122.6 1.6 %copy-start.12 = (f32[128]{0:T(128)S(1)}, f32[128]{0:T(128)}, u32[]{:S(2)}) copy-start(f32[128]{0:T(128)} %copy-done.11) | copy-start | bytes 1540
  122.6 1.6 %copy-start.14 = (f32[128]{0:T(128)S(1)}, f32[128]{0:T(128)}, u32[]{:S(2)}) copy-start(f32[128]{0:T(128)} %get-tuple-element.109) | copy-start | bytes 1540
  123.5 1.6 %copy-start.27 = (bf16[2,128,128]{2,1,0:T(8,128)(2,1)S(1)}, bf16[2,128,128]{2,1,0:T(8,128)(2,1)}, u32[]{:S(2)}) copy-start(bf16[2,128,128]{2,1,0:T(8,128)(2,1)} %param.21) | copy-start | bytes 196612
  127.5 1.0 copy-start.2
  142.2 0.6 copy-start.21
  142.2 0.6 copy-start.22
  142.9 1.7 %copy-start.1 = (f32[2,48,48,128]{3,2,1,0:T(8,128)S(1)}, f32[2,48,48,128]{3,2,1,0:T(8,128)}, u32[]{:S(2)}) copy-start(f32[2,48,48,128]{3,2,1,0:T(8,128)} %pad_maximum_fusion) | copy-start | bytes 7077892

commit v5 on v2

--- a/solution.py
+++ b/solution.py
@@ -171,13 +171,12 @@
     next_left, scaled = gather_col(next_left, places, left, main_tile)
     next_left = next_left.reshape(2 * tile, tile, hidden)
     current = finish(pair_rep, scaled, gate, w_out[0])
-    gate = gate_of(norm_in(current, 1), 1).reshape(current.shape)
-    kept = lax.optimization_barrier(jnp.stack([gate, current.astype(jnp.float32)]))
+    gate = gate_of(norm_in(current, 1), 1)
 
     contracted = jnp.einsum(
         "kih,kjh->hij", next_left, next_right, preferred_element_type=jnp.float32
     )
-    return finish(kept[1], scale(spread_of(contracted), 1), kept[0], w_out[1])
+    return finish(current, scale(spread_of(contracted), 1), gate, w_out[1])
 
 
 def solution(mesh):

time: 145 us -> 147 us (1.014)
  other arithmetic: 10.7 us -> 8.92 us
  waiting for transfers between devices: 33.3 us -> 34.9 us
    another operation x2 -> x0, other arithmetic: 1.67 us -> none  [body(): jnp.stack([gate, current.astype(jnp.float32)])]
    all_to_all x1, waiting for transfers between devices: 3.85 us -> 5.4 us  [body(): lax.all_to_all(copies, 'row', 0, 0, tiled=True)]
    unnamed x72 -> x74, local copies, waits for them, and re-layouts: 3.22 us -> 3.25 us
  transfers between devices with their start and end apart: 15 -> 15, of which waited for: 8 -> 8; matrix products, arithmetic and copies ran while one was open for 20% -> 19% of each run, Pallas kernels for 0% -> 0%
where the time goes in v5:
time: 147 us; the launch traced here: 146 us
  starting transfers between devices  52.8 us (36%)
  waiting for transfers between devices  34.9 us (24%)
  local copies, waits for them, and re-layouts  24.2 us (16%)
  matrix products  13.5 us (9%)
  between operations  11.4 us (8%)
  other arithmetic  8.92 us (6%)
    ppermute x10, waiting for transfers between devices, swap(): return lax.ppermute(x, axis, [(p, p ^ bits) for p in range(n)])  18.4 us
    ppermute x2, starting transfers between devices, transpose_devices(): return lax.ppermute(x, ('row', 'col'), pairs)  18.2 us
    ppermute x10, starting transfers between devices, swap(): return lax.ppermute(x, axis, [(p, p ^ bits) for p in range(n)])  16.3 us
    all_to_all x1, waiting for transfers between devices, body(): chunks = lax.all_to_all(chunks, 'row', 0, 0, tiled=True)  8.33 us
    all_to_all x1, starting transfers between devices, body(): lax.all_to_all(pair_rep.reshape(n, part, tile, width), 'col', 0, 0, tiled...  7.6 us
    all_to_all x1, starting transfers between devices, body(): chunks = lax.all_to_all(chunks, 'row', 0, 0, tiled=True)  6.24 us
    all_to_all x1, waiting for transfers between devices, body(): lax.all_to_all(copies, 'row', 0, 0, tiled=True)  5.4 us
    all_to_all x1, starting transfers between devices, body(): lax.all_to_all(copies, 'row', 0, 0, tiled=True)  4.55 us
  transfers between devices with their start and end apart: 15, of which 8 were waited for; matrix products, arithmetic and copies ran while one was open for 19% of the time, Pallas kernels for 0%

profile of v5, /device:TPU:4, one launch (start us, length us, event | category | flops | bytes accessed | tf_op | source)
XLA Modules:
  0.0 145.7 jit_solution(16804709151447299673)
XLA Ops:
  0.1 7.6 %all-to-all-start = ((bf16[16,3,48,128]{3,2,1,0:T(8,128)(2,1)}), bf16[16,3,48,128]{3,2,1,0:T(8,128)(2,1)S(1)}, u32[]{:S(2)}, u32[]{:S(2)}) async-start(bf16[16,3,48,128]{3,2,1,0:T(8,128)(2,1)} %bitcast.168), calls=%async_computation | async-start | bytes 1179648 | tf_op jit(solution)/shard_map/all_to_all | solution.py:131
  7.7 0.7 fusion.98
  11.4 0.6 slice_bitcast_fusion.5
  14.9 0.7 mul.302
  17.0 1.3 all-to-all-done
  18.9 11.1 %collective-permute-start = (bf16[3,96,128]{2,1,0:T(8,128)(2,1)S(1)}, bf16[3,96,128]{2,1,0:T(8,128)(2,1)S(1)}, u32[]{:S(2)}, u32[]{:S(2)}) collective-permute-start(bf16[3,96,128]{2,1,0:T(8,128)(2,1)S(1)} %fusion.68), channel_id=1, source_target_pairs={{0,0},{1,16},{2,32},{3,48},{4,64},{5,80},{6,96},{7,112},{8,128},{9... | collective-permute-start | bytes 221192 | tf_op jit(solution)/shard_map/ppermute | solution.py:73
  30.4 0.7 fusion.26
  31.2 0.8 fusion.29
  32.0 1.5 %fusion.5 = f32[2304,128]{1,0:T(8,128)} fusion(bf16[2304,128]{1,0:T(8,128)(2,1)S(1)} %bitcast.180, bf16[2,128,128]{2,1,0:T(8,128)(2,1)S(1)} %copy-done.34), kind=kOutput, calls=%fused_computation.7 | convolution fusion | flops 76382208 | bytes 1802240 | tf_op jit(solution)/shard_map/dot_general | solution.py:26
  34.5 1.3 pad_maximum_fusion
  35.8 6.2 %all-to-all-start.1 = ((bf16[16,3,144,128]{3,2,1,0:T(8,128)(2,1)}), bf16[16,3,144,128]{3,2,1,0:T(8,128)(2,1)S(1)}, u32[]{:S(2)}, u32[]{:S(2)}) async-start(bf16[16,3,144,128]{3,2,1,0:T(8,128)(2,1)} %pad_maximum_fusion), calls=%async_computation.1 | async-start | bytes 3538944 | tf_op jit(solution)/shard_map/all_to_all | solution.py:148
  42.1 1.1 collective-permute-start.1
  43.2 6.2 %collective-permute-done.1 = bf16[2,3,96,128]{3,2,1,0:T(8,128)(2,1)S(1)} collective-permute-done((bf16[2,3,96,128]{3,2,1,0:T(8,128)(2,1)S(1)}, bf16[2,3,96,128]{3,2,1,0:T(8,128)(2,1)S(1)}, u32[]{:S(2)}, u32[]{:S(2)}) %collective-permute-start.1) | collective-permute-done | bytes 147488 | tf_op jit(solution)/shard_map/ppermute | solution.py:48
  49.4 5.6 %collective-permute-start.2 = (bf16[2,2,3,96,128]{4,3,2,0,1:T(8,128)(2,1)S(1)}, bf16[2,2,3,96,128]{4,3,2,0,1:T(8,128)(2,1)S(1)}, u32[]{:S(2)}, u32[]{:S(2)}) collective-permute-start(bf16[2,2,3,96,128]{4,3,2,0,1:T(8,128)(2,1)S(1)} %bitcast_dynamic-update-slice_fusion.8), channel_id=1, source_target_pairs={{0,8},{1,9},{2,10},{3,11},{4,12},{5,13},{6,14},{7,15},{8,0},{9,1},... | collective-permute-start | bytes 884744 | tf_op jit(solution)/shard_map/ppermute | solution.py:48
  55.1 0.9 collective-permute-start.3
  56.2 6.8 %collective-permute-done.2 = bf16[2,2,3,96,128]{4,3,2,0,1:T(8,128)(2,1)S(1)} collective-permute-done((bf16[2,2,3,96,128]{4,3,2,0,1:T(8,128)(2,1)S(1)}, bf16[2,2,3,96,128]{4,3,2,0,1:T(8,128)(2,1)S(1)}, u32[]{:S(2)}, u32[]{:S(2)}) %collective-permute-start.2) | collective-permute-done | bytes 294944 | tf_op jit(solution)/shard_map/ppermute | solution.py:48
  63.0 5.1 %collective-permute-done.3 = bf16[2,2,3,96,128]{4,3,2,0,1:T(8,128)(2,1)S(1)} collective-permute-done((bf16[2,2,3,96,128]{4,3,2,0,1:T(8,128)(2,1)S(1)}, bf16[2,2,3,96,128]{4,3,2,0,1:T(8,128)(2,1)S(1)}, u32[]{:S(2)}, u32[]{:S(2)}) %collective-permute-start.3) | collective-permute-done | bytes 294944 | tf_op jit(solution)/shard_map/ppermute | solution.py:48
  73.3 1.4 bitcast_dynamic-update-slice_fusion.1
  74.7 1.2 fusion.96
  75.9 0.8 copy.38
  76.7 0.8 copy.39
  77.5 8.3 %all-to-all-done.1 = bf16[16,3,144,128]{3,2,1,0:T(8,128)(2,1)S(1)} async-done(((bf16[16,3,144,128]{3,2,1,0:T(8,128)(2,1)}), bf16[16,3,144,128]{3,2,1,0:T(8,128)(2,1)S(1)}, u32[]{:S(2)}, u32[]{:S(2)}) %all-to-all-start.1) | async-done | bytes 1769504 | tf_op jit(solution)/shard_map/all_to_all | solution.py:148
  85.9 0.6 dynamic-slice_bitcast_fusion
  86.6 1.0 copy.40
  87.7 1.9 %fusion.99 = (f32[6,48]{1,0:T(8,128)S(1)}, f32[128,6,48]{2,1,0:T(8,128)S(1)}) fusion(bf16[48,96,128]{1,0,2:T(8,128)(2,1)S(1)} %copy.40, bf16[3,96,128]{1,0,2:T(4,128)(2,1)} %bitcast.182, bf16[3,96,128]{1,0,2:T(4,128)(2,1)S(1)} %bitcast.181), kind=kOutput, calls=%fused_computation.181 | convolution fusion | flops 7409376 | bytes 1475712 | tf_op jit(solution)/shard_map/ikh,jkh->hij/dot_general | solution.py:157
  92.0 7.0 %collective-permute-start.6 = (bf16[6,48,128]{2,1,0:T(8,128)(2,1)S(1)}, bf16[6,48,128]{2,1,0:T(8,128)(2,1)}, u32[]{:S(2)}, u32[]{:S(2)}) collective-permute-start(bf16[6,48,128]{2,1,0:T(8,128)(2,1)S(1)} %get-tuple-element.70), channel_id=1, source_target_pairs={{0,0},{1,16},{2,32},{3,48},{4,64},{5,80},{6,96},{7,112},{8,128},{9... | collective-permute-start | bytes 221192 | tf_op jit(solution)/shard_map/ppermute | solution.py:73
  99.1 1.2 broadcast_in_dim.23
  100.2 4.5 %all-to-all-start.2 = ((bf16[16,6,48,128]{3,2,1,0:T(8,128)(2,1)}), bf16[16,6,48,128]{3,2,1,0:T(8,128)(2,1)}, u32[]{:S(2)}, u32[]{:S(2)}) async-start(bf16[16,6,48,128]{3,2,1,0:T(8,128)(2,1)} %broadcast_in_dim.23), calls=%async_computation.2 | async-start | bytes 2359296 | tf_op jit(solution)/shard_map/all_to_all | solution.py:163
  104.8 1.5 %collective-permute-done.6 = bf16[6,48,128]{2,1,0:T(8,128)(2,1)} collective-permute-done((bf16[6,48,128]{2,1,0:T(8,128)(2,1)S(1)}, bf16[6,48,128]{2,1,0:T(8,128)(2,1)}, u32[]{:S(2)}, u32[]{:S(2)}) %collective-permute-start.6) | collective-permute-done | bytes 73760 | tf_op jit(solution)/shard_map/ppermute | solution.py:73
  106.3 4.2 %collective-permute-start.7 = (bf16[6,48,128]{2,1,0:T(8,128)(2,1)}, bf16[6,48,128]{2,1,0:T(8,128)(2,1)}, u32[]{:S(2)}, u32[]{:S(2)}) collective-permute-start(bf16[6,48,128]{2,1,0:T(8,128)(2,1)} %collective-permute-done.6), channel_id=1, source_target_pairs={{0,2},{1,3},{2,0},{3,1},{4,6},{5,7},{6,4},{7,5},{8,10},{9,11},{10,... | collective-permute-start | bytes 221192 | tf_op jit(solution)/shard_map/ppermute | solution.py:48
  110.5 0.9 bitcast_dynamic-update-slice_fusion.15
  111.4 1.8 %copy.42 = bf16[48,96,128]{1,0,2:T(8,128)(2,1)} copy(bf16[48,96,128]{2,1,0:T(8,128)(2,1)S(1)} %bitcast.174) | data formatting | bytes 2359296 | tf_op jit(solution)/shard_map/optimization_barrier | solution.py:169
  113.2 0.9 bitcast_dynamic-update-slice_fusion.14
  114.4 2.3 %collective-permute-start.9 = (bf16[2,6,48,128]{3,2,1,0:T(8,128)(2,1)S(1)}, bf16[2,6,48,128]{3,2,1,0:T(8,128)(2,1)S(1)}, u32[]{:S(2)}, u32[]{:S(2)}) collective-permute-start(bf16[2,6,48,128]{3,2,1,0:T(8,128)(2,1)S(1)} %bitcast_dynamic-update-slice_fusion.14), channel_id=1, source_target_pairs={{0,4},{1,5},{2,6},{3,7},{4,0},{5,1},{6,2},{7,3},{8,12},{9,13},{10,... | collective-permute-start | bytes 442376 | tf_op jit(solution)/shard_map/ppermute | solution.py:48
  116.7 1.8 %collective-permute-start.10 = (bf16[2,6,48,128]{3,2,1,0:T(8,128)(2,1)S(1)}, bf16[2,6,48,128]{3,2,1,0:T(8,128)(2,1)S(1)}, u32[]{:S(2)}, u32[]{:S(2)}) collective-permute-start(bf16[2,6,48,128]{3,2,1,0:T(8,128)(2,1)S(1)} %bitcast_dynamic-update-slice_fusion.14), channel_id=1, source_target_pairs={{0,12},{1,13},{2,14},{3,15},{4,8},{5,9},{6,10},{7,11},{8,4},{9,5},... | collective-permute-start | bytes 442376 | tf_op jit(solution)/shard_map/ppermute | solution.py:48
  118.5 2.3 %fusion.101 = (f32[48,48]{1,0:T(8,128)S(1)}, f32[128,48,48]{2,1,0:T(8,128)S(1)}) fusion(bf16[128,48,96]{2,1,0:T(8,128)(2,1)} %bitcast.171, bf16[48,96,128]{1,0,2:T(8,128)(2,1)S(1)} %copy.40), kind=kOutput, calls=%fused_computation.183 | convolution fusion | flops 56915712 | bytes 3548160 | tf_op jit(solution)/shard_map/hik,jkh->hij/dot_general | solution.py:166
  122.7 0.6 copy-done.3
  123.4 0.8 convert_reduce_fusion
  124.2 0.7 fusion.22
  125.6 0.8 fusion.25
  126.4 1.5 %fusion.2 = f32[2304,128]{1,0:T(8,128)} fusion(bf16[2304,128]{1,0:T(8,128)(2,1)S(1)} %bitcast.179, bf16[2,128,128]{2,1,0:T(8,128)(2,1)S(1)} %copy-done.36), kind=kOutput, calls=%fused_computation.3 | convolution fusion | flops 76382208 | bytes 1802240 | tf_op jit(solution)/shard_map/dot_general | solution.py:26
  128.0 1.0 copy-done.1
  129.0 2.4 %copy.47 = bf16[96,48,128]{0,1,2:T(8,128)(2,1)S(1)} copy(bf16[96,48,128]{2,1,0:T(8,128)(2,1)} %bitcast.172) | data formatting | bytes 2359296 | tf_op jit(solution)/shard_map/reshape;reshape | solution.py:172
  131.4 5.4 %all-to-all-done.2 = bf16[16,6,48,128]{3,2,1,0:T(8,128)(2,1)} async-done(((bf16[16,6,48,128]{3,2,1,0:T(8,128)(2,1)}), bf16[16,6,48,128]{3,2,1,0:T(8,128)(2,1)}, u32[]{:S(2)}, u32[]{:S(2)}) %all-to-all-start.2) | async-done | bytes 1179680 | tf_op jit(solution)/shard_map/all_to_all | solution.py:163
  136.8 3.1 %copy.48 = bf16[96,48,128]{0,1,2:T(8,128)(2,1)} copy(bf16[96,48,128]{2,1,0:T(8,128)(2,1)} %bitcast.75) | data formatting | bytes 2359296 | tf_op jit(solution)/shard_map/reshape | solution.py:163
  140.0 2.3 %fusion.102 = (f32[48,48]{1,0:T(8,128)S(1)}, f32[128,48,48]{2,1,0:T(8,128)S(1)}) fusion(bf16[96,48,128]{0,1,2:T(8,128)(2,1)S(1)} %copy.47, bf16[96,48,128]{0,1,2:T(8,128)(2,1)} %copy.48), kind=kOutput, calls=%fused_computation.184 | convolution fusion | flops 56915712 | bytes 3548160 | tf_op jit(solution)/shard_map/kih,kjh->hij/dot_general | solution.py:176
  143.6 0.7 copy-done.4
  144.3 1.4 fusion.19
  (162 shorter events, 10.8 us)
Async XLA Ops:
  0.0 30.0 %copy-start = (bf16[48,48,128]{2,1,0:T(8,128)(2,1)S(1)}, bf16[48,48,128]{2,1,0:T(8,128)(2,1)}, u32[]{:S(2)}) copy-start(bf16[48,48,128]{2,1,0:T(8,128)(2,1)} %param.11) | copy-start | bytes 1769476
  0.0 7.6 %copy-start.27 = (s32[2,2]{1,0:T(2,128)S(1)}, s32[2,2]{1,0:T(2,128)}, u32[]{:S(2)}) copy-start(s32[2,2]{1,0:T(2,128)} %param.13) | copy-start | bytes 52
  0.0 9.7 %copy-start.26 = (s32[768]{0:T(1024)S(1)}, s32[768]{0:T(1024)}, u32[]{:S(2)}) copy-start(s32[768]{0:T(1024)} %param.12) | copy-start | bytes 9220
  0.0 11.4 %copy-start.31 = (f32[2,128]{1,0:T(2,128)S(1)}, f32[2,128]{1,0:T(2,128)}, u32[]{:S(2)}) copy-start(f32[2,128]{1,0:T(2,128)} %param.14) | copy-start | bytes 3076
  0.0 11.4 %copy-start.30 = (f32[2,128]{1,0:T(2,128)S(1)}, f32[2,128]{1,0:T(2,128)}, u32[]{:S(2)}) copy-start(f32[2,128]{1,0:T(2,128)} %param.15) | copy-start | bytes 3076
  0.0 16.9 %copy-start.8 = (bf16[2,128,256]{2,1,0:T(8,128)(2,1)S(1)}, bf16[2,128,256]{2,1,0:T(8,128)(2,1)}, u32[]{:S(2)}) copy-start(bf16[2,128,256]{2,1,0:T(8,128)(2,1)} %param.16) | copy-start | bytes 393220
  0.0 16.9 %copy-start.11 = (bf16[2,128,256]{2,1,0:T(8,128)(2,1)S(1)}, bf16[2,128,256]{2,1,0:T(8,128)(2,1)}, u32[]{:S(2)}) copy-start(bf16[2,128,256]{2,1,0:T(8,128)(2,1)} %param.17) | copy-start | bytes 393220
  0.1 18.3 %all-to-all-start = ((bf16[16,3,48,128]{3,2,1,0:T(8,128)(2,1)}), bf16[16,3,48,128]{3,2,1,0:T(8,128)(2,1)S(1)}, u32[]{:S(2)}, u32[]{:S(2)}) async-start(bf16[16,3,48,128]{3,2,1,0:T(8,128)(2,1)} %bitcast.168), calls=%async_computation | async-start | bytes 1179648 | tf_op jit(solution)/shard_map/all_to_all | solution.py:131
  12.0 19.9 %copy-start.13 = (f32[128]{0:T(128)}, f32[128]{0:T(128)S(1)}, u32[]{:S(2)}) copy-start(f32[128]{0:T(128)S(1)} %get-tuple-element.87) | copy-start | bytes 1540
  12.0 19.9 %copy-start.15 = (f32[128]{0:T(128)}, f32[128]{0:T(128)S(1)}, u32[]{:S(2)}) copy-start(f32[128]{0:T(128)S(1)} %get-tuple-element.104) | copy-start | bytes 1540
  18.9 13.1 %copy-start.34 = (bf16[2,128,128]{2,1,0:T(8,128)(2,1)S(1)}, bf16[2,128,128]{2,1,0:T(8,128)(2,1)}, u32[]{:S(2)}) copy-start(bf16[2,128,128]{2,1,0:T(8,128)(2,1)} %param.21) | copy-start | bytes 196612
  18.9 15.0 %collective-permute-start = (bf16[3,96,128]{2,1,0:T(8,128)(2,1)S(1)}, bf16[3,96,128]{2,1,0:T(8,128)(2,1)S(1)}, u32[]{:S(2)}, u32[]{:S(2)}) collective-permute-start(bf16[3,96,128]{2,1,0:T(8,128)(2,1)S(1)} %fusion.68), channel_id=1, source_target_pairs={{0,0},{1,16},{2,32},{3,48},{4,64},{5,80},{6,96},{7,112},{8,128},{9... | collective-permute-start | bytes 221192 | tf_op jit(solution)/shard_map/ppermute | solution.py:73
  35.8 50.0 %all-to-all-start.1 = ((bf16[16,3,144,128]{3,2,1,0:T(8,128)(2,1)}), bf16[16,3,144,128]{3,2,1,0:T(8,128)(2,1)S(1)}, u32[]{:S(2)}, u32[]{:S(2)}) async-start(bf16[16,3,144,128]{3,2,1,0:T(8,128)(2,1)} %pad_maximum_fusion), calls=%async_computation.1 | async-start | bytes 3538944 | tf_op jit(solution)/shard_map/all_to_all | solution.py:148
  42.1 7.4 %collective-permute-start.1 = (bf16[2,3,96,128]{3,2,1,0:T(8,128)(2,1)S(1)}, bf16[2,3,96,128]{3,2,1,0:T(8,128)(2,1)S(1)}, u32[]{:S(2)}, u32[]{:S(2)}) collective-permute-start(bf16[2,3,96,128]{3,2,1,0:T(8,128)(2,1)S(1)} %pad_maximum_fusion.1), channel_id=1, source_target_pairs={{0,2},{1,3},{2,0},{3,1},{4,6},{5,7},{6,4},{7,5},{8,10},{9,11},{10,... | collective-permute-start | bytes 442376 | tf_op jit(solution)/shard_map/ppermute | solution.py:48
  49.4 13.6 %collective-permute-start.2 = (bf16[2,2,3,96,128]{4,3,2,0,1:T(8,128)(2,1)S(1)}, bf16[2,2,3,96,128]{4,3,2,0,1:T(8,128)(2,1)S(1)}, u32[]{:S(2)}, u32[]{:S(2)}) collective-permute-start(bf16[2,2,3,96,128]{4,3,2,0,1:T(8,128)(2,1)S(1)} %bitcast_dynamic-update-slice_fusion.8), channel_id=1, source_target_pairs={{0,8},{1,9},{2,10},{3,11},{4,12},{5,13},{6,14},{7,15},{8,0},{9,1},... | collective-permute-start | bytes 884744 | tf_op jit(solution)/shard_map/ppermute | solution.py:48
  55.1 13.1 %collective-permute-start.3 = (bf16[2,2,3,96,128]{4,3,2,0,1:T(8,128)(2,1)S(1)}, bf16[2,2,3,96,128]{4,3,2,0,1:T(8,128)(2,1)S(1)}, u32[]{:S(2)}, u32[]{:S(2)}) collective-permute-start(bf16[2,2,3,96,128]{4,3,2,0,1:T(8,128)(2,1)S(1)} %bitcast_dynamic-update-slice_fusion.8), channel_id=1, source_target_pairs={{0,4},{1,5},{2,6},{3,7},{4,0},{5,1},{6,2},{7,3},{8,12},{9,13},{10,... | collective-permute-start | bytes 884744 | tf_op jit(solution)/shard_map/ppermute | solution.py:48
  55.9 12.2 %collective-permute-start.4 = (bf16[2,2,3,96,128]{4,3,2,0,1:T(8,128)(2,1)S(1)}, bf16[2,2,3,96,128]{4,3,2,0,1:T(8,128)(2,1)S(1)}, u32[]{:S(2)}, u32[]{:S(2)}) collective-permute-start(bf16[2,2,3,96,128]{4,3,2,0,1:T(8,128)(2,1)S(1)} %bitcast_dynamic-update-slice_fusion.8), channel_id=1, source_target_pairs={{0,12},{1,13},{2,14},{3,15},{4,8},{5,9},{6,10},{7,11},{8,4},{9,5},... | collective-permute-start | bytes 884744 | tf_op jit(solution)/shard_map/ppermute | solution.py:48
  56.2 15.8 %copy-start.32 = (f32[2,128]{1,0:T(2,128)S(1)}, f32[2,128]{1,0:T(2,128)}, u32[]{:S(2)}) copy-start(f32[2,128]{1,0:T(2,128)} %param.19) | copy-start | bytes 3076
  56.2 15.8 %copy-start.33 = (f32[2,128]{1,0:T(2,128)S(1)}, f32[2,128]{1,0:T(2,128)}, u32[]{:S(2)}) copy-start(f32[2,128]{1,0:T(2,128)} %param.18) | copy-start | bytes 3076
  68.2 5.0 %collective-permute-start.5 = (bf16[4,2,2,3,96,128]{5,4,3,1,0,2:T(8,128)(2,1)S(1)}, bf16[4,2,2,3,96,128]{5,4,3,1,0,2:T(8,128)(2,1)}, u32[]{:S(2)}, u32[]{:S(2)}) collective-permute-start(bf16[4,2,2,3,96,128]{5,4,3,1,0,2:T(8,128)(2,1)S(1)} %bitcast_dynamic-update-slice_fusion.7), channel_id=1, source_target_pairs={{0,1},{1,0},{2,3},{3,2},{4,5},{5,4},{6,7},{7,6},{8,9},{9,8},{10,11... | collective-permute-start | bytes 3538952 | tf_op jit(solution)/shard_map/ppermute | solution.py:48
  86.6 1.0 copy-start.7
  87.6 2.1 %copy-start.5 = (bf16[3,48,128]{2,1,0:T(8,128)(2,1)S(1)}, bf16[3,48,128]{2,1,0:T(8,128)(2,1)}, u32[]{:S(2)}) copy-start(bf16[3,48,128]{2,1,0:T(8,128)(2,1)} %get-tuple-element.42) | copy-start | bytes 110596
  87.6 2.1 %copy-start.6 = (bf16[3,48,128]{2,1,0:T(8,128)(2,1)S(1)}, bf16[3,48,128]{2,1,0:T(8,128)(2,1)}, u32[]{:S(2)}) copy-start(bf16[3,48,128]{2,1,0:T(8,128)(2,1)} %get-tuple-element.41) | copy-start | bytes 110596
  87.6 2.4 %copy-start.14 = (f32[128]{0:T(128)S(1)}, f32[128]{0:T(128)}, u32[]{:S(2)}) copy-start(f32[128]{0:T(128)} %copy-done.13) | copy-start | bytes 1540
  87.7 2.4 %copy-start.16 = (f32[128]{0:T(128)S(1)}, f32[128]{0:T(128)}, u32[]{:S(2)}) copy-start(f32[128]{0:T(128)} %copy-done.15) | copy-start | bytes 1540
  87.7 2.6 %copy-start.35 = (bf16[2,128,128]{2,1,0:T(8,128)(2,1)S(1)}, bf16[2,128,128]{2,1,0:T(8,128)(2,1)}, u32[]{:S(2)}) copy-start(bf16[2,128,128]{2,1,0:T(8,128)(2,1)} %param.21) | copy-start | bytes 196612
  89.5 0.9 copy-start.22
  89.5 1.0 copy-start.24
  89.6 1.3 copy-start.10
  90.1 1.3 copy-start.18
  90.1 1.3 copy-start.20
  90.3 1.3 copy-start.12
  90.8 1.0 copy-start.9
  90.9 1.0 copy-start.17
  92.0 14.2 %collective-permute-start.6 = (bf16[6,48,128]{2,1,0:T(8,128)(2,1)S(1)}, bf16[6,48,128]{2,1,0:T(8,128)(2,1)}, u32[]{:S(2)}, u32[]{:S(2)}) collective-permute-start(bf16[6,48,128]{2,1,0:T(8,128)(2,1)S(1)} %get-tuple-element.70), channel_id=1, source_target_pairs={{0,0},{1,16},{2,32},{3,48},{4,64},{5,80},{6,96},{7,112},{8,128},{9... | collective-permute-start | bytes 221192 | tf_op jit(solution)/shard_map/ppermute | solution.py:73
  100.2 11.2 %copy-start.2 = (bf16[16,1,3,96,128]{4,3,2,0,1:T(8,128)(2,1)S(1)}, bf16[16,1,3,96,128]{4,3,2,0,1:T(8,128)(2,1)}, u32[]{:S(2)}) copy-start(bf16[16,1,3,96,128]{4,3,2,0,1:T(8,128)(2,1)} %get-tuple-element.61) | copy-start | bytes 3538948
  100.2 36.6 %all-to-all-start.2 = ((bf16[16,6,48,128]{3,2,1,0:T(8,128)(2,1)}), bf16[16,6,48,128]{3,2,1,0:T(8,128)(2,1)}, u32[]{:S(2)}, u32[]{:S(2)}) async-start(bf16[16,6,48,128]{3,2,1,0:T(8,128)(2,1)} %broadcast_in_dim.23), calls=%async_computation.2 | async-start | bytes 2359296 | tf_op jit(solution)/shard_map/all_to_all | solution.py:163
  106.3 6.9 %collective-permute-start.7 = (bf16[6,48,128]{2,1,0:T(8,128)(2,1)}, bf16[6,48,128]{2,1,0:T(8,128)(2,1)}, u32[]{:S(2)}, u32[]{:S(2)}) collective-permute-start(bf16[6,48,128]{2,1,0:T(8,128)(2,1)} %collective-permute-done.6), channel_id=1, source_target_pairs={{0,2},{1,3},{2,0},{3,1},{4,6},{5,7},{6,4},{7,5},{8,10},{9,11},{10,... | collective-permute-start | bytes 221192 | tf_op jit(solution)/shard_map/ppermute | solution.py:48
  114.1 8.1 %collective-permute-start.8 = (bf16[2,6,48,128]{3,2,1,0:T(8,128)(2,1)S(1)}, bf16[2,6,48,128]{3,2,1,0:T(8,128)(2,1)S(1)}, u32[]{:S(2)}, u32[]{:S(2)}) collective-permute-start(bf16[2,6,48,128]{3,2,1,0:T(8,128)(2,1)S(1)} %bitcast_dynamic-update-slice_fusion.14), channel_id=1, source_target_pairs={{0,8},{1,9},{2,10},{3,11},{4,12},{5,13},{6,14},{7,15},{8,0},{9,1},... | collective-permute-start | bytes 442376 | tf_op jit(solution)/shard_map/ppermute | solution.py:48
  114.4 7.9 %collective-permute-start.9 = (bf16[2,6,48,128]{3,2,1,0:T(8,128)(2,1)S(1)}, bf16[2,6,48,128]{3,2,1,0:T(8,128)(2,1)S(1)}, u32[]{:S(2)}, u32[]{:S(2)}) collective-permute-start(bf16[2,6,48,128]{3,2,1,0:T(8,128)(2,1)S(1)} %bitcast_dynamic-update-slice_fusion.14), channel_id=1, source_target_pairs={{0,4},{1,5},{2,6},{3,7},{4,0},{5,1},{6,2},{7,3},{8,12},{9,13},{10,... | collective-permute-start | bytes 442376 | tf_op jit(solution)/shard_map/ppermute | solution.py:48
  116.7 5.9 %collective-permute-start.10 = (bf16[2,6,48,128]{3,2,1,0:T(8,128)(2,1)S(1)}, bf16[2,6,48,128]{3,2,1,0:T(8,128)(2,1)S(1)}, u32[]{:S(2)}, u32[]{:S(2)}) collective-permute-start(bf16[2,6,48,128]{3,2,1,0:T(8,128)(2,1)S(1)} %bitcast_dynamic-update-slice_fusion.14), channel_id=1, source_target_pairs={{0,12},{1,13},{2,14},{3,15},{4,8},{5,9},{6,10},{7,11},{8,4},{9,5},... | collective-permute-start | bytes 442376 | tf_op jit(solution)/shard_map/ppermute | solution.py:48
  120.8 0.7 copy-start.23
  122.1 1.3 copy-start.3
  122.6 5.3 %collective-permute-start.11 = (bf16[4,2,6,48,128]{4,3,2,1,0:T(8,128)(2,1)S(1)}, bf16[4,2,6,48,128]{4,3,2,1,0:T(8,128)(2,1)S(1)}, u32[]{:S(2)}, u32[]{:S(2)}) collective-permute-start(bf16[4,2,6,48,128]{4,3,2,1,0:T(8,128)(2,1)S(1)} %bitcast_dynamic-update-slice_fusion.10), channel_id=1, source_target_pairs={{0,1},{1,0},{2,3},{3,2},{4,5},{5,4},{6,7},{7,6},{8,9},{9,8},{10,11... | collective-permute-start | bytes 1769480 | tf_op jit(solution)/shard_map/ppermute | solution.py:48
  124.9 0.7 copy-start.21
  125.1 1.3 copy-start.36
  128.0 1.0 copy-start.1
  143.0 1.3 copy-start.4
  (4 other events, 2.6 us)

commit v6 on v2

--- a/solution.py
+++ b/solution.py
@@ -138,18 +138,17 @@
     source, band = lax.optimization_barrier((pair_rep, band))
     gate = gate_of(norm_in(source, 0), 0)
     left_own = gate_project(band, band_keep, w_proj[0][:, :hidden], w_gate[0][:, :hidden])
-    moved, gate, left_own = lax.optimization_barrier((moved, gate, left_own))
+    tiles, left_own = lax.optimization_barrier((pair_rep, left_own))
+    shares = lax.all_to_all(tiles.reshape(n, part, tile, width), "row", 0, 0, tiled=True)
+    moved, gate, left_own, shares = lax.optimization_barrier((moved, gate, left_own, shares))
     gated = gate_project(moved, moved_keep, w_proj[0], w_gate[0])
     left_moved, right_moved = gated[..., :hidden], gated[..., hidden:]
 
-    rows = pair_rep.reshape(n, part, tile, width)
-    chunks = jnp.concatenate([jnp.broadcast_to(right_moved, (n,) + right_moved.shape), rows], axis=2)
+    chunks = jnp.broadcast_to(right_moved, (n,) + right_moved.shape)
     chunks, left_own = lax.optimization_barrier((chunks, left_own))
     chunks = lax.all_to_all(chunks, "row", 0, 0, tiled=True)
-    rows = pick(chunks[:, :, 2 * tile :], 1)
-    chunks, rows = lax.optimization_barrier((chunks, rows))
-    rows = jnp.concatenate(rows, axis=0)
-    right = chunks[:, :, : 2 * tile].reshape(tile, 2 * tile, hidden)
+    rows = jnp.concatenate(pick(shares, 1), axis=0)
+    right = chunks.reshape(tile, 2 * tile, hidden)
     lefts, _ = gather_col(jnp.stack([left_own, left_moved]), places)
     left = lefts[:, 0].reshape(tile, 2 * tile, hidden)
     left_rows = jnp.concatenate(pick(lefts[:, 1], 1), axis=0)

time: 145 us -> 150 us (1.034)
  the two profiles are of different devices: /device:TPU:4 before, /device:TPU:8 now
where the time goes in v6:
time: 150 us; the launch traced here: 149 us
  starting transfers between devices  52.8 us (35%)
  waiting for transfers between devices  48.3 us (32%)
  local copies, waits for them, and re-layouts  14.9 us (10%)
  other arithmetic  12.4 us (8%)
  between operations  10.6 us (7%)
  matrix products  9.68 us (6%)
    ppermute x10, waiting for transfers between devices, swap(): return lax.ppermute(x, axis, [(p, p ^ bits) for p in range(n)])  18 us
    ppermute x10, starting transfers between devices, swap(): return lax.ppermute(x, axis, [(p, p ^ bits) for p in range(n)])  13.8 us
    all_to_all x1, starting transfers between devices, body(): lax.all_to_all(copies, 'row', 0, 0, tiled=True)  13.5 us
    all_to_all x1, starting transfers between devices, body(): lax.all_to_all(tiles.reshape(n, part, tile, width), 'row', 0, 0, tiled=True)  9.95 us
    all_to_all x1, waiting for transfers between devices, body(): lax.all_to_all(tiles.reshape(n, part, tile, width), 'row', 0, 0, tiled=True)  9.78 us
    all_to_all x1, waiting for transfers between devices, body(): chunks = lax.all_to_all(chunks, 'row', 0, 0, tiled=True)  7.95 us
    all_to_all x1, waiting for transfers between devices, body(): lax.all_to_all(copies, 'row', 0, 0, tiled=True)  7.16 us
    all_to_all x1, starting transfers between devices, body(): lax.all_to_all(pair_rep.reshape(n, part, tile, width), 'col', 0, 0, tiled...  6.28 us
  transfers between devices with their start and end apart: 16, of which 12 were waited for; matrix products, arithmetic and copies ran while one was open for 16% of the time, Pallas kernels for 0%

profile of v6, /device:TPU:8, one launch (start us, length us, event | category | flops | bytes accessed | tf_op | source)
XLA Modules:
  0.0 148.7 jit_solution(16086909487335217082)
XLA Ops:
  0.0 6.3 %all-to-all-start = ((bf16[16,3,48,128]{3,2,1,0:T(8,128)(2,1)}), bf16[16,3,48,128]{3,2,1,0:T(8,128)(2,1)S(1)}, u32[]{:S(2)}, u32[]{:S(2)}) async-start(bf16[16,3,48,128]{3,2,1,0:T(8,128)(2,1)} %bitcast), calls=%async_computation | async-start | bytes 1179648 | tf_op jit(solution)/shard_map/all_to_all | solution.py:131
  6.3 0.6 fusion.99
  13.9 5.5 %all-to-all-done = bf16[16,3,48,128]{3,2,1,0:T(8,128)(2,1)S(1)} async-done(((bf16[16,3,48,128]{3,2,1,0:T(8,128)(2,1)}), bf16[16,3,48,128]{3,2,1,0:T(8,128)(2,1)S(1)}, u32[]{:S(2)}, u32[]{:S(2)}) %all-to-all-start) | async-done | bytes 589856 | tf_op jit(solution)/shard_map/all_to_all | solution.py:131
  19.9 1.9 %collective-permute-start = (bf16[3,96,128]{2,1,0:T(8,128)(2,1)S(1)}, bf16[3,96,128]{2,1,0:T(8,128)(2,1)S(1)}, u32[]{:S(2)}, u32[]{:S(2)}) collective-permute-start(bf16[3,96,128]{2,1,0:T(8,128)(2,1)S(1)} %fusion.69), channel_id=1, source_target_pairs={{0,0},{1,16},{2,32},{3,48},{4,64},{5,80},{6,96},{7,112},{8,128},{9... | collective-permute-start | bytes 221192 | tf_op jit(solution)/shard_map/ppermute | solution.py:73
  22.2 9.9 %all-to-all-start.1 = ((bf16[16,3,48,128]{3,2,1,0:T(8,128)(2,1)}), bf16[16,3,48,128]{3,2,1,0:T(8,128)(2,1)S(1)}, u32[]{:S(2)}, u32[]{:S(2)}) async-start(bf16[16,3,48,128]{3,2,1,0:T(8,128)(2,1)} %bitcast.22), calls=%async_computation.1 | async-start | bytes 1179648 | tf_op jit(solution)/shard_map/all_to_all | solution.py:142
  32.2 1.5 %convert_reduce_fusion.1 = f32[48,48]{1,0:T(8,128)S(1)} fusion(bf16[48,48,128]{2,1,0:T(8,128)(2,1)} %param.11), kind=kLoop, calls=%fused_computation.21 | loop fusion | flops 587520 | bytes 599040 | tf_op jit(solution)/shard_map/reduce_sum | solution.py:10
  33.7 1.8 %fusion.27 = f32[48,48]{1,0:T(8,128)S(1)} fusion(bf16[48,48,128]{2,1,0:T(8,128)(2,1)} %param.11, f32[48,48]{1,0:T(8,128)S(1)} %broadcast_multiply_fusion.3), kind=kLoop, calls=%fused_computation.33 | loop fusion | flops 1177344 | bytes 608256 | tf_op jit(solution)/shard_map/reduce_sum | solution.py:12
  35.5 1.8 %fusion.30 = bf16[48,48,128]{2,1,0:T(8,128)(2,1)S(1)} fusion(bf16[48,48,128]{2,1,0:T(8,128)(2,1)} %param.11, f32[128]{0:T(128)S(1)} %get-tuple-element.87, f32[128]{0:T(128)S(1)} %get-tuple-element.104, f32[48,48]{1,0:T(8,128)S(1)} %add_rsqrt_fusion.3, f32[48,48]{1,0:T(8,128)S(1)} %broadcast_multiply_fusion.3), kind=kLoop, calls=%fused_computation.36 | loop fusion | flops 1769472 | bytes 1199104 | tf_op jit(solution)/shard_map/convert_element_type | solution.py:104
  37.2 1.5 fusion.5
  38.7 9.8 %all-to-all-done.1 = bf16[16,3,48,128]{3,2,1,0:T(8,128)(2,1)S(1)} async-done(((bf16[16,3,48,128]{3,2,1,0:T(8,128)(2,1)}), bf16[16,3,48,128]{3,2,1,0:T(8,128)(2,1)S(1)}, u32[]{:S(2)}, u32[]{:S(2)}) %all-to-all-start.1) | async-done | bytes 589856 | tf_op jit(solution)/shard_map/all_to_all | solution.py:142
  49.0 1.2 broadcast_in_dim.21
  50.2 4.0 %collective-permute-start.1 = (bf16[2,3,96,128]{3,2,1,0:T(8,128)(2,1)S(1)}, bf16[2,3,96,128]{3,2,1,0:T(8,128)(2,1)S(1)}, u32[]{:S(2)}, u32[]{:S(2)}) collective-permute-start(bf16[2,3,96,128]{3,2,1,0:T(8,128)(2,1)S(1)} %pad_maximum_fusion.1), channel_id=1, source_target_pairs={{0,2},{1,3},{2,0},{3,1},{4,6},{5,7},{6,4},{7,5},{8,10},{9,11},{10,... | collective-permute-start | bytes 442376 | tf_op jit(solution)/shard_map/ppermute | solution.py:48
  57.9 5.5 %all-to-all-start.2 = ((bf16[16,3,96,128]{3,2,1,0:T(8,128)(2,1)}), bf16[16,3,96,128]{3,2,1,0:T(8,128)(2,1)S(1)}, u32[]{:S(2)}, u32[]{:S(2)}) async-start(bf16[16,3,96,128]{3,2,1,0:T(8,128)(2,1)} %broadcast_in_dim.21), calls=%async_computation.2 | async-start | bytes 2359296 | tf_op jit(solution)/shard_map/all_to_all | solution.py:149
  63.5 4.5 %collective-permute-start.2 = (bf16[2,2,3,96,128]{4,3,2,0,1:T(8,128)(2,1)S(1)}, bf16[2,2,3,96,128]{4,3,2,0,1:T(8,128)(2,1)S(1)}, u32[]{:S(2)}, u32[]{:S(2)}) collective-permute-start(bf16[2,2,3,96,128]{4,3,2,0,1:T(8,128)(2,1)S(1)} %bitcast_dynamic-update-slice_fusion.8), channel_id=1, source_target_pairs={{0,8},{1,9},{2,10},{3,11},{4,12},{5,13},{6,14},{7,15},{8,0},{9,1},... | collective-permute-start | bytes 884744 | tf_op jit(solution)/shard_map/ppermute | solution.py:48
  68.2 0.6 collective-permute-start.4
  69.0 6.9 %collective-permute-done.2 = bf16[2,2,3,96,128]{4,3,2,0,1:T(8,128)(2,1)S(1)} collective-permute-done((bf16[2,2,3,96,128]{4,3,2,0,1:T(8,128)(2,1)S(1)}, bf16[2,2,3,96,128]{4,3,2,0,1:T(8,128)(2,1)S(1)}, u32[]{:S(2)}, u32[]{:S(2)}) %collective-permute-start.2) | collective-permute-done | bytes 294944 | tf_op jit(solution)/shard_map/ppermute | solution.py:48
  75.9 3.1 %collective-permute-done.3 = bf16[2,2,3,96,128]{4,3,2,0,1:T(8,128)(2,1)S(1)} collective-permute-done((bf16[2,2,3,96,128]{4,3,2,0,1:T(8,128)(2,1)S(1)}, bf16[2,2,3,96,128]{4,3,2,0,1:T(8,128)(2,1)S(1)}, u32[]{:S(2)}, u32[]{:S(2)}) %collective-permute-start.3) | collective-permute-done | bytes 294944 | tf_op jit(solution)/shard_map/ppermute | solution.py:48
  79.9 0.5 broadcast_in_dim.18
  80.6 1.6 %collective-permute-done.5 = bf16[4,2,2,3,96,128]{5,4,3,1,0,2:T(8,128)(2,1)S(1)} collective-permute-done((bf16[4,2,2,3,96,128]{5,4,3,1,0,2:T(8,128)(2,1)S(1)}, bf16[4,2,2,3,96,128]{5,4,3,1,0,2:T(8,128)(2,1)S(1)}, u32[]{:S(2)}, u32[]{:S(2)}) %collective-permute-start.5) | collective-permute-done | bytes 1179680 | tf_op jit(solution)/shard_map/ppermute | solution.py:48
  82.3 1.2 fusion.97
  83.9 8.0 %all-to-all-done.2 = bf16[16,3,96,128]{3,2,1,0:T(8,128)(2,1)S(1)} async-done(((bf16[16,3,96,128]{3,2,1,0:T(8,128)(2,1)}), bf16[16,3,96,128]{3,2,1,0:T(8,128)(2,1)S(1)}, u32[]{:S(2)}, u32[]{:S(2)}) %all-to-all-start.2) | async-done | bytes 1179680 | tf_op jit(solution)/shard_map/all_to_all | solution.py:149
  91.8 1.0 copy.37
  92.8 0.9 fusion.100
  95.7 1.9 %collective-permute-start.6 = (bf16[6,48,128]{2,1,0:T(8,128)(2,1)S(1)}, bf16[6,48,128]{2,1,0:T(8,128)(2,1)S(1)}, u32[]{:S(2)}, u32[]{:S(2)}) collective-permute-start(bf16[6,48,128]{2,1,0:T(8,128)(2,1)S(1)} %get-tuple-element.70), channel_id=1, source_target_pairs={{0,0},{1,16},{2,32},{3,48},{4,64},{5,80},{6,96},{7,112},{8,128},{9... | collective-permute-start | bytes 221192 | tf_op jit(solution)/shard_map/ppermute | solution.py:73
  97.7 1.2 broadcast_in_dim.23
  98.8 13.5 %all-to-all-start.3 = ((bf16[16,6,48,128]{3,2,1,0:T(8,128)(2,1)}), bf16[16,6,48,128]{3,2,1,0:T(8,128)(2,1)}, u32[]{:S(2)}, u32[]{:S(2)}) async-start(bf16[16,6,48,128]{3,2,1,0:T(8,128)(2,1)} %broadcast_in_dim.23), calls=%async_computation.3 | async-start | bytes 2359296 | tf_op jit(solution)/shard_map/all_to_all | solution.py:162
  112.4 2.0 %copy.39 = bf16[48,96,128]{1,0,2:T(8,128)(2,1)S(1)} copy(bf16[48,96,128]{2,1,0:T(8,128)(2,1)} %bitcast.183) | data formatting | bytes 2359296 | tf_op jit(solution)/shard_map/optimization_barrier | solution.py:168
  114.4 3.9 %collective-permute-done.7 = bf16[6,48,128]{2,1,0:T(8,128)(2,1)S(1)} collective-permute-done((bf16[6,48,128]{2,1,0:T(8,128)(2,1)S(1)}, bf16[6,48,128]{2,1,0:T(8,128)(2,1)S(1)}, u32[]{:S(2)}, u32[]{:S(2)}) %collective-permute-start.7) | collective-permute-done | bytes 73760 | tf_op jit(solution)/shard_map/ppermute | solution.py:48
  118.7 2.3 %collective-permute-start.9 = (bf16[2,6,48,128]{3,2,1,0:T(8,128)(2,1)S(1)}, bf16[2,6,48,128]{3,2,1,0:T(8,128)(2,1)S(1)}, u32[]{:S(2)}, u32[]{:S(2)}) collective-permute-start(bf16[2,6,48,128]{3,2,1,0:T(8,128)(2,1)S(1)} %bitcast_dynamic-update-slice_fusion.14), channel_id=1, source_target_pairs={{0,4},{1,5},{2,6},{3,7},{4,0},{5,1},{6,2},{7,3},{8,12},{9,13},{10,... | collective-permute-start | bytes 442376 | tf_op jit(solution)/shard_map/ppermute | solution.py:48
  120.9 1.8 %collective-permute-start.10 = (bf16[2,6,48,128]{3,2,1,0:T(8,128)(2,1)S(1)}, bf16[2,6,48,128]{3,2,1,0:T(8,128)(2,1)S(1)}, u32[]{:S(2)}, u32[]{:S(2)}) collective-permute-start(bf16[2,6,48,128]{3,2,1,0:T(8,128)(2,1)S(1)} %bitcast_dynamic-update-slice_fusion.14), channel_id=1, source_target_pairs={{0,12},{1,13},{2,14},{3,15},{4,8},{5,9},{6,10},{7,11},{8,4},{9,5},... | collective-permute-start | bytes 442376 | tf_op jit(solution)/shard_map/ppermute | solution.py:48
  122.7 0.9 fusion.102
  123.7 0.5 multiply_reduce_fusion.1
  124.2 0.6 add_convert_fusion.1
  124.9 0.4 collective-permute-done.8
  125.6 1.6 %collective-permute-done.10 = bf16[2,6,48,128]{3,2,1,0:T(8,128)(2,1)S(1)} collective-permute-done((bf16[2,6,48,128]{3,2,1,0:T(8,128)(2,1)S(1)}, bf16[2,6,48,128]{3,2,1,0:T(8,128)(2,1)S(1)}, u32[]{:S(2)}, u32[]{:S(2)}) %collective-permute-start.10) | collective-permute-done | bytes 147488 | tf_op jit(solution)/shard_map/ppermute | solution.py:48
  127.4 1.9 %convert_reduce_fusion = (f32[48,48]{1,0:T(8,128)S(1)}, bf16[48,48,128]{2,1,0:T(8,128)(2,1)S(1)}) fusion(f32[48,48,128]{2,1,0:T(8,128)S(1)} %bitcast.184, bf16[2,128,128]{2,1,0:T(8,128)(2,1)S(1)} %copy-done.3, bf16[128,48,48]{2,1,0:T(8,128)(2,1)S(1)} %add_convert_fusion.1, bf16[48,48,128]{2,1,0:T(8,128)(2,1)} %param.11), kind=kOutput, calls=%fused_computation.15 | convolution fusion | flops 77264640 | bytes 3974144 | tf_op jit(solution)/shard_map/hij,hc->ijc/dot_general | solution.py:41
  129.3 0.7 fusion.23
  130.1 0.8 fusion.26
  130.9 0.5 fusion.2
  131.4 1.6 %pad_maximum_fusion = f32[2,48,48,128]{3,2,1,0:T(8,128)} fusion(f32[1,48,48,128]{3,2,1,0:T(8,128)S(1)} %convert_bitcast_fusion, f32[1,48,48,128]{3,2,1,0:T(8,128)S(1)} %bitcast.185), kind=kLoop, calls=%fused_computation.12 | loop fusion | flops 589824 | bytes 4718592 | tf_op jit(solution)/shard_map/stack | solution.py:174
  133.3 1.3 copy.44
  134.7 7.2 %all-to-all-done.3 = bf16[16,6,48,128]{3,2,1,0:T(8,128)(2,1)} async-done(((bf16[16,6,48,128]{3,2,1,0:T(8,128)(2,1)}), bf16[16,6,48,128]{3,2,1,0:T(8,128)(2,1)}, u32[]{:S(2)}, u32[]{:S(2)}) %all-to-all-start.3) | async-done | bytes 1179680 | tf_op jit(solution)/shard_map/all_to_all | solution.py:162
  141.8 2.4 %copy.45 = bf16[96,48,128]{0,1,2:T(8,128)(2,1)S(1)} copy(bf16[96,48,128]{2,1,0:T(8,128)(2,1)} %bitcast.81) | data formatting | bytes 2359296 | tf_op jit(solution)/shard_map/reshape | solution.py:162
  144.2 0.9 fusion.103
  145.2 0.5 multiply_reduce_fusion
  145.7 0.6 add_convert_fusion
  146.2 1.1 copy-done
  147.3 1.4 fusion.20
  (117 shorter events, 7.4 us)
Async XLA Ops:
  0.0 6.3 %copy-start.7 = (s32[2,2]{1,0:T(2,128)S(1)}, s32[2,2]{1,0:T(2,128)}, u32[]{:S(2)}) copy-start(s32[2,2]{1,0:T(2,128)} %param.13) | copy-start | bytes 52
  0.0 8.2 %copy-start.6 = (s32[768]{0:T(1024)S(1)}, s32[768]{0:T(1024)}, u32[]{:S(2)}) copy-start(s32[768]{0:T(1024)} %param.12) | copy-start | bytes 9220
  0.0 9.9 %copy-start.9 = (f32[2,128]{1,0:T(2,128)S(1)}, f32[2,128]{1,0:T(2,128)}, u32[]{:S(2)}) copy-start(f32[2,128]{1,0:T(2,128)} %param.14) | copy-start | bytes 3076
  0.0 9.9 %copy-start.8 = (f32[2,128]{1,0:T(2,128)S(1)}, f32[2,128]{1,0:T(2,128)}, u32[]{:S(2)}) copy-start(f32[2,128]{1,0:T(2,128)} %param.15) | copy-start | bytes 3076
  0.0 13.9 %copy-start.2 = (bf16[2,128,256]{2,1,0:T(8,128)(2,1)S(1)}, bf16[2,128,256]{2,1,0:T(8,128)(2,1)}, u32[]{:S(2)}) copy-start(bf16[2,128,256]{2,1,0:T(8,128)(2,1)} %param.16) | copy-start | bytes 393220
  0.0 13.9 %copy-start.4 = (bf16[2,128,256]{2,1,0:T(8,128)(2,1)S(1)}, bf16[2,128,256]{2,1,0:T(8,128)(2,1)}, u32[]{:S(2)}) copy-start(bf16[2,128,256]{2,1,0:T(8,128)(2,1)} %param.17) | copy-start | bytes 393220
  0.0 19.4 %all-to-all-start = ((bf16[16,3,48,128]{3,2,1,0:T(8,128)(2,1)}), bf16[16,3,48,128]{3,2,1,0:T(8,128)(2,1)S(1)}, u32[]{:S(2)}, u32[]{:S(2)}) async-start(bf16[16,3,48,128]{3,2,1,0:T(8,128)(2,1)} %bitcast), calls=%async_computation | async-start | bytes 1179648 | tf_op jit(solution)/shard_map/all_to_all | solution.py:131
  19.9 18.8 %collective-permute-start = (bf16[3,96,128]{2,1,0:T(8,128)(2,1)S(1)}, bf16[3,96,128]{2,1,0:T(8,128)(2,1)S(1)}, u32[]{:S(2)}, u32[]{:S(2)}) collective-permute-start(bf16[3,96,128]{2,1,0:T(8,128)(2,1)S(1)} %fusion.69), channel_id=1, source_target_pairs={{0,0},{1,16},{2,32},{3,48},{4,64},{5,80},{6,96},{7,112},{8,128},{9... | collective-permute-start | bytes 221192 | tf_op jit(solution)/shard_map/ppermute | solution.py:73
  22.2 26.3 %all-to-all-start.1 = ((bf16[16,3,48,128]{3,2,1,0:T(8,128)(2,1)}), bf16[16,3,48,128]{3,2,1,0:T(8,128)(2,1)S(1)}, u32[]{:S(2)}, u32[]{:S(2)}) async-start(bf16[16,3,48,128]{3,2,1,0:T(8,128)(2,1)} %bitcast.22), calls=%async_computation.1 | async-start | bytes 1179648 | tf_op jit(solution)/shard_map/all_to_all | solution.py:142
  32.2 5.1 %copy-start.12 = (bf16[2,128,128]{2,1,0:T(8,128)(2,1)S(1)}, bf16[2,128,128]{2,1,0:T(8,128)(2,1)}, u32[]{:S(2)}) copy-start(bf16[2,128,128]{2,1,0:T(8,128)(2,1)} %param.21) | copy-start | bytes 196612
  48.7 5.5 %copy-start.10 = (f32[2,128]{1,0:T(2,128)S(1)}, f32[2,128]{1,0:T(2,128)}, u32[]{:S(2)}) copy-start(f32[2,128]{1,0:T(2,128)} %param.19) | copy-start | bytes 3076
  48.8 5.5 %copy-start.11 = (f32[2,128]{1,0:T(2,128)S(1)}, f32[2,128]{1,0:T(2,128)}, u32[]{:S(2)}) copy-start(f32[2,128]{1,0:T(2,128)} %param.18) | copy-start | bytes 3076
  50.2 13.2 %collective-permute-start.1 = (bf16[2,3,96,128]{3,2,1,0:T(8,128)(2,1)S(1)}, bf16[2,3,96,128]{3,2,1,0:T(8,128)(2,1)S(1)}, u32[]{:S(2)}, u32[]{:S(2)}) collective-permute-start(bf16[2,3,96,128]{3,2,1,0:T(8,128)(2,1)S(1)} %pad_maximum_fusion.1), channel_id=1, source_target_pairs={{0,2},{1,3},{2,0},{3,1},{4,6},{5,7},{6,4},{7,5},{8,10},{9,11},{10,... | collective-permute-start | bytes 442376 | tf_op jit(solution)/shard_map/ppermute | solution.py:48
  57.9 33.9 %all-to-all-start.2 = ((bf16[16,3,96,128]{3,2,1,0:T(8,128)(2,1)}), bf16[16,3,96,128]{3,2,1,0:T(8,128)(2,1)S(1)}, u32[]{:S(2)}, u32[]{:S(2)}) async-start(bf16[16,3,96,128]{3,2,1,0:T(8,128)(2,1)} %broadcast_in_dim.21), calls=%async_computation.2 | async-start | bytes 2359296 | tf_op jit(solution)/shard_map/all_to_all | solution.py:149
  63.5 12.4 %collective-permute-start.2 = (bf16[2,2,3,96,128]{4,3,2,0,1:T(8,128)(2,1)S(1)}, bf16[2,2,3,96,128]{4,3,2,0,1:T(8,128)(2,1)S(1)}, u32[]{:S(2)}, u32[]{:S(2)}) collective-permute-start(bf16[2,2,3,96,128]{4,3,2,0,1:T(8,128)(2,1)S(1)} %bitcast_dynamic-update-slice_fusion.8), channel_id=1, source_target_pairs={{0,8},{1,9},{2,10},{3,11},{4,12},{5,13},{6,14},{7,15},{8,0},{9,1},... | collective-permute-start | bytes 884744 | tf_op jit(solution)/shard_map/ppermute | solution.py:48
  68.1 10.9 %collective-permute-start.3 = (bf16[2,2,3,96,128]{4,3,2,0,1:T(8,128)(2,1)S(1)}, bf16[2,2,3,96,128]{4,3,2,0,1:T(8,128)(2,1)S(1)}, u32[]{:S(2)}, u32[]{:S(2)}) collective-permute-start(bf16[2,2,3,96,128]{4,3,2,0,1:T(8,128)(2,1)S(1)} %bitcast_dynamic-update-slice_fusion.8), channel_id=1, source_target_pairs={{0,4},{1,5},{2,6},{3,7},{4,0},{5,1},{6,2},{7,3},{8,12},{9,13},{10,... | collective-permute-start | bytes 884744 | tf_op jit(solution)/shard_map/ppermute | solution.py:48
  68.2 11.0 %collective-permute-start.4 = (bf16[2,2,3,96,128]{4,3,2,0,1:T(8,128)(2,1)S(1)}, bf16[2,2,3,96,128]{4,3,2,0,1:T(8,128)(2,1)S(1)}, u32[]{:S(2)}, u32[]{:S(2)}) collective-permute-start(bf16[2,2,3,96,128]{4,3,2,0,1:T(8,128)(2,1)S(1)} %bitcast_dynamic-update-slice_fusion.8), channel_id=1, source_target_pairs={{0,12},{1,13},{2,14},{3,15},{4,8},{5,9},{6,10},{7,11},{8,4},{9,5},... | collective-permute-start | bytes 884744 | tf_op jit(solution)/shard_map/ppermute | solution.py:48
  79.2 2.9 %collective-permute-start.5 = (bf16[4,2,2,3,96,128]{5,4,3,1,0,2:T(8,128)(2,1)S(1)}, bf16[4,2,2,3,96,128]{5,4,3,1,0,2:T(8,128)(2,1)S(1)}, u32[]{:S(2)}, u32[]{:S(2)}) collective-permute-start(bf16[4,2,2,3,96,128]{5,4,3,1,0,2:T(8,128)(2,1)S(1)} %bitcast_dynamic-update-slice_fusion.7), channel_id=1, source_target_pairs={{0,1},{1,0},{2,3},{3,2},{4,5},{5,4},{6,7},{7,6},{8,9},{9,8},{10,11... | collective-permute-start | bytes 3538952 | tf_op jit(solution)/shard_map/ppermute | solution.py:48
  93.7 0.8 copy-start.3
  93.8 1.5 %copy-start.5 = (bf16[2,128,256]{2,1,0:T(8,128)(2,1)S(1)}, bf16[2,128,256]{2,1,0:T(8,128)(2,1)}, u32[]{:S(2)}) copy-start(bf16[2,128,256]{2,1,0:T(8,128)(2,1)} %param.17) | copy-start | bytes 393220
  95.7 16.6 %collective-permute-start.6 = (bf16[6,48,128]{2,1,0:T(8,128)(2,1)S(1)}, bf16[6,48,128]{2,1,0:T(8,128)(2,1)S(1)}, u32[]{:S(2)}, u32[]{:S(2)}) collective-permute-start(bf16[6,48,128]{2,1,0:T(8,128)(2,1)S(1)} %get-tuple-element.70), channel_id=1, source_target_pairs={{0,0},{1,16},{2,32},{3,48},{4,64},{5,80},{6,96},{7,112},{8,128},{9... | collective-permute-start | bytes 221192 | tf_op jit(solution)/shard_map/ppermute | solution.py:73
  98.8 43.0 %all-to-all-start.3 = ((bf16[16,6,48,128]{3,2,1,0:T(8,128)(2,1)}), bf16[16,6,48,128]{3,2,1,0:T(8,128)(2,1)}, u32[]{:S(2)}, u32[]{:S(2)}) async-start(bf16[16,6,48,128]{3,2,1,0:T(8,128)(2,1)} %broadcast_in_dim.23), calls=%async_computation.3 | async-start | bytes 2359296 | tf_op jit(solution)/shard_map/all_to_all | solution.py:162
  112.3 6.1 %collective-permute-start.7 = (bf16[6,48,128]{2,1,0:T(8,128)(2,1)S(1)}, bf16[6,48,128]{2,1,0:T(8,128)(2,1)S(1)}, u32[]{:S(2)}, u32[]{:S(2)}) collective-permute-start(bf16[6,48,128]{2,1,0:T(8,128)(2,1)S(1)} %collective-permute-done.6), channel_id=1, source_target_pairs={{0,2},{1,3},{2,0},{3,1},{4,6},{5,7},{6,4},{7,5},{8,10},{9,11},{10,... | collective-permute-start | bytes 221192 | tf_op jit(solution)/shard_map/ppermute | solution.py:48
  118.4 6.9 %collective-permute-start.8 = (bf16[2,6,48,128]{3,2,1,0:T(8,128)(2,1)S(1)}, bf16[2,6,48,128]{3,2,1,0:T(8,128)(2,1)S(1)}, u32[]{:S(2)}, u32[]{:S(2)}) collective-permute-start(bf16[2,6,48,128]{3,2,1,0:T(8,128)(2,1)S(1)} %bitcast_dynamic-update-slice_fusion.14), channel_id=1, source_target_pairs={{0,8},{1,9},{2,10},{3,11},{4,12},{5,13},{6,14},{7,15},{8,0},{9,1},... | collective-permute-start | bytes 442376 | tf_op jit(solution)/shard_map/ppermute | solution.py:48
  118.7 7.0 %collective-permute-start.9 = (bf16[2,6,48,128]{3,2,1,0:T(8,128)(2,1)S(1)}, bf16[2,6,48,128]{3,2,1,0:T(8,128)(2,1)S(1)}, u32[]{:S(2)}, u32[]{:S(2)}) collective-permute-start(bf16[2,6,48,128]{3,2,1,0:T(8,128)(2,1)S(1)} %bitcast_dynamic-update-slice_fusion.14), channel_id=1, source_target_pairs={{0,4},{1,5},{2,6},{3,7},{4,0},{5,1},{6,2},{7,3},{8,12},{9,13},{10,... | collective-permute-start | bytes 442376 | tf_op jit(solution)/shard_map/ppermute | solution.py:48
  120.9 6.4 %collective-permute-start.10 = (bf16[2,6,48,128]{3,2,1,0:T(8,128)(2,1)S(1)}, bf16[2,6,48,128]{3,2,1,0:T(8,128)(2,1)S(1)}, u32[]{:S(2)}, u32[]{:S(2)}) collective-permute-start(bf16[2,6,48,128]{3,2,1,0:T(8,128)(2,1)S(1)} %bitcast_dynamic-update-slice_fusion.14), channel_id=1, source_target_pairs={{0,12},{1,13},{2,14},{3,15},{4,8},{5,9},{6,10},{7,11},{8,4},{9,5},... | collective-permute-start | bytes 442376 | tf_op jit(solution)/shard_map/ppermute | solution.py:48
  124.8 2.6 %copy-start.1 = (f32[2304,128]{1,0:T(8,128)S(1)}, f32[2304,128]{1,0:T(8,128)}, u32[]{:S(2)}) copy-start(f32[2304,128]{1,0:T(8,128)} %fusion.5) | copy-start | bytes 3538948
  127.3 5.9 %collective-permute-start.11 = (bf16[4,2,6,48,128]{4,3,2,1,0:T(8,128)(2,1)S(1)}, bf16[4,2,6,48,128]{4,3,2,1,0:T(8,128)(2,1)S(1)}, u32[]{:S(2)}, u32[]{:S(2)}) collective-permute-start(bf16[4,2,6,48,128]{4,3,2,1,0:T(8,128)(2,1)S(1)} %bitcast_dynamic-update-slice_fusion.10), channel_id=1, source_target_pairs={{0,1},{1,0},{2,3},{3,2},{4,5},{5,4},{6,7},{7,6},{8,9},{9,8},{10,11... | collective-permute-start | bytes 1769480 | tf_op jit(solution)/shard_map/ppermute | solution.py:48
  129.3 1.5 %copy-start.13 = (bf16[2,128,128]{2,1,0:T(8,128)(2,1)S(1)}, bf16[2,128,128]{2,1,0:T(8,128)(2,1)}, u32[]{:S(2)}) copy-start(bf16[2,128,128]{2,1,0:T(8,128)(2,1)} %param.21) | copy-start | bytes 196612
  145.6 1.7 %copy-start = (f32[2,48,48,128]{3,2,1,0:T(8,128)S(1)}, f32[2,48,48,128]{3,2,1,0:T(8,128)}, u32[]{:S(2)}) copy-start(f32[2,48,48,128]{3,2,1,0:T(8,128)} %pad_maximum_fusion) | copy-start | bytes 7077892

commit v7 on v6

--- a/solution.py
+++ b/solution.py
@@ -96,7 +96,9 @@
 
     def pick(stacked, update):
         return [
-            lax.dynamic_index_in_dim(stacked, windows[update, slot], 0, keepdims=False)
+            lax.dynamic_index_in_dim(
+                stacked, windows[update, slot], 0, keepdims=False, allow_negative_indices=update == 0
+            )
             for slot in range(2)
         ]
 

time: 150 us -> 146 us (0.973)
  between operations: 10.6 us -> 6.99 us
  waiting for transfers between devices: 48.3 us -> 45.7 us
  local copies, waits for them, and re-layouts: 14.9 us -> 17.4 us
    all_to_all x1, waiting for transfers between devices: 7.95 us -> 6.19 us  [body(): chunks = lax.all_to_all(chunks, 'row', 0, 0, tiled=True)]
  transfers between devices with their start and end apart: 16 -> 16, of which waited for: 12 -> 12; matrix products, arithmetic and copies ran while one was open for 16% -> 18% of each run, Pallas kernels for 0% -> 0%
where the time goes in v7:
time: 146 us; the launch traced here: 145 us
  starting transfers between devices  52.8 us (36%)
  waiting for transfers between devices  45.7 us (31%)
  local copies, waits for them, and re-layouts  17.4 us (12%)
  other arithmetic  12.4 us (8%)
  matrix products  9.67 us (7%)
  between operations  6.99 us (5%)
    ppermute x10, waiting for transfers between devices, swap(): return lax.ppermute(x, axis, [(p, p ^ bits) for p in range(n)])  17.2 us
    ppermute x10, starting transfers between devices, swap(): return lax.ppermute(x, axis, [(p, p ^ bits) for p in range(n)])  13.8 us
    all_to_all x1, starting transfers between devices, body(): lax.all_to_all(copies, 'row', 0, 0, tiled=True)  13.5 us
    all_to_all x1, starting transfers between devices, body(): lax.all_to_all(tiles.reshape(n, part, tile, width), 'row', 0, 0, tiled=True)  9.95 us
    all_to_all x1, waiting for transfers between devices, body(): lax.all_to_all(tiles.reshape(n, part, tile, width), 'row', 0, 0, tiled=True)  9.78 us
    all_to_all x1, waiting for transfers between devices, body(): lax.all_to_all(copies, 'row', 0, 0, tiled=True)  7.15 us
    all_to_all x1, starting transfers between devices, body(): lax.all_to_all(pair_rep.reshape(n, part, tile, width), 'col', 0, 0, tiled...  6.28 us
    all_to_all x1, waiting for transfers between devices, body(): chunks = lax.all_to_all(chunks, 'row', 0, 0, tiled=True)  6.19 us
  transfers between devices with their start and end apart: 16, of which 12 were waited for; matrix products, arithmetic and copies ran while one was open for 18% of the time, Pallas kernels for 0%

profile of v7, /device:TPU:8, one launch (start us, length us, event | category | flops | bytes accessed | tf_op | source)
XLA Modules:
  0.0 145.1 jit_solution(17236986961492381895)
XLA Ops:
  0.0 6.3 %all-to-all-start = ((bf16[16,3,48,128]{3,2,1,0:T(8,128)(2,1)}), bf16[16,3,48,128]{3,2,1,0:T(8,128)(2,1)S(1)}, u32[]{:S(2)}, u32[]{:S(2)}) async-start(bf16[16,3,48,128]{3,2,1,0:T(8,128)(2,1)} %bitcast), calls=%async_computation | async-start | bytes 1179648 | tf_op jit(solution)/shard_map/all_to_all | solution.py:133
  6.3 0.6 fusion.99
  14.0 5.4 %all-to-all-done = bf16[16,3,48,128]{3,2,1,0:T(8,128)(2,1)S(1)} async-done(((bf16[16,3,48,128]{3,2,1,0:T(8,128)(2,1)}), bf16[16,3,48,128]{3,2,1,0:T(8,128)(2,1)S(1)}, u32[]{:S(2)}, u32[]{:S(2)}) %all-to-all-start) | async-done | bytes 589856 | tf_op jit(solution)/shard_map/all_to_all | solution.py:133
  19.9 1.9 %collective-permute-start = (bf16[3,96,128]{2,1,0:T(8,128)(2,1)S(1)}, bf16[3,96,128]{2,1,0:T(8,128)(2,1)S(1)}, u32[]{:S(2)}, u32[]{:S(2)}) collective-permute-start(bf16[3,96,128]{2,1,0:T(8,128)(2,1)S(1)} %fusion.69), channel_id=1, source_target_pairs={{0,0},{1,16},{2,32},{3,48},{4,64},{5,80},{6,96},{7,112},{8,128},{9... | collective-permute-start | bytes 221192 | tf_op jit(solution)/shard_map/ppermute | solution.py:73
  22.2 9.9 %all-to-all-start.1 = ((bf16[16,3,48,128]{3,2,1,0:T(8,128)(2,1)}), bf16[16,3,48,128]{3,2,1,0:T(8,128)(2,1)S(1)}, u32[]{:S(2)}, u32[]{:S(2)}) async-start(bf16[16,3,48,128]{3,2,1,0:T(8,128)(2,1)} %bitcast.22), calls=%async_computation.1 | async-start | bytes 1179648 | tf_op jit(solution)/shard_map/all_to_all | solution.py:144
  32.2 1.5 %convert_reduce_fusion.1 = f32[48,48]{1,0:T(8,128)S(1)} fusion(bf16[48,48,128]{2,1,0:T(8,128)(2,1)} %param.11), kind=kLoop, calls=%fused_computation.21 | loop fusion | flops 587520 | bytes 599040 | tf_op jit(solution)/shard_map/reduce_sum | solution.py:10
  33.7 1.8 %fusion.27 = f32[48,48]{1,0:T(8,128)S(1)} fusion(bf16[48,48,128]{2,1,0:T(8,128)(2,1)} %param.11, f32[48,48]{1,0:T(8,128)S(1)} %broadcast_multiply_fusion.3), kind=kLoop, calls=%fused_computation.33 | loop fusion | flops 1177344 | bytes 608256 | tf_op jit(solution)/shard_map/reduce_sum | solution.py:12
  35.5 1.8 %fusion.30 = bf16[48,48,128]{2,1,0:T(8,128)(2,1)S(1)} fusion(bf16[48,48,128]{2,1,0:T(8,128)(2,1)} %param.11, f32[128]{0:T(128)S(1)} %get-tuple-element.87, f32[128]{0:T(128)S(1)} %get-tuple-element.104, f32[48,48]{1,0:T(8,128)S(1)} %add_rsqrt_fusion.3, f32[48,48]{1,0:T(8,128)S(1)} %broadcast_multiply_fusion.3), kind=kLoop, calls=%fused_computation.36 | loop fusion | flops 1769472 | bytes 1199104 | tf_op jit(solution)/shard_map/convert_element_type | solution.py:106
  37.2 1.5 %fusion.5 = f32[2304,128]{1,0:T(8,128)} fusion(bf16[2304,128]{1,0:T(8,128)(2,1)S(1)} %bitcast.189, bf16[2,128,128]{2,1,0:T(8,128)(2,1)S(1)} %copy-done.12), kind=kOutput, calls=%fused_computation.7 | convolution fusion | flops 76382208 | bytes 1802240 | tf_op jit(solution)/shard_map/dot_general | solution.py:26
  38.7 9.8 %all-to-all-done.1 = bf16[16,3,48,128]{3,2,1,0:T(8,128)(2,1)S(1)} async-done(((bf16[16,3,48,128]{3,2,1,0:T(8,128)(2,1)}), bf16[16,3,48,128]{3,2,1,0:T(8,128)(2,1)S(1)}, u32[]{:S(2)}, u32[]{:S(2)}) %all-to-all-start.1) | async-done | bytes 589856 | tf_op jit(solution)/shard_map/all_to_all | solution.py:144
  49.0 1.2 broadcast_in_dim.21
  50.2 4.0 %collective-permute-start.1 = (bf16[2,3,96,128]{3,2,1,0:T(8,128)(2,1)S(1)}, bf16[2,3,96,128]{3,2,1,0:T(8,128)(2,1)S(1)}, u32[]{:S(2)}, u32[]{:S(2)}) collective-permute-start(bf16[2,3,96,128]{3,2,1,0:T(8,128)(2,1)S(1)} %pad_maximum_fusion.1), channel_id=1, source_target_pairs={{0,2},{1,3},{2,0},{3,1},{4,6},{5,7},{6,4},{7,5},{8,10},{9,11},{10,... | collective-permute-start | bytes 442376 | tf_op jit(solution)/shard_map/ppermute | solution.py:48
  54.2 5.5 %all-to-all-start.2 = ((bf16[16,3,96,128]{3,2,1,0:T(8,128)(2,1)}), bf16[16,3,96,128]{3,2,1,0:T(8,128)(2,1)S(1)}, u32[]{:S(2)}, u32[]{:S(2)}) async-start(bf16[16,3,96,128]{3,2,1,0:T(8,128)(2,1)} %broadcast_in_dim.21), calls=%async_computation.2 | async-start | bytes 2359296 | tf_op jit(solution)/shard_map/all_to_all | solution.py:151
  59.8 4.5 %collective-permute-start.2 = (bf16[2,2,3,96,128]{4,3,2,0,1:T(8,128)(2,1)S(1)}, bf16[2,2,3,96,128]{4,3,2,0,1:T(8,128)(2,1)S(1)}, u32[]{:S(2)}, u32[]{:S(2)}) collective-permute-start(bf16[2,2,3,96,128]{4,3,2,0,1:T(8,128)(2,1)S(1)} %bitcast_dynamic-update-slice_fusion.8), channel_id=1, source_target_pairs={{0,8},{1,9},{2,10},{3,11},{4,12},{5,13},{6,14},{7,15},{8,0},{9,1},... | collective-permute-start | bytes 884744 | tf_op jit(solution)/shard_map/ppermute | solution.py:48
  64.3 1.3 dynamic-slice_bitcast_fusion.1
  65.8 0.6 collective-permute-start.4
  66.7 5.6 %collective-permute-done.2 = bf16[2,2,3,96,128]{4,3,2,0,1:T(8,128)(2,1)S(1)} collective-permute-done((bf16[2,2,3,96,128]{4,3,2,0,1:T(8,128)(2,1)S(1)}, bf16[2,2,3,96,128]{4,3,2,0,1:T(8,128)(2,1)S(1)}, u32[]{:S(2)}, u32[]{:S(2)}) %collective-permute-start.2) | collective-permute-done | bytes 294944 | tf_op jit(solution)/shard_map/ppermute | solution.py:48
  72.3 3.1 %collective-permute-done.3 = bf16[2,2,3,96,128]{4,3,2,0,1:T(8,128)(2,1)S(1)} collective-permute-done((bf16[2,2,3,96,128]{4,3,2,0,1:T(8,128)(2,1)S(1)}, bf16[2,2,3,96,128]{4,3,2,0,1:T(8,128)(2,1)S(1)}, u32[]{:S(2)}, u32[]{:S(2)}) %collective-permute-start.3) | collective-permute-done | bytes 294944 | tf_op jit(solution)/shard_map/ppermute | solution.py:48
  75.4 0.6 collective-permute-done.4
  76.8 0.5 broadcast_in_dim.18
  77.4 1.6 %collective-permute-done.5 = bf16[4,2,2,3,96,128]{5,4,3,1,0,2:T(8,128)(2,1)S(1)} collective-permute-done((bf16[4,2,2,3,96,128]{5,4,3,1,0,2:T(8,128)(2,1)S(1)}, bf16[4,2,2,3,96,128]{5,4,3,1,0,2:T(8,128)(2,1)S(1)}, u32[]{:S(2)}, u32[]{:S(2)}) %collective-permute-start.5) | collective-permute-done | bytes 1179680 | tf_op jit(solution)/shard_map/ppermute | solution.py:48
  79.2 1.2 fusion.97
  80.4 1.3 constant_dynamic-slice_fusion.4
  82.0 6.2 %all-to-all-done.2 = bf16[16,3,96,128]{3,2,1,0:T(8,128)(2,1)S(1)} async-done(((bf16[16,3,96,128]{3,2,1,0:T(8,128)(2,1)}), bf16[16,3,96,128]{3,2,1,0:T(8,128)(2,1)S(1)}, u32[]{:S(2)}, u32[]{:S(2)}) %all-to-all-start.2) | async-done | bytes 1179680 | tf_op jit(solution)/shard_map/all_to_all | solution.py:151
  88.2 1.0 copy.37
  89.2 0.9 fusion.100
  92.1 1.9 %collective-permute-start.6 = (bf16[6,48,128]{2,1,0:T(8,128)(2,1)S(1)}, bf16[6,48,128]{2,1,0:T(8,128)(2,1)S(1)}, u32[]{:S(2)}, u32[]{:S(2)}) collective-permute-start(bf16[6,48,128]{2,1,0:T(8,128)(2,1)S(1)} %get-tuple-element.70), channel_id=1, source_target_pairs={{0,0},{1,16},{2,32},{3,48},{4,64},{5,80},{6,96},{7,112},{8,128},{9... | collective-permute-start | bytes 221192 | tf_op jit(solution)/shard_map/ppermute | solution.py:73
  94.0 1.2 broadcast_in_dim.23
  95.2 13.5 %all-to-all-start.3 = ((bf16[16,6,48,128]{3,2,1,0:T(8,128)(2,1)}), bf16[16,6,48,128]{3,2,1,0:T(8,128)(2,1)}, u32[]{:S(2)}, u32[]{:S(2)}) async-start(bf16[16,6,48,128]{3,2,1,0:T(8,128)(2,1)} %broadcast_in_dim.23), calls=%async_computation.3 | async-start | bytes 2359296 | tf_op jit(solution)/shard_map/all_to_all | solution.py:164
  108.8 2.0 %copy.39 = bf16[48,96,128]{1,0,2:T(8,128)(2,1)S(1)} copy(bf16[48,96,128]{2,1,0:T(8,128)(2,1)} %bitcast.183) | data formatting | bytes 2359296 | tf_op jit(solution)/shard_map/optimization_barrier | solution.py:170
  110.8 3.9 %collective-permute-done.7 = bf16[6,48,128]{2,1,0:T(8,128)(2,1)S(1)} collective-permute-done((bf16[6,48,128]{2,1,0:T(8,128)(2,1)S(1)}, bf16[6,48,128]{2,1,0:T(8,128)(2,1)S(1)}, u32[]{:S(2)}, u32[]{:S(2)}) %collective-permute-start.7) | collective-permute-done | bytes 73760 | tf_op jit(solution)/shard_map/ppermute | solution.py:48
  115.0 2.3 %collective-permute-start.9 = (bf16[2,6,48,128]{3,2,1,0:T(8,128)(2,1)S(1)}, bf16[2,6,48,128]{3,2,1,0:T(8,128)(2,1)S(1)}, u32[]{:S(2)}, u32[]{:S(2)}) collective-permute-start(bf16[2,6,48,128]{3,2,1,0:T(8,128)(2,1)S(1)} %bitcast_dynamic-update-slice_fusion.14), channel_id=1, source_target_pairs={{0,4},{1,5},{2,6},{3,7},{4,0},{5,1},{6,2},{7,3},{8,12},{9,13},{10,... | collective-permute-start | bytes 442376 | tf_op jit(solution)/shard_map/ppermute | solution.py:48
  117.3 1.8 %collective-permute-start.10 = (bf16[2,6,48,128]{3,2,1,0:T(8,128)(2,1)S(1)}, bf16[2,6,48,128]{3,2,1,0:T(8,128)(2,1)S(1)}, u32[]{:S(2)}, u32[]{:S(2)}) collective-permute-start(bf16[2,6,48,128]{3,2,1,0:T(8,128)(2,1)S(1)} %bitcast_dynamic-update-slice_fusion.14), channel_id=1, source_target_pairs={{0,12},{1,13},{2,14},{3,15},{4,8},{5,9},{6,10},{7,11},{8,4},{9,5},... | collective-permute-start | bytes 442376 | tf_op jit(solution)/shard_map/ppermute | solution.py:48
  119.1 0.9 fusion.102
  120.0 0.5 multiply_reduce_fusion.1
  120.5 0.6 add_convert_fusion.1
  122.0 1.6 %collective-permute-done.10 = bf16[2,6,48,128]{3,2,1,0:T(8,128)(2,1)S(1)} collective-permute-done((bf16[2,6,48,128]{3,2,1,0:T(8,128)(2,1)S(1)}, bf16[2,6,48,128]{3,2,1,0:T(8,128)(2,1)S(1)}, u32[]{:S(2)}, u32[]{:S(2)}) %collective-permute-start.10) | collective-permute-done | bytes 147488 | tf_op jit(solution)/shard_map/ppermute | solution.py:48
  123.8 1.9 %convert_reduce_fusion = (f32[48,48]{1,0:T(8,128)S(1)}, bf16[48,48,128]{2,1,0:T(8,128)(2,1)S(1)}) fusion(f32[48,48,128]{2,1,0:T(8,128)S(1)} %bitcast.184, bf16[2,128,128]{2,1,0:T(8,128)(2,1)S(1)} %copy-done.3, bf16[128,48,48]{2,1,0:T(8,128)(2,1)S(1)} %add_convert_fusion.1, bf16[48,48,128]{2,1,0:T(8,128)(2,1)} %param.11), kind=kOutput, calls=%fused_computation.15 | convolution fusion | flops 77264640 | bytes 3974144 | tf_op jit(solution)/shard_map/hij,hc->ijc/dot_general | solution.py:41
  125.7 0.7 fusion.23
  126.4 0.8 fusion.26
  127.8 1.6 %pad_maximum_fusion = f32[2,48,48,128]{3,2,1,0:T(8,128)} fusion(f32[1,48,48,128]{3,2,1,0:T(8,128)S(1)} %convert_bitcast_fusion, f32[1,48,48,128]{3,2,1,0:T(8,128)S(1)} %bitcast.185), kind=kLoop, calls=%fused_computation.12 | loop fusion | flops 589824 | bytes 4718592 | tf_op jit(solution)/shard_map/stack | solution.py:176
  129.7 1.3 copy.44
  131.0 7.2 %all-to-all-done.3 = bf16[16,6,48,128]{3,2,1,0:T(8,128)(2,1)} async-done(((bf16[16,6,48,128]{3,2,1,0:T(8,128)(2,1)}), bf16[16,6,48,128]{3,2,1,0:T(8,128)(2,1)}, u32[]{:S(2)}, u32[]{:S(2)}) %all-to-all-start.3) | async-done | bytes 1179680 | tf_op jit(solution)/shard_map/all_to_all | solution.py:164
  138.2 2.4 %copy.45 = bf16[96,48,128]{0,1,2:T(8,128)(2,1)S(1)} copy(bf16[96,48,128]{2,1,0:T(8,128)(2,1)} %bitcast.81) | data formatting | bytes 2359296 | tf_op jit(solution)/shard_map/reshape | solution.py:164
  140.6 0.9 fusion.103
  142.0 0.6 add_convert_fusion
  142.6 1.1 copy-done
  143.7 1.4 fusion.20
  (117 shorter events, 8.6 us)
Async XLA Ops:
  0.0 6.3 %copy-start.7 = (s32[2,2]{1,0:T(2,128)S(1)}, s32[2,2]{1,0:T(2,128)}, u32[]{:S(2)}) copy-start(s32[2,2]{1,0:T(2,128)} %param.13) | copy-start | bytes 52
  0.0 8.2 %copy-start.6 = (s32[768]{0:T(1024)S(1)}, s32[768]{0:T(1024)}, u32[]{:S(2)}) copy-start(s32[768]{0:T(1024)} %param.12) | copy-start | bytes 9220
  0.0 10.0 %copy-start.9 = (f32[2,128]{1,0:T(2,128)S(1)}, f32[2,128]{1,0:T(2,128)}, u32[]{:S(2)}) copy-start(f32[2,128]{1,0:T(2,128)} %param.14) | copy-start | bytes 3076
  0.0 10.0 %copy-start.8 = (f32[2,128]{1,0:T(2,128)S(1)}, f32[2,128]{1,0:T(2,128)}, u32[]{:S(2)}) copy-start(f32[2,128]{1,0:T(2,128)} %param.15) | copy-start | bytes 3076
  0.0 13.9 %copy-start.2 = (bf16[2,128,256]{2,1,0:T(8,128)(2,1)S(1)}, bf16[2,128,256]{2,1,0:T(8,128)(2,1)}, u32[]{:S(2)}) copy-start(bf16[2,128,256]{2,1,0:T(8,128)(2,1)} %param.16) | copy-start | bytes 393220
  0.0 13.9 %copy-start.4 = (bf16[2,128,256]{2,1,0:T(8,128)(2,1)S(1)}, bf16[2,128,256]{2,1,0:T(8,128)(2,1)}, u32[]{:S(2)}) copy-start(bf16[2,128,256]{2,1,0:T(8,128)(2,1)} %param.17) | copy-start | bytes 393220
  0.0 19.4 %all-to-all-start = ((bf16[16,3,48,128]{3,2,1,0:T(8,128)(2,1)}), bf16[16,3,48,128]{3,2,1,0:T(8,128)(2,1)S(1)}, u32[]{:S(2)}, u32[]{:S(2)}) async-start(bf16[16,3,48,128]{3,2,1,0:T(8,128)(2,1)} %bitcast), calls=%async_computation | async-start | bytes 1179648 | tf_op jit(solution)/shard_map/all_to_all | solution.py:133
  19.9 18.8 %collective-permute-start = (bf16[3,96,128]{2,1,0:T(8,128)(2,1)S(1)}, bf16[3,96,128]{2,1,0:T(8,128)(2,1)S(1)}, u32[]{:S(2)}, u32[]{:S(2)}) collective-permute-start(bf16[3,96,128]{2,1,0:T(8,128)(2,1)S(1)} %fusion.69), channel_id=1, source_target_pairs={{0,0},{1,16},{2,32},{3,48},{4,64},{5,80},{6,96},{7,112},{8,128},{9... | collective-permute-start | bytes 221192 | tf_op jit(solution)/shard_map/ppermute | solution.py:73
  22.2 26.3 %all-to-all-start.1 = ((bf16[16,3,48,128]{3,2,1,0:T(8,128)(2,1)}), bf16[16,3,48,128]{3,2,1,0:T(8,128)(2,1)S(1)}, u32[]{:S(2)}, u32[]{:S(2)}) async-start(bf16[16,3,48,128]{3,2,1,0:T(8,128)(2,1)} %bitcast.22), calls=%async_computation.1 | async-start | bytes 1179648 | tf_op jit(solution)/shard_map/all_to_all | solution.py:144
  32.2 5.1 %copy-start.12 = (bf16[2,128,128]{2,1,0:T(8,128)(2,1)S(1)}, bf16[2,128,128]{2,1,0:T(8,128)(2,1)}, u32[]{:S(2)}) copy-start(bf16[2,128,128]{2,1,0:T(8,128)(2,1)} %param.21) | copy-start | bytes 196612
  48.7 5.5 %copy-start.10 = (f32[2,128]{1,0:T(2,128)S(1)}, f32[2,128]{1,0:T(2,128)}, u32[]{:S(2)}) copy-start(f32[2,128]{1,0:T(2,128)} %param.19) | copy-start | bytes 3076
  48.8 5.5 %copy-start.11 = (f32[2,128]{1,0:T(2,128)S(1)}, f32[2,128]{1,0:T(2,128)}, u32[]{:S(2)}) copy-start(f32[2,128]{1,0:T(2,128)} %param.18) | copy-start | bytes 3076
  50.2 9.6 %collective-permute-start.1 = (bf16[2,3,96,128]{3,2,1,0:T(8,128)(2,1)S(1)}, bf16[2,3,96,128]{3,2,1,0:T(8,128)(2,1)S(1)}, u32[]{:S(2)}, u32[]{:S(2)}) collective-permute-start(bf16[2,3,96,128]{3,2,1,0:T(8,128)(2,1)S(1)} %pad_maximum_fusion.1), channel_id=1, source_target_pairs={{0,2},{1,3},{2,0},{3,1},{4,6},{5,7},{6,4},{7,5},{8,10},{9,11},{10,... | collective-permute-start | bytes 442376 | tf_op jit(solution)/shard_map/ppermute | solution.py:48
  54.2 33.9 %all-to-all-start.2 = ((bf16[16,3,96,128]{3,2,1,0:T(8,128)(2,1)}), bf16[16,3,96,128]{3,2,1,0:T(8,128)(2,1)S(1)}, u32[]{:S(2)}, u32[]{:S(2)}) async-start(bf16[16,3,96,128]{3,2,1,0:T(8,128)(2,1)} %broadcast_in_dim.21), calls=%async_computation.2 | async-start | bytes 2359296 | tf_op jit(solution)/shard_map/all_to_all | solution.py:151
  59.8 12.4 %collective-permute-start.2 = (bf16[2,2,3,96,128]{4,3,2,0,1:T(8,128)(2,1)S(1)}, bf16[2,2,3,96,128]{4,3,2,0,1:T(8,128)(2,1)S(1)}, u32[]{:S(2)}, u32[]{:S(2)}) collective-permute-start(bf16[2,2,3,96,128]{4,3,2,0,1:T(8,128)(2,1)S(1)} %bitcast_dynamic-update-slice_fusion.8), channel_id=1, source_target_pairs={{0,8},{1,9},{2,10},{3,11},{4,12},{5,13},{6,14},{7,15},{8,0},{9,1},... | collective-permute-start | bytes 884744 | tf_op jit(solution)/shard_map/ppermute | solution.py:48
  65.7 9.6 %collective-permute-start.3 = (bf16[2,2,3,96,128]{4,3,2,0,1:T(8,128)(2,1)S(1)}, bf16[2,2,3,96,128]{4,3,2,0,1:T(8,128)(2,1)S(1)}, u32[]{:S(2)}, u32[]{:S(2)}) collective-permute-start(bf16[2,2,3,96,128]{4,3,2,0,1:T(8,128)(2,1)S(1)} %bitcast_dynamic-update-slice_fusion.8), channel_id=1, source_target_pairs={{0,4},{1,5},{2,6},{3,7},{4,0},{5,1},{6,2},{7,3},{8,12},{9,13},{10,... | collective-permute-start | bytes 884744 | tf_op jit(solution)/shard_map/ppermute | solution.py:48
  65.8 10.2 %collective-permute-start.4 = (bf16[2,2,3,96,128]{4,3,2,0,1:T(8,128)(2,1)S(1)}, bf16[2,2,3,96,128]{4,3,2,0,1:T(8,128)(2,1)S(1)}, u32[]{:S(2)}, u32[]{:S(2)}) collective-permute-start(bf16[2,2,3,96,128]{4,3,2,0,1:T(8,128)(2,1)S(1)} %bitcast_dynamic-update-slice_fusion.8), channel_id=1, source_target_pairs={{0,12},{1,13},{2,14},{3,15},{4,8},{5,9},{6,10},{7,11},{8,4},{9,5},... | collective-permute-start | bytes 884744 | tf_op jit(solution)/shard_map/ppermute | solution.py:48
  76.1 2.9 %collective-permute-start.5 = (bf16[4,2,2,3,96,128]{5,4,3,1,0,2:T(8,128)(2,1)S(1)}, bf16[4,2,2,3,96,128]{5,4,3,1,0,2:T(8,128)(2,1)S(1)}, u32[]{:S(2)}, u32[]{:S(2)}) collective-permute-start(bf16[4,2,2,3,96,128]{5,4,3,1,0,2:T(8,128)(2,1)S(1)} %bitcast_dynamic-update-slice_fusion.7), channel_id=1, source_target_pairs={{0,1},{1,0},{2,3},{3,2},{4,5},{5,4},{6,7},{7,6},{8,9},{9,8},{10,11... | collective-permute-start | bytes 3538952 | tf_op jit(solution)/shard_map/ppermute | solution.py:48
  90.1 0.8 copy-start.3
  90.1 1.5 %copy-start.5 = (bf16[2,128,256]{2,1,0:T(8,128)(2,1)S(1)}, bf16[2,128,256]{2,1,0:T(8,128)(2,1)}, u32[]{:S(2)}) copy-start(bf16[2,128,256]{2,1,0:T(8,128)(2,1)} %param.17) | copy-start | bytes 393220
  92.1 16.6 %collective-permute-start.6 = (bf16[6,48,128]{2,1,0:T(8,128)(2,1)S(1)}, bf16[6,48,128]{2,1,0:T(8,128)(2,1)S(1)}, u32[]{:S(2)}, u32[]{:S(2)}) collective-permute-start(bf16[6,48,128]{2,1,0:T(8,128)(2,1)S(1)} %get-tuple-element.70), channel_id=1, source_target_pairs={{0,0},{1,16},{2,32},{3,48},{4,64},{5,80},{6,96},{7,112},{8,128},{9... | collective-permute-start | bytes 221192 | tf_op jit(solution)/shard_map/ppermute | solution.py:73
  95.2 43.0 %all-to-all-start.3 = ((bf16[16,6,48,128]{3,2,1,0:T(8,128)(2,1)}), bf16[16,6,48,128]{3,2,1,0:T(8,128)(2,1)}, u32[]{:S(2)}, u32[]{:S(2)}) async-start(bf16[16,6,48,128]{3,2,1,0:T(8,128)(2,1)} %broadcast_in_dim.23), calls=%async_computation.3 | async-start | bytes 2359296 | tf_op jit(solution)/shard_map/all_to_all | solution.py:164
  108.7 6.1 %collective-permute-start.7 = (bf16[6,48,128]{2,1,0:T(8,128)(2,1)S(1)}, bf16[6,48,128]{2,1,0:T(8,128)(2,1)S(1)}, u32[]{:S(2)}, u32[]{:S(2)}) collective-permute-start(bf16[6,48,128]{2,1,0:T(8,128)(2,1)S(1)} %collective-permute-done.6), channel_id=1, source_target_pairs={{0,2},{1,3},{2,0},{3,1},{4,6},{5,7},{6,4},{7,5},{8,10},{9,11},{10,... | collective-permute-start | bytes 221192 | tf_op jit(solution)/shard_map/ppermute | solution.py:48
  114.7 6.9 %collective-permute-start.8 = (bf16[2,6,48,128]{3,2,1,0:T(8,128)(2,1)S(1)}, bf16[2,6,48,128]{3,2,1,0:T(8,128)(2,1)S(1)}, u32[]{:S(2)}, u32[]{:S(2)}) collective-permute-start(bf16[2,6,48,128]{3,2,1,0:T(8,128)(2,1)S(1)} %bitcast_dynamic-update-slice_fusion.14), channel_id=1, source_target_pairs={{0,8},{1,9},{2,10},{3,11},{4,12},{5,13},{6,14},{7,15},{8,0},{9,1},... | collective-permute-start | bytes 442376 | tf_op jit(solution)/shard_map/ppermute | solution.py:48
  115.0 7.0 %collective-permute-start.9 = (bf16[2,6,48,128]{3,2,1,0:T(8,128)(2,1)S(1)}, bf16[2,6,48,128]{3,2,1,0:T(8,128)(2,1)S(1)}, u32[]{:S(2)}, u32[]{:S(2)}) collective-permute-start(bf16[2,6,48,128]{3,2,1,0:T(8,128)(2,1)S(1)} %bitcast_dynamic-update-slice_fusion.14), channel_id=1, source_target_pairs={{0,4},{1,5},{2,6},{3,7},{4,0},{5,1},{6,2},{7,3},{8,12},{9,13},{10,... | collective-permute-start | bytes 442376 | tf_op jit(solution)/shard_map/ppermute | solution.py:48
  117.3 6.4 %collective-permute-start.10 = (bf16[2,6,48,128]{3,2,1,0:T(8,128)(2,1)S(1)}, bf16[2,6,48,128]{3,2,1,0:T(8,128)(2,1)S(1)}, u32[]{:S(2)}, u32[]{:S(2)}) collective-permute-start(bf16[2,6,48,128]{3,2,1,0:T(8,128)(2,1)S(1)} %bitcast_dynamic-update-slice_fusion.14), channel_id=1, source_target_pairs={{0,12},{1,13},{2,14},{3,15},{4,8},{5,9},{6,10},{7,11},{8,4},{9,5},... | collective-permute-start | bytes 442376 | tf_op jit(solution)/shard_map/ppermute | solution.py:48
  121.1 2.7 %copy-start.1 = (f32[2304,128]{1,0:T(8,128)S(1)}, f32[2304,128]{1,0:T(8,128)}, u32[]{:S(2)}) copy-start(f32[2304,128]{1,0:T(8,128)} %fusion.5) | copy-start | bytes 3538948
  123.7 5.9 %collective-permute-start.11 = (bf16[4,2,6,48,128]{4,3,2,1,0:T(8,128)(2,1)S(1)}, bf16[4,2,6,48,128]{4,3,2,1,0:T(8,128)(2,1)S(1)}, u32[]{:S(2)}, u32[]{:S(2)}) collective-permute-start(bf16[4,2,6,48,128]{4,3,2,1,0:T(8,128)(2,1)S(1)} %bitcast_dynamic-update-slice_fusion.10), channel_id=1, source_target_pairs={{0,1},{1,0},{2,3},{3,2},{4,5},{5,4},{6,7},{7,6},{8,9},{9,8},{10,11... | collective-permute-start | bytes 1769480 | tf_op jit(solution)/shard_map/ppermute | solution.py:48
  125.7 1.5 %copy-start.13 = (bf16[2,128,128]{2,1,0:T(8,128)(2,1)S(1)}, bf16[2,128,128]{2,1,0:T(8,128)(2,1)}, u32[]{:S(2)}) copy-start(bf16[2,128,128]{2,1,0:T(8,128)(2,1)} %param.21) | copy-start | bytes 196612
  142.0 1.7 %copy-start = (f32[2,48,48,128]{3,2,1,0:T(8,128)S(1)}, f32[2,48,48,128]{3,2,1,0:T(8,128)}, u32[]{:S(2)}) copy-start(f32[2,48,48,128]{3,2,1,0:T(8,128)} %pad_maximum_fusion) | copy-start | bytes 7077892
